TPU v7x, 128 devices: a whole 4x4x4 slice. The times are simulated.
128 devices in a mesh: rows: 8 (over y, core), cols: 16 (over z, x).
Axes of the slice: x: 4, y: 4, z: 4, core: 2. Of those that a mesh axis runs over, the one named last changes fastest.
Arguments:
- points: bfloat16 [4, 9, 32, 16384], P(None, None, None, ('rows', 'cols')), may hold values from -6 to 6
- counts: int32 [4, 16384], P(None, ('rows', 'cols')), may hold values from 1 to 32
- tiles: int32 [4, 16384, 1], P(None, ('rows', 'cols')), may hold values from 0 to 127; in each aligned block of 128 rows (0 to 127, 128 to 255, ..., all dimensions but the last counted through in order) at most 3 rows name the same one
- cells: int32 [4, 16384], P(None, ('rows', 'cols')), may hold values from 0 to 2047
- pfn_weight: bfloat16 [9, 64], P(None, 'rows'), may hold values from -2 to 2
- conv_weight: bfloat16 [2, 576, 64], P(None, 'rows'), may hold values from -0.25 to 0.25
- norm_gain: bfloat16 [3, 64], P(None, 'rows'), may hold values from 0.5 to 1.5
- norm_bias: bfloat16 [3, 64], P(None, 'rows'), may hold values from -3 to 3
- cotangent: bfloat16 [4, 256, 16384], P(None, 'rows', 'cols'), may hold values from -6 to 6
Outputs:
- features: bfloat16 [4, 256, 16384], P(None, 'rows', 'cols')
- point_grads: float32 [4, 9, 32, 16384], P(None, None, None, ('rows', 'cols'))
- pfn_weight_grad: float32 [9, 64], P(None, 'rows')
- conv_weight_grad: float32 [2, 576, 64], P(None, 'rows')
- norm_gain_grad: float32 [3, 64], P(None, 'rows')
- norm_bias_grad: float32 [3, 64], P(None, 'rows')
Inputs may be any that keep to these rules, and one draw needn't show every extreme that they name: `tiles`: at most 3 of one device's pillars in one scene share a tile.
All inputs are finite; a program needn't handle non-finite values.
Results may differ from a plain program's by a relative error of at most 0.023.
Values may be sent and summed in bfloat16 or wider, within the bound.
A program may use at most 128 MiB of HBM per device.

v0:
```python
import jax
import jax.numpy as jnp
from jax import lax
from jax.sharding import PartitionSpec as P

epsilon = 1e-05
highest = lax.Precision.HIGHEST


def from_behind(value, axis, steps):
    count = lax.axis_size(axis)
    initial, last = (max(0, -steps), min(count, count - steps))
    return lax.ppermute(value, axis, [(source, source + steps) for source in range(initial, last)])


def extended_2(shard, sides, width):
    for axis, dim in sides:
        peers, length = (lax.axis_size(axis), shard.shape[dim])
        up = [(i, (i + 1) % peers) for i in range(peers - 1)]
        down = [(j, i) for i, j in up]
        last = lax.slice_in_dim(shard, length - width, length, axis=dim)
        initial = lax.slice_in_dim(shard, 0, width, axis=dim)
        before = lax.ppermute(last, axis, up)
        after = lax.ppermute(initial, axis, down)
        shard = jnp.concatenate([before, shard, after], axis=dim)
    return shard


def smooth_slope(pre_values):
    sigma = jax.nn.sigmoid(pre_values)
    return sigma * (1.0 + pre_values * (1.0 - sigma))


def norm_stats(values, valid_pts):
    if valid_pts is None:
        first_sum = jnp.sum(values, axis=0)
        square_sum = jnp.sum(values * values, axis=0)
        count_sum = jnp.float32(values.shape[0])
    else:
        first_sum = jnp.sum(values * valid_pts, axis=0)
        square_sum = jnp.sum(values * values * valid_pts, axis=0)
        count_sum = jnp.sum(valid_pts)
    total_first, total_square, total_count = lax.psum(
        (first_sum, square_sum, count_sum), ("rows", "cols")
    )
    center = total_first / total_count
    spread = total_square / total_count - center * center
    factor = lax.rsqrt(spread + epsilon)
    return (center, factor, total_count)


def norm_grad(grad_pre, scaled, factor, total_count, gain_row, valid_pts):
    bias_part = jnp.sum(grad_pre, axis=0)
    gain_part = jnp.sum(grad_pre * scaled, axis=0)
    bias_all, gain_all = lax.psum((bias_part, gain_part), ("rows", "cols"))
    grad_values = (
        factor * gain_row * (grad_pre - bias_all / total_count - scaled * gain_all / total_count)
    )
    if valid_pts is not None:
        grad_values = grad_values * valid_pts
    return (grad_values, bias_part, gain_part)


def wide_kernel(kernel):
    channels = kernel.shape[1]
    return kernel.reshape(9, channels, channels).transpose(1, 0, 2).reshape(channels, 9 * channels)


def wide_turned(kernel):
    channels = kernel.shape[1]
    return kernel.reshape(9, channels, channels).transpose(2, 0, 1).reshape(channels, 9 * channels)


def tap_planes(grid, wide):
    grid_rows, grid_cols, channels = grid.shape
    product = jnp.dot(
        grid.reshape(grid_rows * grid_cols, channels), wide, preferred_element_type=jnp.float32
    )
    return product.reshape(grid_rows, grid_cols, 9, wide.shape[1] // 9)


def unit_conv(extended, wide, out_rows, out_cols, flipped):
    planes = tap_planes(extended, wide)
    total = None
    for row_off in range(3):
        for col_off in range(3):
            row_start = 2 - row_off if flipped else row_off
            col_start = 2 - col_off if flipped else col_off
            term = planes[
                row_start : row_start + out_rows,
                col_start : col_start + out_cols,
                3 * row_off + col_off,
            ]
            total = term if total is None else total + term
    return total.reshape(out_rows * out_cols, -1)


def strided_conv(extended, wide, out_rows, out_cols):
    planes = tap_planes(extended, wide)
    grid_rows, grid_cols = (planes.shape[0], planes.shape[1])
    parity = planes.reshape(grid_rows // 2, 2, grid_cols // 2, 2, 9, planes.shape[3])
    total = None
    for row_off in range(3):
        for col_off in range(3):
            row_start = row_off // 2
            col_start = col_off // 2
            term = parity[
                row_start : row_start + out_rows,
                row_off % 2,
                col_start : col_start + out_cols,
                col_off % 2,
                3 * row_off + col_off,
            ]
            total = term if total is None else total + term
    return total.reshape(out_rows * out_cols, -1)


def unit_kernel_grad(extended, grad_grid):
    out_rows, out_cols = (grad_grid.shape[0], grad_grid.shape[1])
    pieces = []
    for row_off in range(3):
        for col_off in range(3):
            window = extended[row_off : row_off + out_rows, col_off : col_off + out_cols]
            pieces.append(
                jnp.einsum("hwc,hwo->co", window, grad_grid, preferred_element_type=jnp.float32)
            )
    return jnp.concatenate(pieces, axis=0)


def strided_kernel_grad(extended, grad_grid, base):
    out_rows, out_cols = (grad_grid.shape[0], grad_grid.shape[1])
    grid_rows, grid_cols, channels = extended.shape
    parity = extended.reshape(grid_rows // 2, 2, grid_cols // 2, 2, channels)
    pieces = []
    for row_off in range(3):
        for col_off in range(3):
            row_start = base + row_off // 2
            col_start = base + col_off // 2
            window = parity[
                row_start : row_start + out_rows,
                row_off % 2,
                col_start : col_start + out_cols,
                col_off % 2,
            ]
            pieces.append(
                jnp.einsum("hwc,hwo->co", window, grad_grid, preferred_element_type=jnp.float32)
            )
    return jnp.concatenate(pieces, axis=0)


def strided_back(grad_ext, kernel, out_rows, out_cols):
    channels = kernel.shape[1]
    planes = tap_planes(grad_ext, wide_turned(kernel))
    parity_blocks = []
    for row_par in range(2):
        row_list = []
        for col_par in range(2):
            total = None
            for row_off in range(3):
                if (0 if row_off == 1 else 1) != row_par:
                    continue
                row_skip = 1 if row_off == 0 else 0
                for col_off in range(3):
                    if (0 if col_off == 1 else 1) != col_par:
                        continue
                    col_skip = 1 if col_off == 0 else 0
                    term = planes[
                        row_skip : row_skip + out_rows,
                        col_skip : col_skip + out_cols,
                        3 * row_off + col_off,
                    ]
                    total = term if total is None else total + term
            row_list.append(total)
        parity_blocks.append(jnp.stack(row_list, axis=2))
    whole = jnp.stack(parity_blocks, axis=1)
    return whole.reshape(4 * out_rows * out_cols, channels)


def body(points, counts, tiles, cells, pfn_weight, conv_weight, norm_gain, norm_bias, cotangent):
    scene_count, feature_count, depth, pillar_count = points.shape
    channels = conv_weight.shape[2]
    half_rows = cotangent.shape[1]
    half_cols = cotangent.shape[2] // channels
    tile_rows = 2 * half_rows
    tile_cols = 2 * half_cols
    pixels = tile_rows * tile_cols
    out_pixels = half_rows * half_cols
    devices = lax.axis_size("rows") * lax.axis_size("cols")
    capacity = max(3, 3 * pillar_count // devices)
    slot_count = devices * capacity
    target = tiles[:, :, 0]
    matches = (target[:, :, None] == jnp.arange(devices, dtype=jnp.int32)[None, None, :]).astype(
        jnp.int32
    )
    before = jnp.cumsum(matches, axis=1) - matches
    ranking = jnp.sum(before * matches, axis=2)
    slot_of = target * capacity + ranking
    chooser = slot_of[:, :, None] == jnp.arange(slot_count, dtype=jnp.int32)[None, None, :]
    send_cells = jnp.sum(jnp.where(chooser, cells[:, :, None] + 1, 0), axis=1) - 1
    recv_cells = lax.all_to_all(
        send_cells.reshape(scene_count, devices, capacity),
        ("rows", "cols"),
        split_axis=1,
        concat_axis=1,
        tiled=True,
    ).reshape(scene_count, slot_count)
    valid_all = (jnp.arange(depth, dtype=jnp.int32)[None, :, None] < counts[:, None, :]).astype(
        jnp.float32
    )
    pixel_ids = jnp.arange(pixels, dtype=jnp.int32)
    pfn_total = jnp.zeros((feature_count, channels), jnp.float32)
    conv_total = jnp.zeros((2, 9 * channels, channels), jnp.float32)
    gain_total = jnp.zeros((3, channels), jnp.float32)
    bias_total = jnp.zeros((3, channels), jnp.float32)
    outputs = []
    point_list = []
    for scene_index in range(scene_count):
        pfn_full, conv_full, gain_full, bias_full = (
            lax.all_gather(pfn_weight, "rows", axis=1, tiled=True),
            lax.all_gather(conv_weight, "rows", axis=1, tiled=True),
            lax.all_gather(norm_gain, "rows", axis=1, tiled=True),
            lax.all_gather(norm_bias, "rows", axis=1, tiled=True),
        )
        gains = gain_full.astype(jnp.float32)
        biases = bias_full.astype(jnp.float32)
        wide_first = wide_kernel(conv_full[0])
        wide_second = wide_kernel(conv_full[1])
        valid_pts = valid_all[scene_index].reshape(depth * pillar_count, 1)
        valid_three = valid_all[scene_index][:, :, None]
        linear = jnp.einsum(
            "cnp,co->npo", points[scene_index], pfn_full, preferred_element_type=jnp.float32
        ).reshape(depth * pillar_count, channels)
        center_pfn, factor_pfn, count_pfn = norm_stats(linear, valid_pts)
        scaled_pfn = (linear - center_pfn) * factor_pfn
        pre_pfn = scaled_pfn * gains[0] + biases[0]
        active = jax.nn.silu(pre_pfn).reshape(depth, pillar_count, channels)
        peak_value = jnp.max(jnp.where(valid_three > 0, active, -1e30), axis=0)
        shifted = jnp.where(valid_three > 0, active - peak_value[None], -1e30)
        pillar = peak_value + jnp.log(jnp.sum(jnp.exp(shifted), axis=0))
        pillar_low = pillar.astype(jnp.bfloat16)
        picker = chooser[scene_index].astype(jnp.bfloat16)
        outgoing = jnp.einsum(
            "ps,pc->sc", picker, pillar_low, preferred_element_type=jnp.float32
        ).astype(jnp.bfloat16)
        incoming = lax.all_to_all(
            outgoing.reshape(devices, capacity, channels),
            ("rows", "cols"),
            split_axis=0,
            concat_axis=0,
            tiled=True,
        ).reshape(slot_count, channels)
        placing = (pixel_ids[:, None] == recv_cells[scene_index][None, :]).astype(jnp.bfloat16)
        canvas = (
            jnp.dot(placing, incoming, preferred_element_type=jnp.float32)
            .astype(jnp.bfloat16)
            .reshape(tile_rows, tile_cols, channels)
        )
        top_row = from_behind(canvas[-1:], "rows", 1)
        ext_rows = jnp.concatenate([top_row, canvas], axis=0)
        left_col = from_behind(ext_rows[:, -1:], "cols", 1)
        ext_one = jnp.pad(jnp.concatenate([left_col, ext_rows], axis=1), ((0, 1), (0, 1), (0, 0)))
        conv_one = strided_conv(ext_one, wide_first, half_rows, half_cols)
        center_one, factor_one, count_one = norm_stats(conv_one, None)
        inner_pre = (conv_one - center_one) * factor_one * gains[1] + biases[1]
        act_inner = (
            jax.nn.silu(inner_pre).astype(jnp.bfloat16).reshape(half_rows, half_cols, channels)
        )
        act_ext = extended_2(act_inner, (("rows", 0), ("cols", 1)), 1)
        first_base = 0
        scaled_one = (conv_one - center_one) * factor_one
        pre_one = scaled_one * gains[1] + biases[1]
        conv_two = unit_conv(act_ext, wide_second, half_rows, half_cols, False)
        center_two, factor_two, count_two = norm_stats(conv_two, None)
        scaled_two = (conv_two - center_two) * factor_two
        pre_two = scaled_two * gains[2] + biases[2]
        outputs.append(
            jax.nn.silu(pre_two).astype(jnp.bfloat16).reshape(half_rows, half_cols * channels)
        )
        grad_pre_two = cotangent[scene_index].reshape(out_pixels, channels).astype(
            jnp.float32
        ) * smooth_slope(pre_two)
        grad_conv_two, bias_two, gain_two = norm_grad(
            grad_pre_two, scaled_two, factor_two, count_two, gains[2], None
        )
        grad_grid_two = grad_conv_two.astype(jnp.bfloat16).reshape(half_rows, half_cols, channels)
        kernel_grad_two = unit_kernel_grad(act_ext, grad_grid_two)
        grad_ext_two = extended_2(grad_grid_two, (("rows", 0), ("cols", 1)), 1)
        grad_act_one = unit_conv(
            grad_ext_two, wide_turned(conv_full[1]), half_rows, half_cols, True
        )
        grad_pre_one = grad_act_one * smooth_slope(pre_one)
        grad_conv_one, bias_one, gain_one = norm_grad(
            grad_pre_one, scaled_one, factor_one, count_one, gains[1], None
        )
        grad_grid = grad_conv_one.astype(jnp.bfloat16).reshape(half_rows, half_cols, channels)
        kernel_grad_one = strided_kernel_grad(ext_one, grad_grid, first_base)
        bottom_row = from_behind(grad_grid[:1], "rows", -1)
        grad_rows_ext = jnp.concatenate([grad_grid, bottom_row], axis=0)
        right_col = from_behind(grad_rows_ext[:, :1], "cols", -1)
        grad_ext_one = jnp.concatenate([grad_rows_ext, right_col], axis=1)
        grad_canvas = strided_back(grad_ext_one, conv_full[0], half_rows, half_cols)
        slot_cells = recv_cells[scene_index]
        slot_grads = (
            jnp.take(grad_canvas, jnp.maximum(slot_cells, 0), axis=0)
            * (slot_cells >= 0).astype(jnp.float32)[:, None]
        )
        returned = lax.all_to_all(
            slot_grads.astype(jnp.bfloat16).reshape(devices, capacity, channels),
            ("rows", "cols"),
            split_axis=0,
            concat_axis=0,
            tiled=True,
        ).reshape(slot_count, channels)
        grad_pillar = jnp.einsum("ps,sc->pc", picker, returned, preferred_element_type=jnp.float32)
        weights_pts = jnp.exp(jnp.where(valid_three > 0, active - pillar[None], -1e30))
        grad_pre_pfn = (grad_pillar[None] * weights_pts).reshape(
            depth * pillar_count, channels
        ) * smooth_slope(pre_pfn)
        grad_linear, bias_pfn, gain_pfn = norm_grad(
            grad_pre_pfn, scaled_pfn, factor_pfn, count_pfn, gains[0], valid_pts
        )
        grad_three = grad_linear.reshape(depth, pillar_count, channels)
        pfn_total = pfn_total + jnp.einsum(
            "cnp,npo->co", points[scene_index].astype(jnp.float32), grad_three, precision=highest
        )
        point_list.append(
            jnp.einsum("co,npo->cnp", pfn_full.astype(jnp.float32), grad_three, precision=highest)
        )
        conv_total = conv_total + jnp.stack([kernel_grad_one, kernel_grad_two])
        gain_total = gain_total + jnp.stack([gain_pfn, gain_one, gain_two])
        bias_total = bias_total + jnp.stack([bias_pfn, bias_one, bias_two])
    pfn_owned, conv_owned, gain_owned, bias_owned = (
        lax.psum_scatter(
            pfn_total.astype(jnp.bfloat16), "rows", scatter_dimension=1, tiled=True
        ).astype(jnp.float32),
        lax.psum_scatter(
            conv_total.astype(jnp.bfloat16), "rows", scatter_dimension=1, tiled=True
        ).astype(jnp.float32),
        lax.psum_scatter(
            gain_total.astype(jnp.bfloat16), "rows", scatter_dimension=1, tiled=True
        ).astype(jnp.float32),
        lax.psum_scatter(
            bias_total.astype(jnp.bfloat16), "rows", scatter_dimension=1, tiled=True
        ).astype(jnp.float32),
    )
    pfn_owned, conv_owned, gain_owned, bias_owned = (
        lax.psum(pfn_owned.astype(jnp.bfloat16), "cols").astype(jnp.float32),
        lax.psum(conv_owned.astype(jnp.bfloat16), "cols").astype(jnp.float32),
        lax.psum(gain_owned.astype(jnp.bfloat16), "cols").astype(jnp.float32),
        lax.psum(bias_owned.astype(jnp.bfloat16), "cols").astype(jnp.float32),
    )
    return (
        jnp.stack(outputs),
        jnp.stack(point_list),
        pfn_owned,
        conv_owned,
        gain_owned,
        bias_owned,
    )


def solution(mesh):
    in_specs = (
        P(None, None, None, ("rows", "cols")),
        P(None, ("rows", "cols")),
        P(None, ("rows", "cols"), None),
        P(None, ("rows", "cols")),
        P(None, "rows"),
        P(None, "rows", None),
        P(None, "rows"),
        P(None, "rows"),
        P(None, "rows", "cols"),
    )
    out_specs = (
        P(None, "rows", "cols"),
        P(None, None, None, ("rows", "cols")),
        P(None, "rows"),
        P(None, "rows", None),
        P(None, "rows"),
        P(None, "rows"),
    )
    return jax.shard_map(body, mesh=mesh, in_specs=in_specs, out_specs=out_specs, check_vma=False)
```

profile of v0, /device:TPU:0, one launch (start us, length us, event | category | flops | bytes accessed | tf_op | source)
XLA Modules:
  0.0 1109.8 jit_solution(9491636565878857926)
XLA Ops:
  11.9 11.7 %all-to-all-start = ((s32[4,128,3]{2,0,1:T(4,128)}), s32[4,128,3]{2,0,1:T(4,128)}, u32[]{:S(2)}, u32[]{:S(2)}) async-start(s32[4,128,3]{2,0,1:T(4,128)} %copy.5476), calls=%async_computation | async-start | bytes 524288 | tf_op jit(solution)/shard_map/all_to_all | solution.py:200
  26.4 10.2 all-gather.1
  37.3 8.4 all-gather
  47.1 11.2 %all_gather.8 = bf16[9,64]{0,1:T(8,128)(2,1)S(1)} all-gather(bf16[9,8]{0,1:T(8,128)(2,1)S(1)} %copy-done.264), channel_id=1, replica_groups=mesh['rows'=8,'cols'=16] {'rows'}, dimensions={1}, use_global_device_ids=true | all-gather | bytes 1296 | tf_op jit(solution)/shard_map/all_gather | solution.py:219
  61.3 66.6 %all-reduce.13 = (f32[64]{0:T(128)S(1)}, f32[]{:T(128)}, f32[64]{0:T(128)S(1)}, f32[64]{0:T(128)S(1)}, f32[]{:T(128)}, /*index=5*/f32[64]{0:T(128)S(1)}, f32[64]...) all-reduce(f32[64]{0:T(128)S(1)} %get-tuple-element.158, ...), channel_id=1, replica_groups=mesh['rows'=8,'cols'=16] {'rows','cols'}, use_global_device_ids=true, to_apply=%region_4.5 | all-reduce | flops 516 | bytes 4128 | tf_op jit(solution)/shard_map/psum | solution.py:43
  127.9 3.1 fusion.404
  131.1 4.0 fusion.419
  136.5 13.1 %all_gather.11 = bf16[2,576,64]{2,1,0:T(8,128)(2,1)S(1)} all-gather(bf16[2,72,64]{2,1,0:T(8,128)(2,1)S(1)} %copy.5485), channel_id=1, replica_groups=mesh['rows'=8,'cols'=16] {'rows'}, dimensions={1}, use_global_device_ids=true | all-gather | bytes 165888 | tf_op jit(solution)/shard_map/all_gather | solution.py:220
  167.8 5.6 all-to-all-start.1
  183.0 7.9 all-to-all-start.2
  193.2 7.3 all-to-all-done.2
  200.5 4.6 all-to-all-start.4
  206.1 8.7 all-to-all-done.4
  214.8 4.6 all-to-all-start.3
  220.4 8.6 all-to-all-done.3
  234.7 2.6 collective-permute-start.18
  239.4 2.5 collective-permute-start.1
  242.1 2.3 collective-permute-start.7
  244.6 4.0 collective-permute-start.19
  248.8 4.3 collective-permute-start.13
  254.2 2.3 reshape.4933
  259.4 6.4 fusion.86
  269.8 6.5 fusion.82
  281.9 2.7 fusion.84
  290.3 63.2 %all-reduce.12 = (f32[]{:T(128)}, f32[64]{0:T(128)S(1)}, f32[64]{0:T(128)S(1)}, f32[64]{0:T(128)}, f32[64]{0:T(128)}, /*index=5*/f32[64]{0:T(128)}, f32[64]{0:T(128)}, f32[64]{0:T(128)}, f32[64]{0:T(128)}) all-reduce(f32[]{:T(128)} %constant.53.clone.1, ...), channel_id=1, replica_groups=mesh['rows'=8,'cols'=16] {'rows','cols'}, use_global_device_ids=true, to_apply=%region_13.14 | all-reduce | flops 513 | bytes 4104 | tf_op jit(solution)/shard_map/psum | solution.py:43
  356.3 2.9 fusion.447
  359.2 2.9 fusion.446
  362.1 2.9 fusion.445
  365.0 2.9 fusion.444
  372.6 3.0 collective-permute-start.20
  377.0 3.4 collective-permute-start.2
  384.6 4.3 collective-permute-start.8
  390.2 4.3 collective-permute-start.14
  395.8 4.5 collective-permute-start.22
  401.8 4.5 collective-permute-start.4
  407.7 4.5 collective-permute-start.10
  415.1 4.7 collective-permute-start.16
  428.6 71.8 %all-reduce.11 = (f32[64]{0:T(128)}, f32[64]{0:T(128)}, f32[64]{0:T(128)}, f32[64]{0:T(128)}, f32[64]{0:T(128)}, /*index=5*/f32[64]{0:T(128)}, f32[64]{0:T(128)}, f32[64]{0:T(128)}) all-reduce(f32[64]{0:T(128)} %get-tuple-element.190, f32[64]{0:T(128)} %get-tuple-element.189, ...), channel_id=1, replica_groups=mesh['rows'=8,'cols'=16] {'rows','cols'}, use_global_device_ids=true, to_apply=%region_17.18 | all-reduce | flops 512 | bytes 4096 | tf_op jit(solution)/shard_map/psum | solution.py:43
  502.4 3.3 fusion.431
  505.7 62.9 %all-reduce.10 = (f32[64]{0:T(128)}, f32[64]{0:T(128)S(1)}, f32[64]{0:T(128)}, f32[64]{0:T(128)}, f32[64]{0:T(128)}, /*index=5*/f32[64]{0:T(128)S(1)}, f32[64]{0:T(128)}, f32[64]{0:T(128)}) all-reduce(f32[64]{0:T(128)} %get-tuple-element.552, f32[64]{0:T(128)} %get-tuple-element.553, ...), channel_id=1, replica_groups=mesh['rows'=8,'cols'=16] {'rows','cols'}, use_global_device_ids=true, to_apply=%region_71.72 | all-reduce | flops 512 | bytes 4096 | tf_op jit(solution)/shard_map/psum | solution.py:55
  634.3 3.6 collective-permute-start.24
  642.1 3.6 collective-permute-start.30
  652.6 2.4 multiply_convert_fusion.21
  655.2 2.4 multiply_convert_fusion.20
  675.9 3.7 collective-permute-start.36
  681.6 4.3 collective-permute-start.42
  687.9 4.5 collective-permute-start.26
  694.4 4.5 collective-permute-start.32
  700.3 4.5 collective-permute-start.38
  708.6 4.5 collective-permute-start.44
  717.9 72.5 %all-reduce.9 = (f32[64]{0:T(128)S(1)}, f32[64]{0:T(128)S(1)}, f32[64]{0:T(128)S(1)}, f32[64]{0:T(128)S(1)}, f32[64]{0:T(128)S(1)}, /*index=5*/f32[64]{0:T(128)S(1)}, f32[64]{0:T(128)S(1)}, f32[64]{0:T(128)S(1)}) all-reduce(f32[64]{0:T(128)S(1)} %get-tuple-element.174, ...), channel_id=1, replica_groups=mesh['rows'=8,'cols'=16] {'rows','cols'}, use_global_device_ids=true, to_apply=%region_75.76 | all-reduce | flops 512 | bytes 4096 | tf_op jit(solution)/shard_map/psum | solution.py:55
  839.9 18.7 %all-to-all-start.5 = ((bf16[128,3,64]{2,1,0:T(4,128)(2,1)}), bf16[128,3,64]{2,1,0:T(4,128)(2,1)}, u32[]{:S(2)}, u32[]{:S(2)}) async-start(bf16[128,3,64]{2,1,0:T(4,128)(2,1)} %reshape.4639), calls=%async_computation.5 | async-start | bytes 262144 | tf_op jit(solution)/shard_map/all_to_all | solution.py:307
  870.5 9.9 all-to-all-start.8
  882.5 7.4 all-to-all-done.8
  889.9 4.6 all-to-all-start.7
  895.6 8.5 all-to-all-done.7
  904.2 4.9 all-to-all-start.6
  910.1 8.6 all-to-all-done.6
  920.2 5.6 fusion.420
  927.4 5.6 fusion.422
  933.0 63.3 %all-reduce.8 = (f32[64]{0:T(128)S(1)}, f32[64]{0:T(128)S(1)}, f32[64]{0:T(128)S(1)}, f32[64]{0:T(128)S(1)}, f32[64]{0:T(128)S(1)}, /*index=5*/f32[64]{0:T(128)S(1)}, f32[64]{0:T(128)S(1)}, f32[64]{0:T(128)S(1)}) all-reduce(f32[64]{0:T(128)S(1)} %get-tuple-element.166, ...), channel_id=1, replica_groups=mesh['rows'=8,'cols'=16] {'rows','cols'}, use_global_device_ids=true, to_apply=%region_79.81 | all-reduce | flops 512 | bytes 4096 | tf_op jit(solution)/shard_map/psum | solution.py:55
  999.0 2.7 convolution_bitcast_fusion
  1014.3 13.0 %all-reduce.15 = (bf16[9,64]{1,0:T(8,128)(2,1)S(1)}, bf16[3,64]{1,0:T(4,128)(2,1)S(1)}, bf16[3,64]{1,0:T(4,128)(2,1)S(1)}) all-reduce(bf16[9,64]{1,0:T(8,128)(2,1)S(1)} %fusion.29, bf16[3,64]{1,0:T(4,128)(2,1)S(1)} %fusion.380, bf16[3,64]{1,0:T(4,128)(2,1)S(1)} %fusion.383), channel_id=2, replica_groups=mesh['rows'=8,'cols'=16] {'rows'}, use_global_device_ids=true, to_apply=%region_116.118.clone | all-reduce | flops 960 | bytes 3840
  1028.5 71.5 %all-reduce.14 = (bf16[9,8]{1,0:T(8,128)(2,1)S(1)}, bf16[2,72,64]{1,2,0:T(8,128)(2,1)S(1)}, bf16[3,8]{1,0:T(4,128)(2,1)S(1)}, bf16[3,8]{1,0:T(4,128)(2,1)S(1)}) all-reduce(bf16[9,8]{1,0:T(8,128)(2,1)S(1)} %constant_dynamic-slice_fusion.3, ...), channel_id=1, replica_groups=mesh['rows'=8,'cols'=16] {'cols'}, use_global_device_ids=true, to_apply=%region_117.119 | all-reduce | flops 9336 | bytes 37344 | tf_op jit(solution)/shard_map/psum | solution.py:347
  (1067 shorter events, 297.9 us)
Async XLA Ops:
  11.9 155.8 %all-to-all-start = ((s32[4,128,3]{2,0,1:T(4,128)}), s32[4,128,3]{2,0,1:T(4,128)}, u32[]{:S(2)}, u32[]{:S(2)}) async-start(s32[4,128,3]{2,0,1:T(4,128)} %copy.5476), calls=%async_computation | async-start | bytes 524288 | tf_op jit(solution)/shard_map/all_to_all | solution.py:200
  23.8 129.0 %copy-start.85 = (pred[4,128,384]{2,1,0:T(32,128)(4,1)}, pred[4,128,384]{2,1,0:T(32,128)(4,1)S(1)}, u32[]{:S(2)}) copy-start(pred[4,128,384]{2,1,0:T(32,128)(4,1)S(1)} %iota_compare_fusion.18) | copy-start | bytes 589828
  26.4 109.1 %copy-start.136 = (pred[32,128]{1,0:T(8,128)(4,1)}, pred[32,128]{1,0:T(8,128)(4,1)S(1)}, u32[]{:S(2)}) copy-start(pred[32,128]{1,0:T(8,128)(4,1)S(1)} %get-tuple-element.469) | copy-start | bytes 12292
  161.2 108.6 %copy-start.13 = (bf16[64,9,64]{0,2,1:T(8,128)(2,1)}, bf16[64,9,64]{0,2,1:T(8,128)(2,1)S(1)}, u32[]{:S(2)}) copy-start(bf16[64,9,64]{0,2,1:T(8,128)(2,1)S(1)} %copy.5486) | copy-start | bytes 221188
  167.8 15.2 %all-to-all-start.1 = ((bf16[128,3,64]{2,1,0:T(4,128)(2,1)}), bf16[128,3,64]{2,1,0:T(4,128)(2,1)S(1)}, u32[]{:S(2)}, u32[]{:S(2)}) async-start(bf16[128,3,64]{2,1,0:T(4,128)(2,1)} %reshape.4619), calls=%async_computation.1 | async-start | bytes 262144 | tf_op jit(solution)/shard_map/all_to_all | solution.py:245
  183.0 17.5 %all-to-all-start.2 = ((bf16[128,3,64]{2,1,0:T(4,128)(2,1)}), bf16[128,3,64]{2,1,0:T(4,128)(2,1)S(1)}, u32[]{:S(2)}, u32[]{:S(2)}) async-start(bf16[128,3,64]{2,1,0:T(4,128)(2,1)} %reshape.4625), calls=%async_computation.2 | async-start | bytes 262144 | tf_op jit(solution)/shard_map/all_to_all | solution.py:245
  191.9 47.4 %collective-permute-start = (bf16[1,32,64]{1,2,0:T(8,128)(2,1)S(1)}, bf16[1,32,64]{1,2,0:T(8,128)(2,1)S(1)}, u32[]{:S(2)}, u32[]{:S(2)}) collective-permute-start(bf16[1,32,64]{1,2,0:T(8,128)(2,1)S(1)} %slice_bitcast_fusion.15), channel_id=1, source_target_pairs={{0,16},{16,32},{32,48},{48,64},{64,80},{80,96},{96,112},{1,17},{17... | collective-permute-start | bytes 12296 | tf_op jit(solution)/shard_map/ppermute | solution.py:13
  200.5 14.2 %all-to-all-start.4 = ((bf16[128,3,64]{2,1,0:T(4,128)(2,1)}), bf16[128,3,64]{2,1,0:T(4,128)(2,1)S(1)}, u32[]{:S(2)}, u32[]{:S(2)}) async-start(bf16[128,3,64]{2,1,0:T(4,128)(2,1)} %reshape.4633), calls=%async_computation.4 | async-start | bytes 262144 | tf_op jit(solution)/shard_map/all_to_all | solution.py:245
  214.8 14.2 %all-to-all-start.3 = ((bf16[128,3,64]{2,1,0:T(4,128)(2,1)}), bf16[128,3,64]{2,1,0:T(4,128)(2,1)S(1)}, u32[]{:S(2)}, u32[]{:S(2)}) async-start(bf16[128,3,64]{2,1,0:T(4,128)(2,1)} %reshape.4629), calls=%async_computation.3 | async-start | bytes 262144 | tf_op jit(solution)/shard_map/all_to_all | solution.py:245
  219.4 808.2 %all-reduce.18.cloned.1.call-start = ((), (), s32[]{:S(2)}) async-start(), calls=%async_computation.9 | async-start | bytes 327680
  232.7 9.2 collective-permute-start.6
  234.7 9.7 collective-permute-start.18
  237.3 11.3 %collective-permute-start.12 = (bf16[1,32,64]{1,2,0:T(8,128)(2,1)S(1)}, bf16[1,32,64]{1,2,0:T(8,128)(2,1)S(1)}, u32[]{:S(2)}, u32[]{:S(2)}) collective-permute-start(bf16[1,32,64]{1,2,0:T(8,128)(2,1)S(1)} %slice_bitcast_fusion.13), channel_id=1, source_target_pairs={{0,16},{16,32},{32,48},{48,64},{64,80},{80,96},{96,112},{1,17},{17... | collective-permute-start | bytes 12296 | tf_op jit(solution)/shard_map/ppermute | solution.py:13
  239.4 13.6 %collective-permute-start.1 = (bf16[65,1,64]{2,1,0:T(2,128)(2,1)S(1)}, bf16[65,1,64]{2,1,0:T(2,128)(2,1)S(1)}, u32[]{:S(2)}, u32[]{:S(2)}) collective-permute-start(bf16[65,1,64]{2,1,0:T(2,128)(2,1)S(1)} %pad_maximum_fusion.29), channel_id=1, source_target_pairs={{0,1},{1,2},{2,3},{3,4},{4,5},{5,6},{6,7},{7,8},{8,9},{9,10},{10,1... | collective-permute-start | bytes 24968 | tf_op jit(solution)/shard_map/ppermute | solution.py:13
  242.1 14.4 %collective-permute-start.7 = (bf16[65,1,64]{2,1,0:T(2,128)(2,1)S(1)}, bf16[65,1,64]{2,1,0:T(2,128)(2,1)S(1)}, u32[]{:S(2)}, u32[]{:S(2)}) collective-permute-start(bf16[65,1,64]{2,1,0:T(2,128)(2,1)S(1)} %pad_maximum_fusion.28), channel_id=1, source_target_pairs={{0,1},{1,2},{2,3},{3,4},{4,5},{5,6},{6,7},{7,8},{8,9},{9,10},{10,1... | collective-permute-start | bytes 24968 | tf_op jit(solution)/shard_map/ppermute | solution.py:13
  244.6 21.3 %collective-permute-start.19 = (bf16[65,1,64]{2,1,0:T(2,128)(2,1)S(1)}, bf16[65,1,64]{2,1,0:T(2,128)(2,1)}, u32[]{:S(2)}, u32[]{:S(2)}) collective-permute-start(bf16[65,1,64]{2,1,0:T(2,128)(2,1)S(1)} %pad_maximum_fusion.26), channel_id=1, source_target_pairs={{0,1},{1,2},{2,3},{3,4},{4,5},{5,6},{6,7},{7,8},{8,9},{9,10},{10,1... | collective-permute-start | bytes 24968 | tf_op jit(solution)/shard_map/ppermute | solution.py:13
  248.8 29.4 %collective-permute-start.13 = (bf16[65,1,64]{2,1,0:T(2,128)(2,1)S(1)}, bf16[65,1,64]{2,1,0:T(2,128)(2,1)}, u32[]{:S(2)}, u32[]{:S(2)}) collective-permute-start(bf16[65,1,64]{2,1,0:T(2,128)(2,1)S(1)} %pad_maximum_fusion.27), channel_id=1, source_target_pairs={{0,1},{1,2},{2,3},{3,4},{4,5},{5,6},{6,7},{7,8},{8,9},{9,10},{10,1... | collective-permute-start | bytes 24968 | tf_op jit(solution)/shard_map/ppermute | solution.py:13
  371.3 13.3 %collective-permute-start.21 = (bf16[1,16,64]{2,0,1:T(2,128)(2,1)S(1)}, bf16[1,16,64]{2,0,1:T(2,128)(2,1)S(1)}, u32[]{:S(2)}, u32[]{:S(2)}) collective-permute-start(bf16[1,16,64]{2,0,1:T(2,128)(2,1)S(1)} %copy.5578), channel_id=1, source_target_pairs={{16,0},{32,16},{48,32},{64,48},{80,64},{96,80},{112,96},{17,1},{33... | collective-permute-start | bytes 6152 | tf_op jit(solution)/shard_map/ppermute | solution.py:24
  372.6 16.2 %collective-permute-start.20 = (bf16[1,16,64]{2,0,1:T(2,128)(2,1)S(1)}, bf16[1,16,64]{2,0,1:T(2,128)(2,1)S(1)}, u32[]{:S(2)}, u32[]{:S(2)}) collective-permute-start(bf16[1,16,64]{2,0,1:T(2,128)(2,1)S(1)} %copy.5577), channel_id=1, source_target_pairs={{0,16},{16,32},{32,48},{48,64},{64,80},{80,96},{96,112},{1,17},{17... | collective-permute-start | bytes 6152 | tf_op jit(solution)/shard_map/ppermute | solution.py:23
  375.7 14.5 %collective-permute-start.3 = (bf16[1,16,64]{2,0,1:T(2,128)(2,1)S(1)}, bf16[1,16,64]{2,0,1:T(2,128)(2,1)S(1)}, u32[]{:S(2)}, u32[]{:S(2)}) collective-permute-start(bf16[1,16,64]{2,0,1:T(2,128)(2,1)S(1)} %copy.5490), channel_id=1, source_target_pairs={{16,0},{32,16},{48,32},{64,48},{80,64},{96,80},{112,96},{17,1},{33... | collective-permute-start | bytes 6152 | tf_op jit(solution)/shard_map/ppermute | solution.py:24
  377.0 17.5 %collective-permute-start.2 = (bf16[1,16,64]{2,0,1:T(2,128)(2,1)S(1)}, bf16[1,16,64]{2,0,1:T(2,128)(2,1)S(1)}, u32[]{:S(2)}, u32[]{:S(2)}) collective-permute-start(bf16[1,16,64]{2,0,1:T(2,128)(2,1)S(1)} %copy.5489), channel_id=1, source_target_pairs={{0,16},{16,32},{32,48},{48,64},{64,80},{80,96},{96,112},{1,17},{17... | collective-permute-start | bytes 6152 | tf_op jit(solution)/shard_map/ppermute | solution.py:23
  380.4 15.4 %collective-permute-start.9 = (bf16[1,16,64]{2,0,1:T(2,128)(2,1)S(1)}, bf16[1,16,64]{2,0,1:T(2,128)(2,1)S(1)}, u32[]{:S(2)}, u32[]{:S(2)}) collective-permute-start(bf16[1,16,64]{2,0,1:T(2,128)(2,1)S(1)} %copy.5520), channel_id=1, source_target_pairs={{16,0},{32,16},{48,32},{64,48},{80,64},{96,80},{112,96},{17,1},{33... | collective-permute-start | bytes 6152 | tf_op jit(solution)/shard_map/ppermute | solution.py:24
  384.6 15.8 %collective-permute-start.8 = (bf16[1,16,64]{2,0,1:T(2,128)(2,1)S(1)}, bf16[1,16,64]{2,0,1:T(2,128)(2,1)S(1)}, u32[]{:S(2)}, u32[]{:S(2)}) collective-permute-start(bf16[1,16,64]{2,0,1:T(2,128)(2,1)S(1)} %copy.5519), channel_id=1, source_target_pairs={{0,16},{16,32},{32,48},{48,64},{64,80},{80,96},{96,112},{1,17},{17... | collective-permute-start | bytes 6152 | tf_op jit(solution)/shard_map/ppermute | solution.py:23
  388.9 12.9 %collective-permute-start.15 = (bf16[1,16,64]{2,0,1:T(2,128)(2,1)S(1)}, bf16[1,16,64]{2,0,1:T(2,128)(2,1)S(1)}, u32[]{:S(2)}, u32[]{:S(2)}) collective-permute-start(bf16[1,16,64]{2,0,1:T(2,128)(2,1)S(1)} %copy.5549), channel_id=1, source_target_pairs={{16,0},{32,16},{48,32},{64,48},{80,64},{96,80},{112,96},{17,1},{33... | collective-permute-start | bytes 6152 | tf_op jit(solution)/shard_map/ppermute | solution.py:24
  390.2 16.1 %collective-permute-start.14 = (bf16[1,16,64]{2,0,1:T(2,128)(2,1)S(1)}, bf16[1,16,64]{2,0,1:T(2,128)(2,1)S(1)}, u32[]{:S(2)}, u32[]{:S(2)}) collective-permute-start(bf16[1,16,64]{2,0,1:T(2,128)(2,1)S(1)} %copy.5548), channel_id=1, source_target_pairs={{0,16},{16,32},{32,48},{48,64},{64,80},{80,96},{96,112},{1,17},{17... | collective-permute-start | bytes 6152 | tf_op jit(solution)/shard_map/ppermute | solution.py:23
  394.5 13.2 %collective-permute-start.23 = (bf16[34,1,64]{2,0,1:T(8,128)(2,1)S(1)}, bf16[34,1,64]{2,0,1:T(8,128)(2,1)S(1)}, u32[]{:S(2)}, u32[]{:S(2)}) collective-permute-start(bf16[34,1,64]{2,0,1:T(8,128)(2,1)S(1)} %get-tuple-element.446), channel_id=1, source_target_pairs={{1,0},{2,1},{3,2},{4,3},{5,4},{6,5},{7,6},{8,7},{9,8},{10,9},{11,1... | collective-permute-start | bytes 13064 | tf_op jit(solution)/shard_map/ppermute | solution.py:24
  395.8 16.4 %collective-permute-start.22 = (bf16[34,1,64]{2,0,1:T(8,128)(2,1)S(1)}, bf16[34,1,64]{2,0,1:T(8,128)(2,1)S(1)}, u32[]{:S(2)}, u32[]{:S(2)}) collective-permute-start(bf16[34,1,64]{2,0,1:T(8,128)(2,1)S(1)} %get-tuple-element.445), channel_id=1, source_target_pairs={{0,1},{1,2},{2,3},{3,4},{4,5},{5,6},{6,7},{7,8},{8,9},{9,10},{10,1... | collective-permute-start | bytes 13064 | tf_op jit(solution)/shard_map/ppermute | solution.py:23
  400.4 14.6 %collective-permute-start.5 = (bf16[34,1,64]{2,0,1:T(8,128)(2,1)S(1)}, bf16[34,1,64]{2,0,1:T(8,128)(2,1)S(1)}, u32[]{:S(2)}, u32[]{:S(2)}) collective-permute-start(bf16[34,1,64]{2,0,1:T(8,128)(2,1)S(1)} %get-tuple-element.444), channel_id=1, source_target_pairs={{1,0},{2,1},{3,2},{4,3},{5,4},{6,5},{7,6},{8,7},{9,8},{10,9},{11,1... | collective-permute-start | bytes 13064 | tf_op jit(solution)/shard_map/ppermute | solution.py:24
  401.8 18.0 %collective-permute-start.4 = (bf16[34,1,64]{2,0,1:T(8,128)(2,1)S(1)}, bf16[34,1,64]{2,0,1:T(8,128)(2,1)S(1)}, u32[]{:S(2)}, u32[]{:S(2)}) collective-permute-start(bf16[34,1,64]{2,0,1:T(8,128)(2,1)S(1)} %get-tuple-element.443), channel_id=1, source_target_pairs={{0,1},{1,2},{2,3},{3,4},{4,5},{5,6},{6,7},{7,8},{8,9},{9,10},{10,1... | collective-permute-start | bytes 13064 | tf_op jit(solution)/shard_map/ppermute | solution.py:23
  406.3 15.0 %collective-permute-start.11 = (bf16[34,1,64]{2,0,1:T(8,128)(2,1)S(1)}, bf16[34,1,64]{2,0,1:T(8,128)(2,1)S(1)}, u32[]{:S(2)}, u32[]{:S(2)}) collective-permute-start(bf16[34,1,64]{2,0,1:T(8,128)(2,1)S(1)} %get-tuple-element.442), channel_id=1, source_target_pairs={{1,0},{2,1},{3,2},{4,3},{5,4},{6,5},{7,6},{8,7},{9,8},{10,9},{11,1... | collective-permute-start | bytes 13064 | tf_op jit(solution)/shard_map/ppermute | solution.py:24
  407.7 13.6 %collective-permute-start.10 = (bf16[34,1,64]{2,0,1:T(8,128)(2,1)S(1)}, bf16[34,1,64]{2,0,1:T(8,128)(2,1)S(1)}, u32[]{:S(2)}, u32[]{:S(2)}) collective-permute-start(bf16[34,1,64]{2,0,1:T(8,128)(2,1)S(1)} %get-tuple-element.441), channel_id=1, source_target_pairs={{0,1},{1,2},{2,3},{3,4},{4,5},{5,6},{6,7},{7,8},{8,9},{9,10},{10,1... | collective-permute-start | bytes 13064 | tf_op jit(solution)/shard_map/ppermute | solution.py:23
  412.3 11.4 %collective-permute-start.17 = (bf16[34,1,64]{2,0,1:T(8,128)(2,1)S(1)}, bf16[34,1,64]{2,0,1:T(8,128)(2,1)S(1)}, u32[]{:S(2)}, u32[]{:S(2)}) collective-permute-start(bf16[34,1,64]{2,0,1:T(8,128)(2,1)S(1)} %get-tuple-element.440), channel_id=1, source_target_pairs={{1,0},{2,1},{3,2},{4,3},{5,4},{6,5},{7,6},{8,7},{9,8},{10,9},{11,1... | collective-permute-start | bytes 13064 | tf_op jit(solution)/shard_map/ppermute | solution.py:24
  415.1 8.7 collective-permute-start.16
  632.4 43.4 %collective-permute-start.25 = (bf16[1,16,64]{2,0,1:T(2,128)(2,1)}, bf16[1,16,64]{2,0,1:T(2,128)(2,1)}, u32[]{:S(2)}, u32[]{:S(2)}) collective-permute-start(bf16[1,16,64]{2,0,1:T(2,128)(2,1)} %copy.5592), channel_id=1, source_target_pairs={{16,0},{32,16},{48,32},{64,48},{80,64},{96,80},{112,96},{17,1},{33... | collective-permute-start | bytes 6152 | tf_op jit(solution)/shard_map/ppermute | solution.py:24
  634.3 45.2 %collective-permute-start.24 = (bf16[1,16,64]{2,0,1:T(2,128)(2,1)}, bf16[1,16,64]{2,0,1:T(2,128)(2,1)}, u32[]{:S(2)}, u32[]{:S(2)}) collective-permute-start(bf16[1,16,64]{2,0,1:T(2,128)(2,1)} %copy.5590), channel_id=1, source_target_pairs={{0,16},{16,32},{32,48},{48,64},{64,80},{80,96},{96,112},{1,17},{17... | collective-permute-start | bytes 6152 | tf_op jit(solution)/shard_map/ppermute | solution.py:23
  640.2 41.3 %collective-permute-start.31 = (bf16[1,16,64]{2,0,1:T(2,128)(2,1)}, bf16[1,16,64]{2,0,1:T(2,128)(2,1)}, u32[]{:S(2)}, u32[]{:S(2)}) collective-permute-start(bf16[1,16,64]{2,0,1:T(2,128)(2,1)} %copy.5609), channel_id=1, source_target_pairs={{16,0},{32,16},{48,32},{64,48},{80,64},{96,80},{112,96},{17,1},{33... | collective-permute-start | bytes 6152 | tf_op jit(solution)/shard_map/ppermute | solution.py:24
  642.1 43.7 %collective-permute-start.30 = (bf16[1,16,64]{2,0,1:T(2,128)(2,1)}, bf16[1,16,64]{2,0,1:T(2,128)(2,1)}, u32[]{:S(2)}, u32[]{:S(2)}) collective-permute-start(bf16[1,16,64]{2,0,1:T(2,128)(2,1)} %copy.5607), channel_id=1, source_target_pairs={{0,16},{16,32},{32,48},{48,64},{64,80},{80,96},{96,112},{1,17},{17... | collective-permute-start | bytes 6152 | tf_op jit(solution)/shard_map/ppermute | solution.py:23
  648.6 39.2 %collective-permute-start.37 = (bf16[1,16,64]{2,0,1:T(2,128)(2,1)}, bf16[1,16,64]{2,0,1:T(2,128)(2,1)}, u32[]{:S(2)}, u32[]{:S(2)}) collective-permute-start(bf16[1,16,64]{2,0,1:T(2,128)(2,1)} %copy.5626), channel_id=1, source_target_pairs={{16,0},{32,16},{48,32},{64,48},{80,64},{96,80},{112,96},{17,1},{33... | collective-permute-start | bytes 6152 | tf_op jit(solution)/shard_map/ppermute | solution.py:24
  675.9 16.5 %collective-permute-start.36 = (bf16[1,16,64]{2,0,1:T(2,128)(2,1)S(1)}, bf16[1,16,64]{2,0,1:T(2,128)(2,1)S(1)}, u32[]{:S(2)}, u32[]{:S(2)}) collective-permute-start(bf16[1,16,64]{2,0,1:T(2,128)(2,1)S(1)} %copy.5624), channel_id=1, source_target_pairs={{0,16},{16,32},{32,48},{48,64},{64,80},{80,96},{96,112},{1,17},{17... | collective-permute-start | bytes 6152 | tf_op jit(solution)/shard_map/ppermute | solution.py:23
  679.6 14.8 %collective-permute-start.43 = (bf16[1,16,64]{2,0,1:T(2,128)(2,1)S(1)}, bf16[1,16,64]{2,0,1:T(2,128)(2,1)S(1)}, u32[]{:S(2)}, u32[]{:S(2)}) collective-permute-start(bf16[1,16,64]{2,0,1:T(2,128)(2,1)S(1)} %copy.5643), channel_id=1, source_target_pairs={{16,0},{32,16},{48,32},{64,48},{80,64},{96,80},{112,96},{17,1},{33... | collective-permute-start | bytes 6152 | tf_op jit(solution)/shard_map/ppermute | solution.py:24
  681.6 17.4 %collective-permute-start.42 = (bf16[1,16,64]{2,0,1:T(2,128)(2,1)S(1)}, bf16[1,16,64]{2,0,1:T(2,128)(2,1)S(1)}, u32[]{:S(2)}, u32[]{:S(2)}) collective-permute-start(bf16[1,16,64]{2,0,1:T(2,128)(2,1)S(1)} %copy.5641), channel_id=1, source_target_pairs={{0,16},{16,32},{32,48},{48,64},{64,80},{80,96},{96,112},{1,17},{17... | collective-permute-start | bytes 6152 | tf_op jit(solution)/shard_map/ppermute | solution.py:23
  685.9 14.4 %collective-permute-start.27 = (bf16[34,1,64]{2,0,1:T(8,128)(2,1)S(1)}, bf16[34,1,64]{2,0,1:T(8,128)(2,1)S(1)}, u32[]{:S(2)}, u32[]{:S(2)}) collective-permute-start(bf16[34,1,64]{2,0,1:T(8,128)(2,1)S(1)} %get-tuple-element.438), channel_id=1, source_target_pairs={{1,0},{2,1},{3,2},{4,3},{5,4},{6,5},{7,6},{8,7},{9,8},{10,9},{11,1... | collective-permute-start | bytes 13064 | tf_op jit(solution)/shard_map/ppermute | solution.py:24
  687.9 17.0 %collective-permute-start.26 = (bf16[34,1,64]{2,0,1:T(8,128)(2,1)S(1)}, bf16[34,1,64]{2,0,1:T(8,128)(2,1)S(1)}, u32[]{:S(2)}, u32[]{:S(2)}) collective-permute-start(bf16[34,1,64]{2,0,1:T(8,128)(2,1)S(1)} %get-tuple-element.437), channel_id=1, source_target_pairs={{0,1},{1,2},{2,3},{3,4},{4,5},{5,6},{6,7},{7,8},{8,9},{9,10},{10,1... | collective-permute-start | bytes 13064 | tf_op jit(solution)/shard_map/ppermute | solution.py:23
  692.4 16.2 %collective-permute-start.33 = (bf16[34,1,64]{2,0,1:T(8,128)(2,1)S(1)}, bf16[34,1,64]{2,0,1:T(8,128)(2,1)S(1)}, u32[]{:S(2)}, u32[]{:S(2)}) collective-permute-start(bf16[34,1,64]{2,0,1:T(8,128)(2,1)S(1)} %get-tuple-element.436), channel_id=1, source_target_pairs={{1,0},{2,1},{3,2},{4,3},{5,4},{6,5},{7,6},{8,7},{9,8},{10,9},{11,1... | collective-permute-start | bytes 13064 | tf_op jit(solution)/shard_map/ppermute | solution.py:24
  694.4 18.8 %collective-permute-start.32 = (bf16[34,1,64]{2,0,1:T(8,128)(2,1)S(1)}, bf16[34,1,64]{2,0,1:T(8,128)(2,1)S(1)}, u32[]{:S(2)}, u32[]{:S(2)}) collective-permute-start(bf16[34,1,64]{2,0,1:T(8,128)(2,1)S(1)} %get-tuple-element.435), channel_id=1, source_target_pairs={{0,1},{1,2},{2,3},{3,4},{4,5},{5,6},{6,7},{7,8},{8,9},{9,10},{10,1... | collective-permute-start | bytes 13064 | tf_op jit(solution)/shard_map/ppermute | solution.py:23
  698.9 16.0 %collective-permute-start.39 = (bf16[34,1,64]{2,0,1:T(8,128)(2,1)S(1)}, bf16[34,1,64]{2,0,1:T(8,128)(2,1)S(1)}, u32[]{:S(2)}, u32[]{:S(2)}) collective-permute-start(bf16[34,1,64]{2,0,1:T(8,128)(2,1)S(1)} %get-tuple-element.434), channel_id=1, source_target_pairs={{1,0},{2,1},{3,2},{4,3},{5,4},{6,5},{7,6},{8,7},{9,8},{10,9},{11,1... | collective-permute-start | bytes 13064 | tf_op jit(solution)/shard_map/ppermute | solution.py:24
  700.3 14.7 %collective-permute-start.38 = (bf16[34,1,64]{2,0,1:T(8,128)(2,1)S(1)}, bf16[34,1,64]{2,0,1:T(8,128)(2,1)S(1)}, u32[]{:S(2)}, u32[]{:S(2)}) collective-permute-start(bf16[34,1,64]{2,0,1:T(8,128)(2,1)S(1)} %get-tuple-element.433), channel_id=1, source_target_pairs={{0,1},{1,2},{2,3},{3,4},{4,5},{5,6},{6,7},{7,8},{8,9},{9,10},{10,1... | collective-permute-start | bytes 13064 | tf_op jit(solution)/shard_map/ppermute | solution.py:23
  704.8 11.9 %collective-permute-start.45 = (bf16[34,1,64]{2,0,1:T(8,128)(2,1)S(1)}, bf16[34,1,64]{2,0,1:T(8,128)(2,1)S(1)}, u32[]{:S(2)}, u32[]{:S(2)}) collective-permute-start(bf16[34,1,64]{2,0,1:T(8,128)(2,1)S(1)} %get-tuple-element.432), channel_id=1, source_target_pairs={{1,0},{2,1},{3,2},{4,3},{5,4},{6,5},{7,6},{8,7},{9,8},{10,9},{11,1... | collective-permute-start | bytes 13064 | tf_op jit(solution)/shard_map/ppermute | solution.py:24
  708.6 8.1 collective-permute-start.44
  717.4 87.2 %copy-start.198 = (f32[64]{0:T(128)S(1)}, f32[64]{0:T(128)}, u32[]{:S(2)}) copy-start(f32[64]{0:T(128)} %get-tuple-element.505) | copy-start | bytes 772
  717.8 86.6 %copy-start.256 = (f32[64]{0:T(128)}, f32[64]{0:T(128)S(1)}, u32[]{:S(2)}) copy-start(f32[64]{0:T(128)S(1)} %get-tuple-element.185) | copy-start | bytes 772
  717.8 86.6 %copy-start.258 = (f32[64]{0:T(128)}, f32[64]{0:T(128)S(1)}, u32[]{:S(2)}) copy-start(f32[64]{0:T(128)S(1)} %get-tuple-element.186) | copy-start | bytes 772
  793.2 35.8 %collective-permute-start.28 = (bf16[1,16,64]{2,0,1:T(2,128)(2,1)}, bf16[1,16,64]{2,0,1:T(2,128)(2,1)}, u32[]{:S(2)}, u32[]{:S(2)}) collective-permute-start(bf16[1,16,64]{2,0,1:T(2,128)(2,1)} %copy.5603), channel_id=1, source_target_pairs={{16,0},{32,16},{48,32},{64,48},{80,64},{96,80},{112,96},{17,1},{33... | collective-permute-start | bytes 6152 | tf_op jit(solution)/shard_map/ppermute | solution.py:13
  797.9 33.1 %collective-permute-start.46 = (bf16[1,16,64]{2,0,1:T(2,128)(2,1)}, bf16[1,16,64]{2,0,1:T(2,128)(2,1)S(1)}, u32[]{:S(2)}, u32[]{:S(2)}) collective-permute-start(bf16[1,16,64]{2,0,1:T(2,128)(2,1)} %copy.5654), channel_id=1, source_target_pairs={{16,0},{32,16},{48,32},{64,48},{80,64},{96,80},{112,96},{17,1},{33... | collective-permute-start | bytes 6152 | tf_op jit(solution)/shard_map/ppermute | solution.py:13
  803.1 29.2 %collective-permute-start.40 = (bf16[1,16,64]{2,0,1:T(2,128)(2,1)}, bf16[1,16,64]{2,0,1:T(2,128)(2,1)S(1)}, u32[]{:S(2)}, u32[]{:S(2)}) collective-permute-start(bf16[1,16,64]{2,0,1:T(2,128)(2,1)} %copy.5637), channel_id=1, source_target_pairs={{16,0},{32,16},{48,32},{64,48},{80,64},{96,80},{112,96},{17,1},{33... | collective-permute-start | bytes 6152 | tf_op jit(solution)/shard_map/ppermute | solution.py:13
  807.6 26.0 %collective-permute-start.34 = (bf16[1,16,64]{2,0,1:T(2,128)(2,1)}, bf16[1,16,64]{2,0,1:T(2,128)(2,1)S(1)}, u32[]{:S(2)}, u32[]{:S(2)}) collective-permute-start(bf16[1,16,64]{2,0,1:T(2,128)(2,1)} %copy.5620), channel_id=1, source_target_pairs={{16,0},{32,16},{48,32},{64,48},{80,64},{96,80},{112,96},{17,1},{33... | collective-permute-start | bytes 6152 | tf_op jit(solution)/shard_map/ppermute | solution.py:13
  829.7 5.6 collective-permute-start.29
  831.0 27.6 %collective-permute-start.47 = (bf16[33,1,64]{2,0,1:T(8,128)(2,1)S(1)}, bf16[33,1,64]{2,0,1:T(8,128)(2,1)S(1)}, u32[]{:S(2)}, u32[]{:S(2)}) collective-permute-start(bf16[33,1,64]{2,0,1:T(8,128)(2,1)S(1)} %pad_maximum_fusion.30), channel_id=1, source_target_pairs={{1,0},{2,1},{3,2},{4,3},{5,4},{6,5},{7,6},{8,7},{9,8},{10,9},{11,1... | collective-permute-start | bytes 12680 | tf_op jit(solution)/shard_map/ppermute | solution.py:13
  832.3 27.1 %collective-permute-start.41 = (bf16[33,1,64]{2,0,1:T(8,128)(2,1)S(1)}, bf16[33,1,64]{2,0,1:T(8,128)(2,1)S(1)}, u32[]{:S(2)}, u32[]{:S(2)}) collective-permute-start(bf16[33,1,64]{2,0,1:T(8,128)(2,1)S(1)} %pad_maximum_fusion.34), channel_id=1, source_target_pairs={{1,0},{2,1},{3,2},{4,3},{5,4},{6,5},{7,6},{8,7},{9,8},{10,9},{11,1... | collective-permute-start | bytes 12680 | tf_op jit(solution)/shard_map/ppermute | solution.py:13
  833.7 28.7 %collective-permute-start.35 = (bf16[33,1,64]{2,0,1:T(8,128)(2,1)S(1)}, bf16[33,1,64]{2,0,1:T(8,128)(2,1)S(1)}, u32[]{:S(2)}, u32[]{:S(2)}) collective-permute-start(bf16[33,1,64]{2,0,1:T(8,128)(2,1)S(1)} %pad_maximum_fusion.38), channel_id=1, source_target_pairs={{1,0},{2,1},{3,2},{4,3},{5,4},{6,5},{7,6},{8,7},{9,8},{10,9},{11,1... | collective-permute-start | bytes 12680 | tf_op jit(solution)/shard_map/ppermute | solution.py:13
  839.9 30.6 %all-to-all-start.5 = ((bf16[128,3,64]{2,1,0:T(4,128)(2,1)}), bf16[128,3,64]{2,1,0:T(4,128)(2,1)}, u32[]{:S(2)}, u32[]{:S(2)}) async-start(bf16[128,3,64]{2,1,0:T(4,128)(2,1)} %reshape.4639), calls=%async_computation.5 | async-start | bytes 262144 | tf_op jit(solution)/shard_map/all_to_all | solution.py:307
  870.5 19.5 %all-to-all-start.8 = ((bf16[128,3,64]{2,1,0:T(4,128)(2,1)}), bf16[128,3,64]{2,1,0:T(4,128)(2,1)S(1)}, u32[]{:S(2)}, u32[]{:S(2)}) async-start(bf16[128,3,64]{2,1,0:T(4,128)(2,1)} %reshape.4651), calls=%async_computation.8 | async-start | bytes 262144 | tf_op jit(solution)/shard_map/all_to_all | solution.py:307
  889.9 14.2 %all-to-all-start.7 = ((bf16[128,3,64]{2,1,0:T(4,128)(2,1)}), bf16[128,3,64]{2,1,0:T(4,128)(2,1)S(1)}, u32[]{:S(2)}, u32[]{:S(2)}) async-start(bf16[128,3,64]{2,1,0:T(4,128)(2,1)} %reshape.4647), calls=%async_computation.7 | async-start | bytes 262144 | tf_op jit(solution)/shard_map/all_to_all | solution.py:307
  904.2 14.6 %all-to-all-start.6 = ((bf16[128,3,64]{2,1,0:T(4,128)(2,1)}), bf16[128,3,64]{2,1,0:T(4,128)(2,1)S(1)}, u32[]{:S(2)}, u32[]{:S(2)}) async-start(bf16[128,3,64]{2,1,0:T(4,128)(2,1)} %reshape.4643), calls=%async_computation.6 | async-start | bytes 262144 | tf_op jit(solution)/shard_map/all_to_all | solution.py:307
  (266 other events, 4522.3 us)
Sparse Core Ops, SparseCore 0:
  829.1 59.8 all-reduce.17
where the time goes:
time: 1120 us; the launch traced here: 1110 us
  blocking collectives  528 us (47%)
  starting transfers between devices  192 us (17%)
  local copies, waits for them, and re-layouts  119 us (11%)
  other arithmetic  105 us (9%)
  matrix products  93 us (8%)
  waiting for transfers between devices  51.5 us (5%)
  between operations  21.4 us (2%)
    psum x3, blocking collectives, norm_stats(): lax.psum((first_sum, square_sum, count_sum), ('rows', 'cols'))  202 us
    psum x3, blocking collectives, norm_grad(): bias_all, gain_all = lax.psum((bias_part, gain_part), ('rows', 'cols'))  199 us
    psum x1, blocking collectives, body(): lax.psum(pfn_owned.astype(jnp.bfloat16), 'cols').astype(jnp.float32)  71.5 us
    ppermute x16, starting transfers between devices, extended_2(): before = lax.ppermute(last, axis, up)  66.7 us
    all_to_all x4, starting transfers between devices, body(): lax.all_to_all(slot_grads.astype(jnp.bfloat16).reshape(devices, capacity,...  38.1 us
    ppermute x16, starting transfers between devices, from_behind(): lax.ppermute(value, axis, [(source, source + steps) for source in range(i...  31.5 us
    dot_general x36, matrix products, unit_kernel_grad(): jnp.einsum('hwc,hwo->co', window, grad_grid, preferred_element_type=jnp.f...  28.1 us
    dot_general x16, matrix products, tap_planes(): jnp.dot(grid.reshape(grid_rows * grid_cols, channels), wide, preferred_el...  27.7 us
  transfers between devices with their start and end apart: 58, of which 8 were waited for; matrix products, arithmetic and copies ran while one was open for 18% of the time, Pallas kernels for 0%

commit v1 on v0

v1 whole, which is shorter than its diff:
```python
import functools
import types

import jax
import jax.numpy as jnp
from jax import lax
from jax.experimental import pallas as pl
from jax.experimental.pallas import tpu as pltpu
from jax.sharding import PartitionSpec as P

EPSILON = 1e-05
HIGH = lax.Precision.HIGHEST
MESH = pl.DeviceIdType.MESH
F32, BF16, I32 = jnp.float32, jnp.bfloat16, jnp.int32

SCENES = 4
PAIRS = 2
FEATS = 9
DEPTH = 32
PILLARS = 128
CH = 64
LANES = 128
HALF_ROWS = 32
HALF_COLS = 16
PIXELS = HALF_ROWS * HALF_COLS
SLOTS = 3
EDGE = 8
EXT_COLS = 32
EXT_ROWS = HALF_ROWS + 2
TAPS = 9
OWN_ROWS = 72
PAD_ROWS = 80


def dot_nn(a, b, precision=None):
    return lax.dot_general(
        a, b, (((1,), (0,)), ((), ())), precision=precision, preferred_element_type=F32
    )


def dot_nt(a, b, precision=None):
    return lax.dot_general(
        a, b, (((1,), (1,)), ((), ())), precision=precision, preferred_element_type=F32
    )


def dot_tn(a, b):
    return lax.dot_general(a, b, (((0,), (0,)), ((), ())), preferred_element_type=F32)


def iota(shape, dim):
    return lax.broadcasted_iota(I32, shape, dim)


def sigmoid(v):
    return 1.0 / (1.0 + jnp.exp(-v))


def low(v):
    return v.astype(BF16).astype(F32)


def one_hot(mask):
    return jnp.where(mask, 1.0, 0.0).astype(BF16)


def roll64(v):
    return pltpu.roll(v, CH, axis=1)


SCRATCH = dict(
    w_tmp=((16, LANES), F32),
    w_send=((16, LANES), F32),
    w_land=((8, 16, LANES), F32),
    c_send=((PAD_ROWS, LANES), BF16),
    c_land=((8, PAD_ROWS, LANES), BF16),
    taps=((TAPS * CH, LANES), F32),
    wide1=((TAPS * LANES, LANES), BF16),
    wide2=((TAPS * LANES, LANES), BF16),
    back2=((TAPS * LANES, LANES), BF16),
    back1=((4 * LANES, 4 * LANES), BF16),
    pts32=((SCENES, 16 * DEPTH, LANES), F32),
    aug=((SCENES, 16, DEPTH * LANES), BF16),
    hot=((SCENES * SLOTS, LANES, LANES), BF16),
    b_send=((128, 8, LANES), F32),
    b_land=((128, 8, LANES), F32),
    gram=((SCENES, 16, LANES), F32),
    place=((PAIRS, 4 * PIXELS, 6 * LANES), BF16),
    fetch=((PAIRS, 6 * LANES, 4 * PIXELS), BF16),
    pre=((SCENES, DEPTH, CH, LANES), F32),
    act=((SCENES, DEPTH, CH, LANES), F32),
    slope=((SCENES, DEPTH, CH, LANES), F32),
    pil=((SCENES, CH, LANES), F32),
    t_sum=((SCENES, FEATS, CH, LANES), F32),
    q_sum=((SCENES, 2, CH, LANES), F32),
    x_send=((128, 8, LANES), F32),
    x_land=((128, 8, LANES), F32),
    y_send=((128, 8, LANES), F32),
    y_land=((128, 8, LANES), F32),
    canvas=((PAIRS, 4, 33 * 24, LANES), F32),
    drow_land=((PAIRS, 2, HALF_COLS, LANES), F32),
    drow_send=((PAIRS, 2, HALF_COLS, LANES), F32),
    dcol_send=((PAIRS, 2, HALF_ROWS, LANES), F32),
    dcol_land=((PAIRS, 2, HALF_ROWS, LANES), F32),
    dcor_land=((PAIRS, 8, LANES), F32),
    im1=((PAIRS, PIXELS, TAPS * LANES), BF16),
    im2=((PAIRS, PIXELS, TAPS * LANES), BF16),
    y1=((PAIRS, PIXELS, LANES), F32),
    y2=((PAIRS, PIXELS, LANES), F32),
    x1=((PAIRS, PIXELS, LANES), F32),
    x2=((PAIRS, PIXELS, LANES), F32),
    s1=((PAIRS, PIXELS, LANES), F32),
    g1=((PAIRS, PIXELS, LANES), F32),
    g2=((PAIRS, PIXELS, LANES), F32),
    feat=((PAIRS, PIXELS, LANES), F32),
    cot=((PAIRS, PIXELS, LANES), F32),
    d1=((PAIRS, PIXELS, LANES), BF16),
    d2=((PAIRS, PIXELS, LANES), BF16),
    cols=((4, 2, PAIRS, HALF_ROWS, LANES), F32),
    halo=((4, PAIRS, LANES, LANES), F32),
    ext=((3, PAIRS, EXT_ROWS * EXT_COLS, LANES), F32),
    back=((PAIRS, 4 * PIXELS, LANES), BF16),
    st_send=((4, 4, LANES), F32),
    st_land=((4, 128, 4, LANES), F32),
    k_send=((4, LANES), F32),
    k_land=((128, 4, LANES), F32),
    p_col=((CH, LANES), F32),
    p_send=((8, 8, LANES), F32),
    p_land=((8, 8, LANES), F32),
    p2_send=((8, LANES), F32),
    p2_land=((16, 8, LANES), F32),
    dk=((TAPS * CH, LANES), F32),
    g_send=((8, PAD_ROWS, LANES), BF16),
    g_land=((8, PAD_ROWS, LANES), BF16),
    g2_send=((PAD_ROWS, LANES), BF16),
    g2_land=((16, PAD_ROWS, LANES), BF16),
    upd=((SCENES, 16, DEPTH * LANES), F32),
    small=((8, LANES), F32),
)
SEMS = 64


class Wire:
    def __init__(self, n_rows, n_cols, send_sems, recv_sems):
        self.n_rows, self.n_cols = n_rows, n_cols
        self.total = n_rows * n_cols
        self.row, self.col = lax.axis_index("rows"), lax.axis_index("cols")
        self.me = self.row * n_cols + self.col
        self.send_sems, self.recv_sems = send_sems, recv_sems
        self.used = 0
        self.sent = []

    def any_peer(self, step):
        other = lax.rem(self.me + step + self.total, self.total)
        return (other // self.n_cols, lax.rem(other, self.n_cols))

    def row_peer(self, step):
        return (lax.rem(self.row + step + self.n_rows, self.n_rows), self.col)

    def col_peer(self, step):
        return (self.row, lax.rem(self.col + step + self.n_cols, self.n_cols))

    def near(self, down, right):
        return (
            lax.rem(self.row + down + self.n_rows, self.n_rows),
            lax.rem(self.col + right + self.n_cols, self.n_cols),
        )

    def copy(self, src, dst, sem, peer):
        return pltpu.make_async_remote_copy(
            src_ref=src,
            dst_ref=dst,
            send_sem=self.send_sems.at[sem],
            recv_sem=self.recv_sems.at[sem],
            device_id=peer,
            device_id_type=MESH,
        )

    def one(self, src, dst, peer):
        sem = self.used
        self.used += 1
        copy = self.copy(src, dst, sem, peer)
        copy.start()
        self.sent.append(copy)
        return copy

    def spread(self, count, peer_of, src_of, dst_of, whole):
        sem = self.used
        self.used += 1

        def step(i, carry):
            self.copy(src_of(i), dst_of(i), sem, peer_of(i)).start()
            return carry

        lax.fori_loop(1, count, step, 0)
        copy = self.copy(whole, whole, sem, peer_of(1))
        self.sent.append(copy)
        return copy

    def settle(self):
        for copy in self.sent:
            copy.wait_send()


def step_kernel(n_rows, n_cols, *refs):
    ref = types.SimpleNamespace(**dict(zip(SCRATCH, refs[15:], strict=False)))
    ref.points, ref.counts, ref.tiles, ref.cells, ref.pfn, ref.conv = refs[:6]
    ref.gain, ref.bias, ref.cotangent, ref.features, ref.point_grads = refs[6:11]
    ref.pfn_grad, ref.conv_grad, ref.gain_grad, ref.bias_grad = refs[11:15]
    ref.send_sems, ref.recv_sems = refs[-2:]
    wire = Wire(n_rows, n_cols, ref.send_sems, ref.recv_sems)
    total, row, col, me = wire.total, wire.row, wire.col, wire.me
    lane = iota((1, LANES), 1)
    first_half = lane < CH

    barrier = pltpu.get_barrier_semaphore()

    def greet(i, carry):
        pl.semaphore_signal(barrier, inc=1, device_id=wire.any_peer(i), device_id_type=MESH)
        return carry

    lax.fori_loop(1, total, greet, 0)

    w_tmp = ref.w_tmp
    w_tmp[...] = jnp.zeros((16, LANES), F32)
    w_tmp[0:9, 0:8] = ref.pfn[...].astype(F32)
    w_tmp[9:12, 0:8] = ref.gain[...].astype(F32)
    w_tmp[12:15, 0:8] = ref.bias[...].astype(F32)
    ref.w_send[...] = pltpu.roll(w_tmp[...], row * 8, axis=1)
    ref.w_land[0] = ref.w_send[...]
    own_taps = jnp.concatenate(
        [ref.conv[0].astype(F32), ref.conv[1].astype(F32)], axis=1
    )
    own_taps = jnp.concatenate([own_taps, jnp.zeros((PAD_ROWS - OWN_ROWS, LANES), F32)], axis=0)
    ref.c_send[...] = own_taps.astype(BF16)
    ref.c_land[0] = ref.c_send[...]

    pts32, aug = ref.pts32, ref.aug
    slot_number = iota((DEPTH, LANES), 0)
    for s in range(SCENES):
        valid = slot_number < ref.counts[s : s + 1, :]
        for c in range(FEATS):
            block = ref.points[s, c * DEPTH : (c + 1) * DEPTH, :].astype(F32)
            pts32[s, c * DEPTH : (c + 1) * DEPTH, :] = jnp.where(valid, block, 0.0)
        pts32[s, FEATS * DEPTH : (FEATS + 1) * DEPTH, :] = jnp.where(valid, 1.0, 0.0)
        pts32[s, (FEATS + 1) * DEPTH :, :] = jnp.zeros((6 * DEPTH, LANES), F32)
        scene_pts = pts32.at[s]
        for n in range(DEPTH):
            aug[s, :, n * LANES : (n + 1) * LANES] = scene_pts[pl.ds(n, 16, stride=DEPTH), :].astype(
                BF16
            )
    stacked = jnp.concatenate([aug[s] for s in range(SCENES)], axis=0)
    gram_all = dot_nt(stacked, jnp.concatenate([stacked, stacked], axis=0))
    moments = jnp.zeros((4, LANES), F32)
    for s in range(SCENES):
        for b in range(3):
            piece = gram_all[16 * s + 4 * b : 16 * s + 4 * b + 4, :]
            at = 40 * b + 10 * s
            piece = pltpu.roll(piece, (at - 16 * s) % LANES, axis=1)
            moments = moments + jnp.where((lane >= at) & (lane < at + 10), piece, 0.0)

    hot = ref.hot
    above = iota((LANES, LANES), 0) < iota((LANES, LANES), 1)
    slot_row = iota((LANES, LANES), 0).astype(F32) * 4.0
    for s in range(SCENES):
        tile = lax.rem(ref.tiles[s : s + 1, :] - me + total, total).astype(F32)
        wide = jnp.broadcast_to(tile, (LANES, LANES))
        same = (jnp.transpose(wide) == wide) & above
        rank = jnp.sum(jnp.where(same, 1.0, 0.0), axis=0, keepdims=True)
        code = tile * 4.0 + rank
        for k in range(SLOTS):
            hot[s * SLOTS + k] = one_hot(slot_row + float(k) == code)

    b_send = ref.b_send.reshape(128 * 8, LANES)
    lane_row = iota((LANES, LANES), 0)
    for q in range(4):
        extra = jnp.zeros((LANES, LANES), F32)
        for pair in range(PAIRS):
            s = 2 * pair + q // 2
            cell = ref.cells[s : s + 1, :]
            place = (jnp.bitwise_and(cell, 31) if q % 2 else jnp.right_shift(cell, 5)) + 1
            for k in range(SLOTS):
                spot = jnp.where(lane_row == 120 + 3 * pair + k, place.astype(F32), 0.0)
                extra = extra + dot_nt(hot[s * SLOTS + k], spot.astype(BF16))
        b_send[pl.ds(q, 128, stride=8), :] = extra + moments[q : q + 1, :]
    ref.b_land[0, 0:4, :] = ref.b_send[0, 0:4, :]

    pl.semaphore_wait(barrier, total - 1)

    w_wait = wire.spread(
        n_rows,
        wire.row_peer,
        lambda i: ref.w_send,
        lambda i: ref.w_land.at[i],
        ref.w_land.at[pl.ds(1, n_rows - 1)],
    )
    b_wait = wire.spread(
        total,
        wire.any_peer,
        lambda i: ref.b_send.at[i, pl.ds(0, 4)],
        lambda i: ref.b_land.at[i, pl.ds(0, 4)],
        ref.b_land.at[pl.ds(1, total - 1), pl.ds(0, 4)],
    )
    c_wait = wire.spread(
        n_rows,
        wire.row_peer,
        lambda i: ref.c_send,
        lambda i: ref.c_land.at[i],
        ref.c_land.at[pl.ds(1, n_rows - 1)],
    )

    def halo_send(values, index, full):
        cols, halo = ref.cols.at[index], ref.halo.at[index]
        for pair in range(PAIRS):
            for side in range(2):
                start = side * (HALF_COLS - 1)
                cols[side, pair] = values.at[pair][pl.ds(start, HALF_ROWS, stride=HALF_COLS), :]
        waits = [
            wire.one(values.at[:, pl.ds(0, 16)], halo.at[:, pl.ds(16, 16)], wire.near(-1, 0)),
            wire.one(cols.at[0], halo.at[:, pl.ds(64, 32)], wire.near(0, -1)),
            wire.one(values.at[:, pl.ds(0, 8)], halo.at[:, pl.ds(120, 8)], wire.near(-1, -1)),
        ]
        if full:
            waits += [
                wire.one(values.at[:, pl.ds(496, 16)], halo.at[:, pl.ds(0, 16)], wire.near(1, 0)),
                wire.one(cols.at[1], halo.at[:, pl.ds(32, 32)], wire.near(0, 1)),
                wire.one(values.at[:, pl.ds(8, 8)], halo.at[:, pl.ds(112, 8)], wire.near(-1, 1)),
                wire.one(values.at[:, pl.ds(496, 8)], halo.at[:, pl.ds(104, 8)], wire.near(1, -1)),
                wire.one(values.at[:, pl.ds(504, 8)], halo.at[:, pl.ds(96, 8)], wire.near(1, 1)),
            ]
        return waits

    def there(cond):
        return jnp.where(cond, 1.0, 0.0)

    up, down = there(row > 0), there(row < n_rows - 1)
    left, right = there(col > 0), there(col < n_cols - 1)
    spot = iota((LANES, LANES), 0)
    halo_mask = jnp.where(spot < 16, up, jnp.where(spot < 32, down, jnp.where(spot < 64, left, right)))
    halo_mask = jnp.where(spot < 96, halo_mask, jnp.where(spot < 112, up, down))
    halo_mask = jnp.where(
        spot < 96,
        halo_mask,
        halo_mask * jnp.where((spot < 104) | ((spot >= 112) & (spot < 120)), left, right),
    )

    def fill_ext(index, pair, inner, edge):
        grid = ref.ext.at[index, pair]
        for i in range(HALF_ROWS):
            at = (i + 1) * EXT_COLS + EDGE
            grid[at : at + HALF_COLS, :] = inner[i * HALF_COLS : (i + 1) * HALF_COLS, :]
        grid[EDGE : EDGE + HALF_COLS, :] = edge[0:16, :]
        last = (EXT_ROWS - 1) * EXT_COLS
        grid[last + EDGE : last + EDGE + HALF_COLS, :] = edge[16:32, :]
        grid[pl.ds(EXT_COLS + EDGE - 1, HALF_ROWS, stride=EXT_COLS), :] = edge[32:64, :]
        grid[pl.ds(EXT_COLS + EDGE + HALF_COLS, HALF_ROWS, stride=EXT_COLS), :] = edge[64:96, :]
        grid[EDGE - 1 : EDGE, :] = edge[103:104, :]
        grid[EDGE + HALF_COLS : EDGE + HALF_COLS + 1, :] = edge[104:105, :]
        grid[last + EDGE - 1 : last + EDGE, :] = edge[119:120, :]
        grid[last + EDGE + HALF_COLS : last + EDGE + HALF_COLS + 1, :] = edge[120:121, :]

    def shifted(index, pair, shift, rows):
        grid = ref.ext.at[index, pair]
        start = EDGE - 1 + shift
        return [
            grid[i * EXT_COLS + start : i * EXT_COLS + start + HALF_COLS, :].astype(BF16)
            for i in rows
        ]

    def global_sums(index, rows_of):
        send, land = ref.st_send.at[index], ref.st_land.at[index]
        for i, value in enumerate(rows_of):
            send[i : i + 1, :] = value
        land[0] = send[...]
        return wire.spread(
            total,
            wire.any_peer,
            lambda i: send,
            lambda i: land.at[i],
            land.at[pl.ds(1, total - 1)],
        )

    def summed(index):
        return jnp.sum(ref.st_land[index], axis=0)

    def column_sum(v):
        return jnp.sum(v, axis=0, keepdims=True)

    cot = ref.cot
    for pair in range(PAIRS):
        spread_to = cot.at[pair]
        for m in range(HALF_COLS // 2):
            a = ref.cotangent[2 * pair, :, m * LANES : (m + 1) * LANES].astype(F32)
            b = ref.cotangent[2 * pair + 1, :, m * LANES : (m + 1) * LANES].astype(F32)
            spread_to[pl.ds(2 * m, HALF_ROWS, stride=HALF_COLS), :] = jnp.where(
                first_half, a, roll64(b)
            )
            spread_to[pl.ds(2 * m + 1, HALF_ROWS, stride=HALF_COLS), :] = jnp.where(
                first_half, roll64(a), b
            )
    cot_waits = halo_send(cot, 0, True)

    w_wait.wait_recv()
    b_wait.wait_recv()
    w_full = jnp.sum(ref.w_land[...], axis=0)
    feature_row = iota((16, LANES), 0)
    w_row = jnp.where(feature_row < FEATS, w_full, 0.0)
    gain0, bias0 = w_full[9:10, :], w_full[12:13, :]
    gain1, bias1 = w_full[10:11, :] + roll64(w_full[10:11, :]), w_full[13:14, :] + roll64(w_full[13:14, :])
    gain2, bias2 = w_full[11:12, :] + roll64(w_full[11:12, :]), w_full[14:15, :] + roll64(w_full[14:15, :])
    moments = jnp.sum(ref.b_land[:, 0:4, :], axis=0)
    gram = ref.gram
    norm0 = []
    for s in range(SCENES):
        gram[s] = jnp.zeros((16, LANES), F32)
        for b in range(3):
            piece = pltpu.roll(moments, (LANES - 40 * b - 10 * s) % LANES, axis=1)
            gram[s, 4 * b : 4 * b + 4, :] = jnp.where(lane < 10, piece, 0.0)
        products = gram[s]
        cross = dot_nn(products[:, 0:16], w_row, HIGH)
        count = products[9:10, 9:10]
        center = cross[9:10, :] / count
        spread = column_sum(w_row * cross) / count - center * center
        factor = lax.rsqrt(spread + EPSILON)
        norm0.append((center, factor, factor * gain0, count, cross, products))

    for s in range(SCENES):
        center, factor, scale, count, _, _ = norm0[s]
        folded = w_row * scale + jnp.where(feature_row == FEATS, bias0 - center * scale, 0.0)
        coarse = low(folded)
        both = jnp.concatenate(
            [coarse, low(folded - coarse), jnp.zeros((LANES - 32, LANES), F32)], axis=0
        )
        matrix = jnp.transpose(both)[0:CH, 0:32].astype(BF16)
        bound = ref.counts[s : s + 1, :]

        def forward(j, peak, s=s, matrix=matrix, bound=bound):
            points = aug[s, :, pl.ds(pl.multiple_of(j * 4 * LANES, 4 * LANES), 4 * LANES)]
            value = dot_nn(matrix, jnp.concatenate([points, points], axis=0))
            for t in range(4):
                pre = value[:, t * LANES : (t + 1) * LANES]
                sigma = sigmoid(pre)
                active = jnp.where(4 * j + t < bound, pre * sigma, -1e30)
                ref.pre[s, 4 * j + t] = pre
                ref.slope[s, 4 * j + t] = sigma
                ref.act[s, 4 * j + t] = active
                peak = jnp.maximum(peak, active)
            return peak

        peak = lax.fori_loop(0, DEPTH // 4, forward, jnp.full((CH, LANES), -1e30, F32))

        def gather_exp(j, whole, s=s, peak=peak):
            for t in range(4):
                whole = whole + jnp.exp(ref.act[s, 4 * j + t] - peak)
            return whole

        whole = lax.fori_loop(0, DEPTH // 4, gather_exp, jnp.zeros((CH, LANES), F32))
        ref.pil[s] = peak + jnp.log(whole)

    x_send = ref.x_send.reshape(128 * 8, LANES)
    for pair in range(PAIRS):
        a, b = ref.pil[2 * pair].astype(BF16), ref.pil[2 * pair + 1].astype(BF16)
        none = jnp.zeros((CH, LANES), BF16)
        both = jnp.concatenate(
            [jnp.concatenate([a, none], axis=1), jnp.concatenate([none, b], axis=1)], axis=0
        )
        for k in range(SLOTS):
            pick = jnp.concatenate(
                [hot[2 * pair * SLOTS + k], hot[(2 * pair + 1) * SLOTS + k]], axis=1
            )
            x_send[pl.ds(3 * pair + k, 128, stride=8), :] = dot_nt(pick, both)
    ref.x_land[0, 0:6, :] = ref.x_send[0, 0:6, :]
    x_wait = wire.spread(
        total,
        wire.any_peer,
        lambda i: ref.x_send.at[i, pl.ds(0, 6)],
        lambda i: ref.x_land.at[i, pl.ds(0, 6)],
        ref.x_land.at[pl.ds(1, total - 1), pl.ds(0, 6)],
    )

    b_land = ref.b_land.reshape(128 * 8, LANES)
    pieces = [b_land[pl.ds(q, 128, stride=8), :] for q in range(4)]
    turned = [jnp.transpose(piece) for piece in pieces]
    place, fetch = ref.place, ref.fetch

    def pixel_of(tall, wide):
        i, j = tall.astype(I32) - 1, wide.astype(I32) - 1
        odd = jnp.bitwise_and(i, 1) * 1024 + jnp.bitwise_and(j, 1) * 512
        return jnp.where(
            i < 0, -1, odd + jnp.right_shift(i, 1) * HALF_COLS + jnp.right_shift(j, 1)
        )

    for pair in range(PAIRS):
        for half in range(2):
            for k in range(SLOTS):
                at = 120 + 3 * pair + k
                block = (half * SLOTS + k) * LANES
                across = pixel_of(
                    turned[2 * half][at : at + 1, :], turned[2 * half + 1][at : at + 1, :]
                )
                along = pixel_of(
                    pieces[2 * half][:, at : at + 1], pieces[2 * half + 1][:, at : at + 1]
                )
                along = jnp.broadcast_to(along, (LANES, LANES))
                for m in range(4 * PIXELS // LANES):
                    place[pair, m * LANES : (m + 1) * LANES, block : block + LANES] = one_hot(
                        iota((LANES, LANES), 0) + m * LANES == across
                    )
                    fetch[pair, block : block + LANES, m * LANES : (m + 1) * LANES] = one_hot(
                        iota((LANES, LANES), 1) + m * LANES == along
                    )

    c_wait.wait_recv()
    taps = ref.taps
    for i in range(n_rows):
        owner = lax.rem(row - i + n_rows, n_rows)
        taps[pl.ds(pl.multiple_of(owner * OWN_ROWS, 8), OWN_ROWS), :] = ref.c_land[i].astype(F32)[
            0:OWN_ROWS, :
        ]
    ref.back1[...] = jnp.zeros((4 * LANES, 4 * LANES), BF16)
    for t in range(TAPS):
        both = taps[t * CH : (t + 1) * CH, :]
        swapped = roll64(both)
        at = t * LANES
        k1 = jnp.concatenate(
            [jnp.where(first_half, both, 0.0), jnp.where(first_half, 0.0, swapped)], axis=0
        )
        k2 = jnp.concatenate(
            [jnp.where(first_half, swapped, 0.0), jnp.where(first_half, 0.0, both)], axis=0
        )
        ref.wide1[at : at + LANES, :] = k1.astype(BF16)
        ref.wide2[at : at + LANES, :] = k2.astype(BF16)
        ref.back2[at : at + LANES, :] = jnp.transpose(k2).astype(BF16)
        a, b = t // 3, t % 3
        window = 2 * (a == 0) + (b == 0)
        parity = 2 * (a != 1) + (b != 1)
        ref.back1[
            window * LANES : (window + 1) * LANES, parity * LANES : (parity + 1) * LANES
        ] = jnp.transpose(k1).astype(BF16)

    def slopes(step, carry):
        s, block = step // 4, lax.rem(step, 4)
        rows = pl.ds(pl.multiple_of(block * 16, 16), 16)
        top = ref.pil[s, rows, :]

        def inner(j, sums):
            sums = list(sums)
            for t in range(2):
                n = 2 * j + t
                active, sigma = ref.act[s, n, rows, :], ref.slope[s, n, rows, :]
                share = jnp.exp(active - top) * (sigma + active * (1.0 - sigma))
                ref.slope[s, n, rows, :] = share
                sums[0] = sums[0] + share
                sums[1] = sums[1] + share * ref.pre[s, n, rows, :]
                for c in range(FEATS):
                    sums[2 + c] = sums[2 + c] + share * pts32[s, pl.ds(c * DEPTH + n, 1), :]
            return tuple(sums)

        zero = jnp.zeros((16, LANES), F32)
        sums = lax.fori_loop(0, DEPTH // 2, inner, (zero,) * (2 + FEATS))
        ref.q_sum[s, 0, rows, :] = sums[0]
        ref.q_sum[s, 1, rows, :] = sums[1]
        for c in range(FEATS):
            ref.t_sum[s, c, rows, :] = sums[2 + c]
        return carry

    lax.fori_loop(0, 4 * SCENES, slopes, 0)

    x_wait.wait_recv()
    x_land = ref.x_land.reshape(128 * 8, LANES)
    canvas = ref.canvas
    for pair in range(PAIRS):
        landed = [x_land[pl.ds(3 * pair + k, 128, stride=8), :] for k in range(SLOTS)]
        values = [jnp.where(first_half, v, 0.0) for v in landed]
        values += [jnp.where(first_half, 0.0, v) for v in landed]
        values = jnp.concatenate(values, axis=0).astype(BF16)
        for plane in range(4):
            grid = low(dot_nn(place[pair, plane * PIXELS : (plane + 1) * PIXELS, :], values))
            for i in range(HALF_ROWS):
                at = (i + 1) * 24 + EDGE
                canvas[pair, plane, at : at + HALF_COLS, :] = grid[
                    i * HALF_COLS : (i + 1) * HALF_COLS, :
                ]
        for p in range(2):
            at = 32 * 24 + EDGE
            ref.drow_send[pair, p] = canvas[pair, 2 + p, at : at + HALF_COLS, :]
            ref.dcol_send[pair, p] = canvas.at[pair, 1 + 2 * p][
                pl.ds(24 + EDGE + HALF_COLS - 1, HALF_ROWS, stride=24), :
            ]
    d_waits = [
        wire.one(ref.drow_send, ref.drow_land, wire.near(1, 0)),
        wire.one(ref.dcol_send, ref.dcol_land, wire.near(0, 1)),
        wire.one(ref.dcol_send.at[:, 1, pl.ds(24, 8)], ref.dcor_land, wire.near(1, 1)),
    ]
    for wait in d_waits:
        wait.wait_recv()
    for pair in range(PAIRS):
        for p in range(2):
            canvas[pair, 2 + p, EDGE : EDGE + HALF_COLS, :] = ref.drow_land[pair, p] * up
            canvas.at[pair, 1 + 2 * p][pl.ds(24 + EDGE - 1, HALF_ROWS, stride=24), :] = (
                ref.dcol_land[pair, p] * left
            )
        canvas[pair, 3, EDGE - 1 : EDGE, :] = ref.dcor_land[pair, 7:8, :] * (up * left)

    sums = []
    y1 = ref.y1
    for pair in range(PAIRS):
        for t in range(TAPS):
            a, b = t // 3, t % 3
            plane = 2 * (a != 1) + (b != 1)
            first, start = (0 if a == 0 else 1), (EDGE - 1 if b == 0 else EDGE)
            for i in range(HALF_ROWS):
                at = (i + first) * 24 + start
                ref.im1[
                    pair, i * HALF_COLS : (i + 1) * HALF_COLS, t * LANES : (t + 1) * LANES
                ] = canvas[pair, plane, at : at + HALF_COLS, :].astype(BF16)
        value = dot_nn(ref.im1[pair], ref.wide1[...])
        y1[pair] = value
        sums += [column_sum(value), column_sum(value * value)]
    e_wait = global_sums(0, sums)
    e_waits = halo_send(y1, 1, True)

    pixel_total = float(PIXELS * total)

    def norm_of(index, pair):
        sums = summed(index)
        center = sums[2 * pair : 2 * pair + 1, :] / pixel_total
        spread = sums[2 * pair + 1 : 2 * pair + 2, :] / pixel_total - center * center
        return center, lax.rsqrt(spread + EPSILON)

    for wait in cot_waits:
        wait.wait_recv()

    e_wait.wait_recv()
    for wait in e_waits:
        wait.wait_recv()

    norm1, sums = [], []
    y2 = ref.y2
    for pair in range(PAIRS):
        center, factor = norm_of(0, pair)
        norm1.append((center, factor))
        scaled = (y1[pair] - center) * factor
        pre = scaled * gain1 + bias1
        sigma = sigmoid(pre)
        active = low(pre * sigma)
        edge = (ref.halo[1, pair] - center) * factor * gain1 + bias1
        edge = low(edge * sigmoid(edge)) * halo_mask
        fill_ext(0, pair, active, edge)
        for b in range(3):
            window = shifted(0, pair, b, range(EXT_ROWS))
            for a in range(3):
                t = 3 * a + b
                ref.im2[pair, :, t * LANES : (t + 1) * LANES] = jnp.concatenate(
                    window[a : a + HALF_ROWS], axis=0
                )
        value = dot_nn(ref.im2[pair], ref.wide2[...])
        y2[pair] = value
        sums += [column_sum(value), column_sum(value * value)]
        ref.x1[pair] = scaled
        ref.s1[pair] = sigma * (1.0 + pre * (1.0 - sigma))
    f_wait = global_sums(1, sums)
    f_waits = halo_send(y2, 2, True)
    f_wait.wait_recv()
    for wait in f_waits:
        wait.wait_recv()

    norm2, sums = [], []
    for pair in range(PAIRS):
        center, factor = norm_of(1, pair)
        norm2.append((center, factor))
        scaled = (y2[pair] - center) * factor
        pre = scaled * gain2 + bias2
        sigma = sigmoid(pre)
        grad = cot[pair] * (sigma * (1.0 + pre * (1.0 - sigma)))
        sums += [column_sum(grad), column_sum(grad * scaled)]
        ref.x2[pair] = scaled
        ref.g2[pair] = grad
        ref.feat[pair] = pre * sigma
    g_wait = global_sums(2, sums)
    for pair in range(PAIRS):
        grid = ref.feat.at[pair]
        for m in range(HALF_COLS // 2):
            a = grid[pl.ds(2 * m, HALF_ROWS, stride=HALF_COLS), :]
            b = grid[pl.ds(2 * m + 1, HALF_ROWS, stride=HALF_COLS), :]
            at = m * LANES
            ref.features[2 * pair, :, at : at + LANES] = jnp.where(
                first_half, a, roll64(b)
            ).astype(BF16)
            ref.features[2 * pair + 1, :, at : at + LANES] = jnp.where(
                first_half, roll64(a), b
            ).astype(BF16)
    edges2 = []
    for pair in range(PAIRS):
        center, factor = norm2[pair]
        scaled = (ref.halo[2, pair] - center) * factor
        pre = scaled * gain2 + bias2
        sigma = sigmoid(pre)
        edges2.append((scaled, ref.halo[0, pair] * (sigma * (1.0 + pre * (1.0 - sigma)))))
    g_wait.wait_recv()

    total2 = summed(2)
    sums = []
    for pair in range(PAIRS):
        scale = norm2[pair][1] * gain2
        mean_grad = total2[2 * pair : 2 * pair + 1, :] / pixel_total
        mean_scaled = total2[2 * pair + 1 : 2 * pair + 2, :] / pixel_total
        inner = low(scale * (ref.g2[pair] - mean_grad - ref.x2[pair] * mean_scaled))
        edge_scaled, edge_grad = edges2[pair]
        edge = low(scale * (edge_grad - mean_grad - edge_scaled * mean_scaled)) * halo_mask
        ref.d2[pair] = inner.astype(BF16)
        fill_ext(1, pair, inner, edge)
        blocks = [None] * TAPS
        for b in range(3):
            window = shifted(1, pair, 2 - b, range(EXT_ROWS))
            for a in range(3):
                blocks[3 * a + b] = jnp.concatenate(window[2 - a : 2 - a + HALF_ROWS], axis=0)
        grad = dot_nn(jnp.concatenate(blocks, axis=1), ref.back2[...]) * ref.s1[pair]
        ref.g1[pair] = grad
        sums += [column_sum(grad), column_sum(grad * ref.x1[pair])]
    h_wait = global_sums(3, sums)
    h_waits = halo_send(ref.g1, 3, False)

    def kernel_grad(windows, grads, t):
        at = t * LANES
        product = dot_tn(windows[0, :, at : at + LANES], grads[0])
        product = product + dot_tn(windows[1, :, at : at + LANES], grads[1])
        return product[0:CH, :] + roll64(product[CH:LANES, :])

    dk = ref.dk
    for t in range(TAPS):
        dk[t * CH : (t + 1) * CH, :] = roll64(kernel_grad(ref.im2, ref.d2, t))

    h_wait.wait_recv()
    for wait in h_waits:
        wait.wait_recv()

    total1 = summed(3)
    y_send = ref.y_send.reshape(128 * 8, LANES)
    for pair in range(PAIRS):
        center, factor = norm1[pair]
        scale = factor * gain1
        mean_grad = total1[2 * pair : 2 * pair + 1, :] / pixel_total
        mean_scaled = total1[2 * pair + 1 : 2 * pair + 2, :] / pixel_total
        inner = low(scale * (ref.g1[pair] - mean_grad - ref.x1[pair] * mean_scaled))
        edge_scaled = (ref.halo[1, pair] - center) * factor
        edge = low(scale * (ref.halo[3, pair] - mean_grad - edge_scaled * mean_scaled))
        edge = jnp.where(halo_mask > 0.0, edge, 0.0)
        ref.d1[pair] = inner.astype(BF16)
        fill_ext(2, pair, inner, edge)
        here = shifted(2, pair, 1, range(1, EXT_ROWS))
        beside = shifted(2, pair, 2, range(1, EXT_ROWS))
        windows = [here[:HALF_ROWS], beside[:HALF_ROWS], here[1:], beside[1:]]
        windows = jnp.concatenate([jnp.concatenate(w, axis=0) for w in windows], axis=1)
        value = dot_nn(windows, ref.back1[...])
        for plane in range(4):
            ref.back[pair, plane * PIXELS : (plane + 1) * PIXELS, :] = value[
                :, plane * LANES : (plane + 1) * LANES
            ].astype(BF16)
        value = dot_nn(fetch[pair], ref.back[pair])
        for k in range(SLOTS):
            y_send[pl.ds(3 * pair + k, 128, stride=8), :] = jnp.where(
                first_half,
                value[k * LANES : (k + 1) * LANES, :],
                value[(SLOTS + k) * LANES : (SLOTS + k + 1) * LANES, :],
            )
    ref.y_land[0, 0:6, :] = ref.y_send[0, 0:6, :]
    y_wait = wire.spread(
        total,
        lambda i: wire.any_peer(-i),
        lambda i: ref.y_send.at[i, pl.ds(0, 6)],
        lambda i: ref.y_land.at[i, pl.ds(0, 6)],
        ref.y_land.at[pl.ds(1, total - 1), pl.ds(0, 6)],
    )

    for t in range(TAPS):
        at = t * CH
        own = kernel_grad(ref.im1, ref.d1, t)
        dk[at : at + CH, :] = jnp.where(first_half, own, dk[at : at + CH, :])
    padding = jnp.zeros((PAD_ROWS - OWN_ROWS, LANES), F32)
    for i in range(n_rows):
        owner = lax.rem(row + i, n_rows)
        block = dk[pl.ds(pl.multiple_of(owner * OWN_ROWS, 8), OWN_ROWS), :]
        block = jnp.concatenate([block, padding], axis=0).astype(BF16)
        ref.g_send[i] = block
        if i == 0:
            ref.g_land[0] = block
    g1_wait = wire.spread(
        n_rows,
        wire.row_peer,
        lambda i: ref.g_send.at[i],
        lambda i: ref.g_land.at[i],
        ref.g_land.at[pl.ds(1, n_rows - 1)],
    )
    g1_wait.wait_recv()
    block = jnp.sum(ref.g_land[...].astype(F32), axis=0).astype(BF16)
    ref.g2_send[...] = block
    ref.g2_land[0] = block
    g2_wait = wire.spread(
        n_cols,
        wire.col_peer,
        lambda i: ref.g2_send,
        lambda i: ref.g2_land.at[i],
        ref.g2_land.at[pl.ds(1, n_cols - 1)],
    )
    scales = jnp.concatenate(
        [norm0[s][2] for s in range(SCENES)] + [jnp.zeros((LANES - SCENES, LANES), F32)], axis=0
    )
    scales = jnp.transpose(scales)[0:CH, :]

    y_wait.wait_recv()
    y_land = ref.y_land.reshape(128 * 8, LANES)
    grads = []
    for pair in range(PAIRS):
        landed = [
            jnp.transpose(y_land[pl.ds(3 * pair + k, 128, stride=8), :]) for k in range(SLOTS)
        ]
        landed = jnp.concatenate(landed, axis=1).astype(BF16)
        for half in range(2):
            s = 2 * pair + half
            pick = jnp.concatenate([hot[s * SLOTS + k] for k in range(SLOTS)], axis=0)
            grads.append(dot_nn(landed[half * CH : (half + 1) * CH, :], pick))

    sums = jnp.zeros((8, CH), F32)
    sub_row = iota((8, LANES), 0)
    for s in range(SCENES):
        for kind in range(2):
            chosen = jnp.where(sub_row == kind * 4 + s, 1.0, 0.0)
            sums = sums + dot_nt(chosen, grads[s] * ref.q_sum[s, kind], HIGH)
    sums = jnp.concatenate([sums, jnp.zeros((8, CH), F32)], axis=1)
    ref.k_send[...] = sums[0:4, :] + roll64(sums[4:8, :])
    ref.k_land[0] = ref.k_send[...]
    k_wait = wire.spread(
        total,
        wire.any_peer,
        lambda i: ref.k_send,
        lambda i: ref.k_land.at[i],
        ref.k_land.at[pl.ds(1, total - 1)],
    )
    scaled_grads = [grads[s] * scales[:, s : s + 1] for s in range(SCENES)]
    weight_grad = jnp.zeros((CH, LANES), F32)
    for c in range(FEATS):
        product = scaled_grads[0] * ref.t_sum[0, c]
        for s in range(1, SCENES):
            product = product + scaled_grads[s] * ref.t_sum[s, c]
        weight_grad = jnp.where(lane == c, jnp.sum(product, axis=1, keepdims=True), weight_grad)
    ref.p_col[...] = weight_grad
    for i in range(n_rows):
        owner = lax.rem(row + i, n_rows)
        block = ref.p_col[pl.ds(pl.multiple_of(owner * 8, 8), 8), :]
        ref.p_send[i] = block
        if i == 0:
            ref.p_land[0] = block
    p_wait = wire.spread(
        n_rows,
        wire.row_peer,
        lambda i: ref.p_send.at[i],
        lambda i: ref.p_land.at[i],
        ref.p_land.at[pl.ds(1, n_rows - 1)],
    )

    for s in range(SCENES):
        scaled_w = w_row * norm0[s][2]
        coarse = low(scaled_w)
        matrix = jnp.where(first_half, coarse, roll64(scaled_w - coarse)).astype(BF16)
        for j in range(DEPTH // 4):
            block = [
                (ref.slope[s, 4 * j + t] * grads[s]).astype(BF16) for t in range(4)
            ]
            block = jnp.concatenate(block, axis=1)
            ref.upd[s, :, j * 4 * LANES : (j + 1) * 4 * LANES] = dot_nn(
                matrix, jnp.concatenate([block, block], axis=0)
            )

    p_wait.wait_recv()
    block = jnp.sum(ref.p_land[...], axis=0)
    ref.p2_send[...] = block
    ref.p2_land[0] = block
    p2_wait = wire.spread(
        n_cols,
        wire.col_peer,
        lambda i: ref.p2_send,
        lambda i: ref.p2_land.at[i],
        ref.p2_land.at[pl.ds(1, n_cols - 1)],
    )

    g2_wait.wait_recv()
    block = jnp.sum(ref.g2_land[...].astype(F32), axis=0)
    ref.conv_grad[0] = block[0:OWN_ROWS, 0:CH]
    ref.conv_grad[1] = roll64(block)[0:OWN_ROWS, 0:CH]

    k_wait.wait_recv()
    sums = jnp.sum(ref.k_land[...], axis=0)
    swapped = roll64(sums)
    bias_sum, gain_sum = jnp.zeros((1, LANES), F32), jnp.zeros((1, LANES), F32)
    correction = jnp.zeros((16, LANES), F32)
    for s in range(SCENES):
        center, factor, scale, count, cross, products = norm0[s]
        grad_sum = jnp.where(first_half, sums[s : s + 1, :], 0.0)
        scaled_sum = jnp.where(first_half, swapped[s : s + 1, :], 0.0)
        gain_safe = jnp.where(first_half, gain0, 1.0)
        scaled_sum = (scaled_sum - bias0 * grad_sum) / gain_safe
        bias_sum, gain_sum = bias_sum + grad_sum, gain_sum + scaled_sum
        grad_mean, scaled_mean = grad_sum / count, scaled_sum / count
        point_sums = products[:, 9:10]
        correction = correction + scale * (
            grad_mean * point_sums + scaled_mean * factor * (cross - center * point_sums)
        )
        unit = w_row * factor - jnp.where(feature_row == FEATS, center * factor, 0.0)
        unit = unit * scaled_mean + jnp.where(feature_row == FEATS, grad_mean, 0.0)
        mix = dot_nt(w_row * scale, unit, HIGH)
        coarse = low(mix)
        fine = mix - coarse
        mix = jnp.concatenate([coarse, fine], axis=1).astype(BF16)
        out = ref.point_grads.at[s]
        for j in range(DEPTH // 4):
            lanes = slice(j * 4 * LANES, (j + 1) * 4 * LANES)
            points = aug[s, :, lanes]
            value = ref.upd[s, :, lanes] - dot_nn(
                mix, jnp.concatenate([points, points], axis=0)
            )
            for t in range(4):
                n = 4 * j + t
                at = slice(t * LANES, (t + 1) * LANES)
                out[pl.ds(n, 8, stride=DEPTH), :] = value[0:8, at]
                out[8 * DEPTH + n : 8 * DEPTH + n + 1, :] = value[8:9, at]

    def own_lanes(values):
        return pltpu.roll(values, lax.rem(LANES - 8 * row, LANES), axis=1)

    def both_scenes(values, index):
        added = values[index : index + 1, :] + values[2 + index : 3 + index, :]
        return added + roll64(added)

    small = ref.small
    small[...] = jnp.zeros((8, LANES), F32)
    small[0:1, :] = bias_sum
    small[1:2, :] = both_scenes(total1, 0)
    small[2:3, :] = both_scenes(total2, 0)
    small[3:4, :] = gain_sum
    small[4:5, :] = both_scenes(total1, 1)
    small[5:6, :] = both_scenes(total2, 1)
    owned = own_lanes(small[...])
    ref.bias_grad[...] = owned[0:3, 0:8]
    ref.gain_grad[...] = owned[3:6, 0:8]
    correction = own_lanes(correction)

    p2_wait.wait_recv()
    block = jnp.sum(ref.p2_land[...], axis=0)
    block = jnp.concatenate([block, jnp.zeros((LANES - 8, LANES), F32)], axis=0)
    ref.pfn_grad[...] = (jnp.transpose(block)[0:16, :] - correction)[0:FEATS, 0:8]
    wire.settle()


def body(points, counts, tiles, cells, pfn_weight, conv_weight, norm_gain, norm_bias, cotangent):
    scenes, feats, depth, pillars = points.shape
    n_rows, n_cols = lax.axis_size("rows"), lax.axis_size("cols")
    vmem = pl.BlockSpec(memory_space=pltpu.VMEM)
    results = pl.pallas_call(
        functools.partial(step_kernel, n_rows, n_cols),
        out_shape=(
            jax.ShapeDtypeStruct(cotangent.shape, BF16),
            jax.ShapeDtypeStruct((scenes, feats * depth, pillars), F32),
            jax.ShapeDtypeStruct(pfn_weight.shape, F32),
            jax.ShapeDtypeStruct(conv_weight.shape, F32),
            jax.ShapeDtypeStruct(norm_gain.shape, F32),
            jax.ShapeDtypeStruct(norm_bias.shape, F32),
        ),
        in_specs=[vmem] * 9,
        out_specs=[vmem] * 6,
        scratch_shapes=[pltpu.VMEM(shape, dtype) for shape, dtype in SCRATCH.values()]
        + [pltpu.SemaphoreType.DMA((SEMS,)), pltpu.SemaphoreType.DMA((SEMS,))],
        compiler_params=pltpu.CompilerParams(
            collective_id=0, has_side_effects=True, vmem_limit_bytes=60 * 2**20
        ),
    )(
        points.reshape(scenes, feats * depth, pillars),
        counts,
        tiles.reshape(scenes, pillars),
        cells,
        pfn_weight,
        conv_weight,
        norm_gain,
        norm_bias,
        cotangent,
    )
    return (results[0], results[1].reshape(points.shape), *results[2:])


def solution(mesh):
    in_specs = (
        P(None, None, None, ("rows", "cols")),
        P(None, ("rows", "cols")),
        P(None, ("rows", "cols"), None),
        P(None, ("rows", "cols")),
        P(None, "rows"),
        P(None, "rows", None),
        P(None, "rows"),
        P(None, "rows"),
        P(None, "rows", "cols"),
    )
    out_specs = (
        P(None, "rows", "cols"),
        P(None, None, None, ("rows", "cols")),
        P(None, "rows"),
        P(None, "rows", None),
        P(None, "rows"),
        P(None, "rows"),
    )
    return jax.shard_map(body, mesh=mesh, in_specs=in_specs, out_specs=out_specs, check_vma=False)
```

time: 1120 us -> 121 us (0.11)
  blocking collectives: 528 us -> 0 us
  starting transfers between devices: 192 us -> 0 us
  Pallas kernels: 0 us -> 110 us
  local copies, waits for them, and re-layouts: 119 us -> 9.58 us
  other arithmetic: 105 us -> 0 us
  matrix products: 93 us -> 0 us
  waiting for transfers between devices: 51.5 us -> 0 us
  between operations: 21.4 us -> 0.66 us
    psum x7 -> x0, blocking collectives: 472 us -> none  [the longest x3 202 us: norm_stats(): lax.psum((first_sum, square_sum, count_sum), ('rows', 'cols'))]
    ppermute x48 -> x0, starting transfers between devices: 119 us -> none  [the longest x16 66.7 us: extended_2(): before = lax.ppermute(last, axis, up)]
    pallas_call x0 -> x1, Pallas kernels: none -> 110 us  [body(): pl.pallas_call(functools.partial(step_kernel, n_rows, n_cols), out_shape=...]
    dot_general x112 -> x0, matrix products: 93 us -> none  [the longest x36 28.1 us: unit_kernel_grad(): jnp.einsum('hwc,hwo->co', window, grad_grid, preferred_element_type=jnp.f...]
    all_to_all x9 -> x0, starting transfers between devices: 72.6 us -> none  [the longest x4 38.1 us: body(): lax.all_to_all(slot_grads.astype(jnp.bfloat16).reshape(devices, capacity,...]
    all_to_all x9 -> x0, waiting for transfers between devices: 51 us -> none  [the longest x4 26.4 us: body(): lax.all_to_all(outgoing.reshape(devices, capacity, channels), ('rows', 'c...]
    all_gather x4 -> x0, blocking collectives: 42.9 us -> none  [the longest x1 13.1 us: body(): lax.all_gather(conv_weight, 'rows', axis=1, tiled=True)]
    convert_element_type x31 -> x0, other arithmetic: 27.7 us -> none  [the longest x8 15.6 us: body(): grad_conv_two.astype(jnp.bfloat16).reshape(half_rows, half_cols, channels)]
  transfers between devices with their start and end apart: 58 -> 0, of which waited for: 8 -> 0; matrix products, arithmetic and copies ran while one was open for 18% -> 0% of each run, Pallas kernels for 0% -> 0%
where the time goes in v1:
time: 121 us; the launch traced here: 120 us
  Pallas kernels  110 us (91%)
  local copies, waits for them, and re-layouts  9.58 us (8%)
    pallas_call x1, Pallas kernels, body(): pl.pallas_call(functools.partial(step_kernel, n_rows, n_cols), out_shape=...  110 us
    unnamed x16, local copies, waits for them, and re-layouts  9.58 us

profile of v1, /device:TPU:0, one launch (start us, length us, event | category | flops | bytes accessed | tf_op | source)
XLA Modules:
  0.0 120.2 jit_solution(8174374937242206919)
XLA Ops:
  0.6 0.0 copy-start.1
  0.6 0.7 copy-done.1
  1.3 0.7 copy.15.refs_4_
  2.0 1.5 %copy.16.refs_5_ = bf16[2,72,64]{2,1,0:T(8,128)(2,1)} copy(bf16[2,72,64]{1,2,0:T(8,128)(2,1)} %param.14) | data formatting | bytes 36864 | tf_op args[5]
  3.5 109.9 %shard_map.136 = (bf16[4,32,1024]{2,1,0:T(8,128)(2,1)}, f32[4,288,128]{2,1,0:T(8,128)}, f32[9,8]{1,0:T(8,128)}, f32[2,72,64]{2,1,0:T(8,128)}, f32[3,8]{1,0:T(4,128)}, /*index=5*/f32[3,8]{1,0:T(4,128)}) custom-call(bf16[4,288,128]{2,1,0:T(8,128)(2,1)} %bitcast.4, s32[4,128]{1,0:T(4,128)} %refs_1_.1, s32[4,128]{1,0:T(4,128)} %bitcast.5, s32[4,128]{1,0:T(4,128)} %refs_3_.1, ...), custom_call_target="tpu_custom_call" | custom-call | tf_op jit(solution)/shard_map/pallas_call | solution.py:959
  113.4 0.0 copy-start
  113.4 1.4 %copy.17 = f32[9,8]{0,1:T(8,128)} copy(f32[9,8]{1,0:T(8,128)} %get-tuple-element.20) | data formatting | bytes 576
  114.8 1.6 %copy.18 = f32[2,72,64]{1,2,0:T(8,128)} copy(f32[2,72,64]{2,1,0:T(8,128)} %get-tuple-element.21) | data formatting | bytes 73728
  116.4 1.7 %copy.23 = bf16[4,32,1024]{2,1,0:T(8,128)(2,1)} copy(bf16[4,32,1024]{2,1,0:T(8,128)(2,1)} %get-tuple-element.30) | data formatting | bytes 524288
  118.1 0.0 copy-done
  118.1 0.0 copy-start.3
  118.1 0.8 copy.24
  118.9 0.0 copy-done.3
  118.9 0.0 copy-start.2
  118.9 0.6 copy.25
  119.5 0.1 copy-done.2
  119.6 0.6 copy.26
Async XLA Ops:
  0.6 0.7 copy-start.1
  113.4 4.7 %copy-start = (f32[4,288,128]{2,1,0:T(8,128)S(1)}, f32[4,288,128]{2,1,0:T(8,128)}, u32[]{:S(2)}) copy-start(f32[4,288,128]{2,1,0:T(8,128)} %get-tuple-element.13) | copy-start | bytes 1769476
  118.1 0.8 copy-start.3
  118.9 0.7 copy-start.2

commit v2 on v1

v2 whole, which is shorter than its diff:
```python
import functools
import types

import jax
import jax.numpy as jnp
from jax import lax
from jax.experimental import pallas as pl
from jax.experimental.pallas import tpu as pltpu
from jax.sharding import PartitionSpec as P

EPSILON = 1e-05
HIGH = lax.Precision.HIGHEST
MESH = pl.DeviceIdType.MESH
F32, BF16, I32 = jnp.float32, jnp.bfloat16, jnp.int32

SCENES = 4
PAIRS = 2
FEATS = 9
DEPTH = 32
PILLARS = 128
CH = 64
LANES = 128
HALF_ROWS = 32
HALF_COLS = 16
PIXELS = HALF_ROWS * HALF_COLS
SLOTS = 3
EDGE = 8
EXT_COLS = 32
EXT_ROWS = HALF_ROWS + 2
TAPS = 9
OWN_ROWS = 72
PAD_ROWS = 80


def dot_nn(a, b, precision=None):
    return lax.dot_general(
        a, b, (((1,), (0,)), ((), ())), precision=precision, preferred_element_type=F32
    )


def dot_nt(a, b, precision=None):
    return lax.dot_general(
        a, b, (((1,), (1,)), ((), ())), precision=precision, preferred_element_type=F32
    )


def dot_tn(a, b):
    return lax.dot_general(a, b, (((0,), (0,)), ((), ())), preferred_element_type=F32)


def iota(shape, dim):
    return lax.broadcasted_iota(I32, shape, dim)


def sigmoid(v):
    return 0.5 * jnp.tanh(0.5 * v) + 0.5


def low(v):
    return v.astype(BF16).astype(F32)


def one_hot(mask):
    return jnp.where(mask, 1.0, 0.0).astype(BF16)


def square_of(v):
    rows, cols = v.shape
    if cols < LANES:
        v = jnp.concatenate([v, jnp.zeros((rows, LANES - cols), v.dtype)], axis=1)
    return jnp.concatenate([v, jnp.zeros((LANES - rows, LANES), v.dtype)], axis=0)


def roll64(v):
    return pltpu.roll(v, CH, axis=1)


SCRATCH = dict(
    points=((SCENES, FEATS * DEPTH, LANES), BF16),
    counts=((SCENES, LANES), I32),
    tiles=((SCENES, LANES), I32),
    cells=((SCENES, LANES), I32),
    pfn=((8, FEATS), BF16),
    conv=((2, CH, OWN_ROWS), BF16),
    gain=((3, 8), BF16),
    bias=((3, 8), BF16),
    cotangent=((SCENES, HALF_ROWS, HALF_COLS * CH), BF16),
    features=((SCENES, HALF_ROWS, HALF_COLS * CH), BF16),
    point_grads=((SCENES, FEATS * DEPTH, LANES), F32),
    pfn_grad=((8, FEATS), F32),
    conv_grad=((2, CH, OWN_ROWS), F32),
    gain_grad=((3, 8), F32),
    bias_grad=((3, 8), F32),
    square=((LANES, LANES), F32),
    w_tmp=((16, LANES), F32),
    w_send=((16, LANES), F32),
    w_land=((8, 16, LANES), F32),
    c_send=((PAD_ROWS, LANES), BF16),
    c_land=((8, PAD_ROWS, LANES), BF16),
    taps=((TAPS * CH, LANES), F32),
    wide1=((TAPS * LANES, LANES), BF16),
    side1=((3 * LANES, LANES), BF16),
    wide2=((TAPS * LANES, LANES), BF16),
    back2=((TAPS * LANES, LANES), BF16),
    back1=((4 * LANES, 4 * LANES), BF16),
    pts32=((SCENES, 16 * DEPTH, LANES), F32),
    aug=((SCENES, 16, DEPTH * LANES), BF16),
    hot=((SCENES * SLOTS, LANES, LANES), BF16),
    b_send=((128, 8, LANES), F32),
    b_land=((128, 8, LANES), F32),
    gram=((SCENES, 16, LANES), F32),
    place=((PAIRS, PIXELS, 6 * LANES), BF16),
    rim=((PAIRS, 48, 6 * LANES), BF16),
    parity=((PAIRS, 6 * LANES, 4 * LANES), BF16),
    fetch=((PAIRS, 6 * LANES, PIXELS), BF16),
    pre=((SCENES, DEPTH, CH, LANES), F32),
    act=((SCENES, DEPTH, CH, LANES), F32),
    share=((SCENES, DEPTH, CH, LANES), F32),
    pil=((SCENES, CH, LANES), F32),
    t_sum=((SCENES, FEATS, CH, LANES), F32),
    q_sum=((SCENES, 2, CH, LANES), F32),
    x_send=((PAIRS, 128, 8, LANES), F32),
    x_land=((PAIRS, 128, 8, LANES), F32),
    y_send=((PAIRS, 128, 8, LANES), F32),
    y_land=((PAIRS, 128, 8, LANES), F32),
    rim_send=((PAIRS, 2, 48, LANES), F32),
    rim_land=((PAIRS, 2, 56, LANES), F32),
    im1=((PAIRS, PIXELS, TAPS * LANES), BF16),
    top1=((PAIRS, 16, 3 * LANES), BF16),
    left1=((PAIRS, 32, 3 * LANES), BF16),
    im2=((PAIRS, PIXELS, TAPS * LANES), BF16),
    y1=((PAIRS, PIXELS, LANES), F32),
    y2=((PAIRS, PIXELS, LANES), F32),
    x1=((PAIRS, PIXELS, LANES), F32),
    x2=((PAIRS, PIXELS, LANES), F32),
    s1=((PAIRS, PIXELS, LANES), F32),
    g1=((PAIRS, PIXELS, LANES), F32),
    g2=((PAIRS, PIXELS, LANES), F32),
    feat=((PAIRS, PIXELS, LANES), F32),
    cot=((PAIRS, PIXELS, LANES), F32),
    d1=((PAIRS, PIXELS, LANES), F32),
    d2=((PAIRS, PIXELS, LANES), BF16),
    cols=((4, PAIRS, 2, HALF_ROWS, LANES), F32),
    halo=((4, PAIRS, LANES, LANES), F32),
    ext=((3, PAIRS, EXT_ROWS * EXT_COLS, LANES), F32),
    st_send=((10, 2, LANES), F32),
    st_land=((10, 128, 2, LANES), F32),
    grads=((SCENES, CH, LANES), F32),
    p_col=((CH, LANES), F32),
    p_send=((8, 8, LANES), F32),
    p_land=((8, 8, LANES), F32),
    p2_send=((8, LANES), F32),
    p2_land=((16, 8, LANES), F32),
    dk=((TAPS * CH, LANES), F32),
    g_send=((8, PAD_ROWS, LANES), BF16),
    g_land=((8, PAD_ROWS, LANES), BF16),
    g2_send=((PAD_ROWS, LANES), BF16),
    g2_land=((16, PAD_ROWS, LANES), BF16),
    upd=((SCENES, 16, DEPTH * LANES), F32),
    small=((8, LANES), F32),
)
INPUTS = 9
RESULTS = 6
SEMS = 96


class Wire:
    def __init__(self, n_rows, n_cols, send_sems, recv_sems):
        self.n_rows, self.n_cols = n_rows, n_cols
        self.total = n_rows * n_cols
        self.row, self.col = lax.axis_index("rows"), lax.axis_index("cols")
        self.me = self.row * n_cols + self.col
        self.send_sems, self.recv_sems = send_sems, recv_sems
        self.used = 0
        self.sent = []

    def any_peer(self, step):
        other = jnp.bitwise_and(self.me + step, self.total - 1)
        return (
            jnp.right_shift(other, self.n_cols.bit_length() - 1),
            jnp.bitwise_and(other, self.n_cols - 1),
        )

    def row_peer(self, step):
        return (lax.rem(self.row + step + self.n_rows, self.n_rows), self.col)

    def col_peer(self, step):
        return (self.row, lax.rem(self.col + step + self.n_cols, self.n_cols))

    def near(self, down, right):
        return (
            lax.rem(self.row + down + self.n_rows, self.n_rows),
            lax.rem(self.col + right + self.n_cols, self.n_cols),
        )

    def copy(self, src, dst, sem, peer):
        return pltpu.make_async_remote_copy(
            src_ref=src,
            dst_ref=dst,
            send_sem=self.send_sems.at[sem],
            recv_sem=self.recv_sems.at[sem],
            device_id=peer,
            device_id_type=MESH,
        )

    def one(self, src, dst, peer):
        sem = self.used
        self.used += 1
        copy = self.copy(src, dst, sem, peer)
        copy.start()
        self.sent.append(copy)
        return copy

    def spread(self, count, peer_of, src_of, dst_of, whole):
        sem = self.used
        self.used += 1

        def step(i, carry):
            self.copy(src_of(i), dst_of(i), sem, peer_of(i)).start()
            return carry

        lax.fori_loop(1, count, step, 0, unroll=8)
        copy = self.copy(whole, whole, sem, peer_of(1))
        self.sent.append(copy)
        return copy

    def local(self, src, dst, sems, index):
        copy = pltpu.make_async_copy(src, dst, sems.at[index])
        copy.start()
        return copy

    def settle(self):
        for copy in self.sent:
            copy.wait_send()


def step_kernel(n_rows, n_cols, *refs):
    inputs, results = refs[:INPUTS], refs[INPUTS : INPUTS + RESULTS]
    ref = types.SimpleNamespace(**dict(zip(SCRATCH, refs[INPUTS + RESULTS :], strict=False)))
    send_sems, recv_sems, in_sems, out_sems = refs[-4:]
    wire = Wire(n_rows, n_cols, send_sems, recv_sems)
    total, row, col, me = wire.total, wire.row, wire.col, wire.me
    lane = iota((1, LANES), 1)
    first_half = lane < CH

    held = [
        ref.points, ref.counts, ref.tiles, ref.cells, ref.pfn, ref.conv, ref.gain, ref.bias,
        ref.cotangent,
    ]
    order = [1, 0, 2, 3, 4, 6, 7, 5, 8]
    loads = {i: wire.local(inputs[i], held[i], in_sems, i) for i in order}
    barrier = pltpu.get_barrier_semaphore()

    def greet(i, carry):
        pl.semaphore_signal(barrier, inc=1, device_id=wire.any_peer(i), device_id_type=MESH)
        return carry

    lax.fori_loop(1, total, greet, 0, unroll=8)

    for i in range(INPUTS):
        loads[i].wait()
    pts32, aug = ref.pts32, ref.aug
    slot_number = iota((DEPTH, LANES), 0)
    for s in range(SCENES):
        valid = slot_number < ref.counts[s : s + 1, :]
        for c in range(FEATS):
            block = ref.points[s, c * DEPTH : (c + 1) * DEPTH, :].astype(F32)
            pts32[s, c * DEPTH : (c + 1) * DEPTH, :] = jnp.where(valid, block, 0.0)
        pts32[s, FEATS * DEPTH : (FEATS + 1) * DEPTH, :] = jnp.where(valid, 1.0, 0.0)
        pts32[s, (FEATS + 1) * DEPTH :, :] = jnp.zeros((6 * DEPTH, LANES), F32)
        scene_pts = pts32.at[s]
        for n in range(DEPTH):
            aug[s, :, n * LANES : (n + 1) * LANES] = scene_pts[pl.ds(n, 16, stride=DEPTH), :].astype(
                BF16
            )
    stacked = jnp.concatenate([aug[s] for s in range(SCENES)], axis=0)
    gram_all = dot_nt(stacked, jnp.concatenate([stacked, stacked], axis=0))
    moments = jnp.zeros((4, LANES), F32)
    for s in range(SCENES):
        for b in range(3):
            piece = gram_all[16 * s + 4 * b : 16 * s + 4 * b + 4, :]
            at = 40 * b + 10 * s
            piece = pltpu.roll(piece, (at - 16 * s) % LANES, axis=1)
            moments = moments + jnp.where((lane >= at) & (lane < at + 10), piece, 0.0)

    hot = ref.hot
    above = iota((LANES, LANES), 0) < iota((LANES, LANES), 1)
    slot_row = iota((LANES, LANES), 0).astype(F32) * 4.0
    for s in range(SCENES):
        tile = lax.rem(ref.tiles[s : s + 1, :] - me + total, total).astype(F32)
        wide = jnp.broadcast_to(tile, (LANES, LANES))
        same = (jnp.transpose(wide) == wide) & above
        rank = jnp.sum(jnp.where(same, 1.0, 0.0), axis=0, keepdims=True)
        code = tile * 4.0 + rank
        for k in range(SLOTS):
            hot[s * SLOTS + k] = one_hot(slot_row + float(k) == code)

    b_send = ref.b_send.reshape(128 * 8, LANES)
    lane_row = iota((LANES, LANES), 0)
    for q in range(4):
        extra = jnp.zeros((LANES, LANES), F32)
        for pair in range(PAIRS):
            s = 2 * pair + q // 2
            cell = ref.cells[s : s + 1, :]
            spot = (jnp.bitwise_and(cell, 31) if q % 2 else jnp.right_shift(cell, 5)) + 1
            for k in range(SLOTS):
                at = jnp.where(lane_row == 120 + 3 * pair + k, spot.astype(F32), 0.0)
                extra = extra + dot_nt(hot[s * SLOTS + k], at.astype(BF16))
        b_send[pl.ds(q, 128, stride=8), :] = extra + moments[q : q + 1, :]
    ref.b_land[0, 0:4, :] = ref.b_send[0, 0:4, :]

    ref.square[...] = jnp.zeros((LANES, LANES), F32)
    ref.square[0:8, 0:FEATS] = ref.pfn[...].astype(F32)
    ref.w_tmp[...] = jnp.transpose(ref.square[...])[0:16, :]
    ref.w_tmp[9:12, 0:8] = ref.gain[...].astype(F32)
    ref.w_tmp[12:15, 0:8] = ref.bias[...].astype(F32)
    ref.w_send[...] = pltpu.roll(ref.w_tmp[...], row * 8, axis=1)
    ref.w_land[0] = ref.w_send[...]
    pl.semaphore_wait(barrier, total - 1)
    w_wait = wire.spread(
        n_rows,
        wire.row_peer,
        lambda i: ref.w_send,
        lambda i: ref.w_land.at[i],
        ref.w_land.at[pl.ds(1, n_rows - 1)],
    )
    b_wait = wire.spread(
        total,
        wire.any_peer,
        lambda i: ref.b_send.at[i, pl.ds(0, 4)],
        lambda i: ref.b_land.at[i, pl.ds(0, 4)],
        ref.b_land.at[pl.ds(1, total - 1), pl.ds(0, 4)],
    )

    def halo_send(values, index, pair, full):
        cols, halo = ref.cols.at[index, pair], ref.halo.at[index, pair]
        inner = values.at[pair]
        for side in range(2 if full else 1):
            cols[side] = inner[pl.ds(side * (HALF_COLS - 1), HALF_ROWS, stride=HALF_COLS), :]

        def send(src, start, count, at, down, right):
            return wire.one(
                src.at[pl.ds(start, count)], halo.at[pl.ds(at, count)], wire.near(down, right)
            )

        waits = [
            send(inner, 0, 8, 120, -1, -1),
            send(cols.at[0], 0, 32, 64, 0, -1),
            send(inner, 0, 16, 16, -1, 0),
        ]
        if full:
            waits += [
                send(inner, 504, 8, 96, 1, 1),
                send(inner, 8, 8, 112, -1, 1),
                send(inner, 496, 8, 104, 1, -1),
                send(cols.at[1], 0, 32, 32, 0, 1),
                send(inner, 496, 16, 0, 1, 0),
            ]
        return waits

    def there(cond):
        return jnp.where(cond, 1.0, 0.0)

    up, down = there(row > 0), there(row < n_rows - 1)
    left, right = there(col > 0), there(col < n_cols - 1)
    spot = iota((LANES, LANES), 0)
    halo_mask = jnp.where(spot < 16, up, jnp.where(spot < 32, down, jnp.where(spot < 64, left, right)))
    halo_mask = jnp.where(spot < 96, halo_mask, jnp.where(spot < 112, up, down))
    halo_mask = jnp.where(
        spot < 96,
        halo_mask,
        halo_mask * jnp.where((spot < 104) | ((spot >= 112) & (spot < 120)), left, right),
    )

    def fill_ext(index, pair, inner, edge):
        grid = ref.ext.at[index, pair]
        for i in range(HALF_ROWS):
            at = (i + 1) * EXT_COLS + EDGE
            grid[at : at + HALF_COLS, :] = inner[i * HALF_COLS : (i + 1) * HALF_COLS, :]
        grid[EDGE : EDGE + HALF_COLS, :] = edge[0:16, :]
        last = (EXT_ROWS - 1) * EXT_COLS
        grid[last + EDGE : last + EDGE + HALF_COLS, :] = edge[16:32, :]
        grid[pl.ds(EXT_COLS + EDGE - 1, HALF_ROWS, stride=EXT_COLS), :] = edge[32:64, :]
        grid[pl.ds(EXT_COLS + EDGE + HALF_COLS, HALF_ROWS, stride=EXT_COLS), :] = edge[64:96, :]
        grid[EDGE - 1 : EDGE, :] = edge[103:104, :]
        grid[EDGE + HALF_COLS : EDGE + HALF_COLS + 1, :] = edge[104:105, :]
        grid[last + EDGE - 1 : last + EDGE, :] = edge[119:120, :]
        grid[last + EDGE + HALF_COLS : last + EDGE + HALF_COLS + 1, :] = edge[120:121, :]

    def shifted(index, pair, shift, rows):
        grid = ref.ext.at[index, pair]
        start = EDGE - 1 + shift
        return [
            grid[i * EXT_COLS + start : i * EXT_COLS + start + HALF_COLS, :].astype(BF16)
            for i in rows
        ]

    def column_sum(v):
        return jnp.sum(v, axis=0, keepdims=True)

    def global_sums(index, first, second):
        send, land = ref.st_send.at[index], ref.st_land.at[index]
        send[0:1, :] = first
        send[1:2, :] = second
        land[0] = send[...]
        return wire.spread(
            total,
            wire.any_peer,
            lambda i: send,
            lambda i: land.at[i],
            land.at[pl.ds(1, total - 1)],
        )

    def summed(index):
        return jnp.sum(ref.st_land[index], axis=0)

    pixel_total = float(PIXELS * total)

    def norm_of(sums):
        center = sums[0:1, :] / pixel_total
        spread = sums[1:2, :] / pixel_total - center * center
        return center, lax.rsqrt(spread + EPSILON)

    cot = ref.cot
    for pair in range(PAIRS):
        spread_to = cot.at[pair]
        for m in range(HALF_COLS // 2):
            a = ref.cotangent[2 * pair, :, m * LANES : (m + 1) * LANES].astype(F32)
            b = ref.cotangent[2 * pair + 1, :, m * LANES : (m + 1) * LANES].astype(F32)
            spread_to[pl.ds(2 * m, HALF_ROWS, stride=HALF_COLS), :] = jnp.where(
                first_half, a, roll64(b)
            )
            spread_to[pl.ds(2 * m + 1, HALF_ROWS, stride=HALF_COLS), :] = jnp.where(
                first_half, roll64(a), b
            )
    ref.square[:, 0:OWN_ROWS] = jnp.concatenate(
        [ref.conv[0].astype(F32), ref.conv[1].astype(F32)], axis=0
    )
    ref.c_send[...] = jnp.transpose(ref.square[...])[0:PAD_ROWS, :].astype(BF16)
    ref.c_land[0] = ref.c_send[...]
    w_wait.wait_recv()
    b_wait.wait_recv()

    c_wait = wire.spread(
        n_rows,
        wire.row_peer,
        lambda i: ref.c_send,
        lambda i: ref.c_land.at[i],
        ref.c_land.at[pl.ds(1, n_rows - 1)],
    )
    cot_waits = [wait for pair in range(PAIRS) for wait in halo_send(cot, 0, pair, True)]
    w_full = jnp.sum(ref.w_land[...], axis=0)
    feature_row = iota((16, LANES), 0)
    w_row = jnp.where(feature_row < FEATS, w_full, 0.0)

    def twice(v):
        return v + roll64(v)

    gain0, bias0 = w_full[9:10, :], w_full[12:13, :]
    gain1, bias1 = twice(w_full[10:11, :]), twice(w_full[13:14, :])
    gain2, bias2 = twice(w_full[11:12, :]), twice(w_full[14:15, :])
    moments = jnp.sum(ref.b_land[:, 0:4, :], axis=0)
    gram = ref.gram
    norm0, matrices = [], []
    for s in range(SCENES):
        gram[s] = jnp.zeros((16, LANES), F32)
        for b in range(3):
            piece = pltpu.roll(moments, (LANES - 40 * b - 10 * s) % LANES, axis=1)
            gram[s, 4 * b : 4 * b + 4, :] = jnp.where(lane < 10, piece, 0.0)
    for s in range(SCENES):
        products = gram[s]
        cross = dot_nn(products[:, 0:16], w_row, HIGH)
        count = products[9:10, 9:10]
        center = cross[9:10, :] / count
        spread = column_sum(w_row * cross) / count - center * center
        factor = lax.rsqrt(spread + EPSILON)
        scale = factor * gain0
        norm0.append((center, factor, scale, count, cross, products))
        folded = w_row * scale + jnp.where(feature_row == FEATS, bias0 - center * scale, 0.0)
        coarse = low(folded)
        both = square_of(jnp.concatenate([coarse, low(folded - coarse)], axis=0))
        matrices.append(jnp.transpose(both)[0:CH, 0:32].astype(BF16))

    STEP = 8
    x_waits = []
    for pair in range(PAIRS):
        for s in (2 * pair, 2 * pair + 1):
            bound = ref.counts[s : s + 1, :]
            matrix = matrices[s]

            def forward(j, peak, s=s, matrix=matrix, bound=bound):
                width = STEP * LANES
                points = aug[s, :, pl.ds(pl.multiple_of(j * width, width), width)]
                value = dot_nn(matrix, jnp.concatenate([points, points], axis=0))
                for t in range(STEP):
                    n = STEP * j + t
                    pre = value[:, t * LANES : (t + 1) * LANES]
                    active = jnp.where(n < bound, pre * sigmoid(pre), -1e30)
                    ref.pre[s, n] = pre
                    ref.act[s, n] = active
                    peak = jnp.maximum(peak, active)
                return peak

            peak = lax.fori_loop(0, DEPTH // STEP, forward, jnp.full((CH, LANES), -1e30, F32))

            def gather_exp(j, whole, s=s, peak=peak):
                for t in range(STEP):
                    whole = whole + jnp.exp(ref.act[s, STEP * j + t] - peak)
                return whole

            whole = lax.fori_loop(0, DEPTH // STEP, gather_exp, jnp.zeros((CH, LANES), F32))
            ref.pil[s] = peak + jnp.log(whole)
        x_send = ref.x_send.at[pair].reshape(128 * 8, LANES)
        a, b = ref.pil[2 * pair].astype(BF16), ref.pil[2 * pair + 1].astype(BF16)
        none = jnp.zeros((CH, LANES), BF16)
        both = jnp.concatenate(
            [jnp.concatenate([a, none], axis=1), jnp.concatenate([none, b], axis=1)], axis=0
        )
        for k in range(SLOTS):
            pick = jnp.concatenate(
                [hot[2 * pair * SLOTS + k], hot[(2 * pair + 1) * SLOTS + k]], axis=1
            )
            x_send[pl.ds(k, 128, stride=8), :] = dot_nt(pick, both)
        ref.x_land[pair, 0, 0:SLOTS, :] = ref.x_send[pair, 0, 0:SLOTS, :]
        x_waits.append(
            wire.spread(
                total,
                wire.any_peer,
                lambda i, pair=pair: ref.x_send.at[pair, i, pl.ds(0, SLOTS)],
                lambda i, pair=pair: ref.x_land.at[pair, i, pl.ds(0, SLOTS)],
                ref.x_land.at[pair, pl.ds(1, total - 1), pl.ds(0, SLOTS)],
            )
        )

    b_land = ref.b_land.reshape(128 * 8, LANES)
    pieces = [b_land[pl.ds(q, 128, stride=8), :] for q in range(4)]
    turned = [jnp.transpose(piece) for piece in pieces]
    place, rim, parity, fetch = ref.place, ref.rim, ref.parity, ref.fetch

    def pixel_of(tall, wide):
        i, j = tall.astype(I32) - 1, wide.astype(I32) - 1
        pixel = jnp.right_shift(i, 1) * HALF_COLS + jnp.right_shift(j, 1)
        plane = 2 * jnp.bitwise_and(i, 1) + jnp.bitwise_and(j, 1)
        return jnp.where(i < 0, -1, pixel), jnp.where(i < 0, -1, plane)

    rim_pixel = iota((48, LANES), 0)
    rim_pixel = jnp.where(rim_pixel < 16, 496 + rim_pixel, rim_pixel * 16 - 241)
    for pair in range(PAIRS):
        for half in range(2):
            for k in range(SLOTS):
                at = 120 + 3 * pair + k
                block = (half * SLOTS + k) * LANES
                blocks = slice(block, block + LANES)
                across, _ = pixel_of(
                    turned[2 * half][at : at + 1, :], turned[2 * half + 1][at : at + 1, :]
                )
                _, along = pixel_of(
                    pieces[2 * half][:, at : at + 1], pieces[2 * half + 1][:, at : at + 1]
                )
                along = jnp.broadcast_to(along, (LANES, LANES))
                for m in range(4):
                    tile = slice(m * LANES, (m + 1) * LANES)
                    place[pair, tile, blocks] = one_hot(
                        iota((LANES, LANES), 0) + m * LANES == across
                    )
                    parity[pair, blocks, tile] = one_hot(along == m)
                rim[pair, :, blocks] = one_hot(rim_pixel == across)

    c_wait.wait_recv()
    taps = ref.taps
    for i in range(n_rows):
        owner = lax.rem(row - i + n_rows, n_rows)
        taps[pl.ds(pl.multiple_of(owner * OWN_ROWS, 8), OWN_ROWS), :] = ref.c_land[i].astype(F32)[
            0:OWN_ROWS, :
        ]
    ref.back1[...] = jnp.zeros((4 * LANES, 4 * LANES), BF16)
    for t in range(TAPS):
        both = taps[t * CH : (t + 1) * CH, :]
        swapped = roll64(both)
        at = t * LANES
        k1 = jnp.concatenate(
            [jnp.where(first_half, both, 0.0), jnp.where(first_half, 0.0, swapped)], axis=0
        )
        k2 = jnp.concatenate(
            [jnp.where(first_half, swapped, 0.0), jnp.where(first_half, 0.0, both)], axis=0
        )
        ref.wide1[at : at + LANES, :] = k1.astype(BF16)
        if t % 3 == 0:
            ref.side1[t // 3 * LANES : (t // 3 + 1) * LANES, :] = k1.astype(BF16)
        ref.wide2[at : at + LANES, :] = k2.astype(BF16)
        ref.back2[at : at + LANES, :] = jnp.transpose(k2).astype(BF16)
        a, b = t // 3, t % 3
        window = 2 * (a == 0) + (b == 0)
        plane = 2 * (a != 1) + (b != 1)
        ref.back1[
            window * LANES : (window + 1) * LANES, plane * LANES : (plane + 1) * LANES
        ] = jnp.transpose(k1).astype(BF16)

    planes_of, d_waits = [], []
    for pair in range(PAIRS):
        x_waits[pair].wait_recv()
        x_land = ref.x_land.at[pair].reshape(128 * 8, LANES)
        landed = [x_land[pl.ds(k, 128, stride=8), :] for k in range(SLOTS)]
        values = [jnp.where(first_half, v, 0.0) for v in landed]
        values += [jnp.where(first_half, 0.0, v) for v in landed]
        values = jnp.concatenate(values, axis=0).astype(BF16)
        values = jnp.concatenate([values] * 4, axis=1) * parity[pair]
        planes_of.append(values)
        edge = low(dot_nn(rim[pair], values))
        rim_send, rim_land = ref.rim_send.at[pair], ref.rim_land.at[pair]
        rim_send[0, 0:16, :] = edge[0:16, 2 * LANES : 3 * LANES]
        rim_send[1, 0:16, :] = edge[0:16, 3 * LANES :]
        rim_send[0, 16:48, :] = edge[16:48, LANES : 2 * LANES]
        rim_send[1, 16:48, :] = edge[16:48, 3 * LANES :]
        d_waits.append(
            [
                wire.one(rim_send.at[1, pl.ds(40, 8)], rim_land.at[0, pl.ds(48, 8)], wire.near(1, 1)),
                wire.one(
                    rim_send.at[:, pl.ds(16, 32)], rim_land.at[:, pl.ds(16, 32)], wire.near(0, 1)
                ),
                wire.one(rim_send.at[:, pl.ds(0, 16)], rim_land.at[:, pl.ds(0, 16)], wire.near(1, 0)),
            ]
        )

    y1 = ref.y1
    first_col = jnp.bitwise_and(iota((PIXELS, LANES), 0), HALF_COLS - 1) == 0
    no_row = jnp.zeros((HALF_COLS, LANES), BF16)
    for pair in range(PAIRS):
        grid = low(dot_nn(place[pair], planes_of[pair]))
        still = [grid[:, q * LANES : (q + 1) * LANES] for q in range(4)]
        moved = {q: jnp.where(first_col, 0.0, pltpu.roll(still[q], 1, axis=0)) for q in (1, 3)}
        for t in range(TAPS):
            a, b = t // 3, t % 3
            plane = 2 * (a != 1) + (b != 1)
            window = (moved[plane] if b == 0 else still[plane]).astype(BF16)
            if a == 0:
                window = jnp.concatenate([no_row, window[: PIXELS - HALF_COLS, :]], axis=0)
            ref.im1[pair, :, t * LANES : (t + 1) * LANES] = window
        y1[pair] = dot_nn(ref.im1[pair], ref.wide1[...])

    e_waits, e_edges = [], []
    for pair in range(PAIRS):
        for wait in d_waits[pair]:
            wait.wait_recv()
        rim_land = ref.rim_land.at[pair]
        rows_in = [rim_land[p, 0:16, :] * up for p in range(2)]
        cols_in = [rim_land[p, 16:48, :] * left for p in range(2)]
        corner = rim_land[0, 55:56, :] * (up * left)
        top = [
            jnp.where(iota((16, LANES), 0) == 0, corner, pltpu.roll(rows_in[1], 1, axis=0)),
            rows_in[0],
            rows_in[1],
        ]
        side = [
            jnp.where(iota((32, LANES), 0) == 0, 0.0, pltpu.roll(cols_in[1], 1, axis=0)),
            cols_in[0],
            cols_in[1],
        ]
        ref.top1[pair] = jnp.concatenate(top, axis=1).astype(BF16)
        ref.left1[pair] = jnp.concatenate(side, axis=1).astype(BF16)
        y1[pair, 0:16, :] += dot_nn(ref.top1[pair], ref.wide1[0 : 3 * LANES, :])
        beside = pl.ds(0, HALF_ROWS, stride=HALF_COLS)
        y1.at[pair][beside, :] += dot_nn(ref.left1[pair], ref.side1[...])
        value = y1[pair]
        e_waits.append(global_sums(pair, column_sum(value), column_sum(value * value)))
        e_edges.append(halo_send(y1, 1, pair, True))

    for pair in range(PAIRS):
        for half in range(2):
            for k in range(SLOTS):
                at = 120 + 3 * pair + k
                block = (half * SLOTS + k) * LANES
                along, _ = pixel_of(
                    pieces[2 * half][:, at : at + 1], pieces[2 * half + 1][:, at : at + 1]
                )
                along = jnp.broadcast_to(along, (LANES, LANES))
                for m in range(4):
                    fetch[pair, block : block + LANES, m * LANES : (m + 1) * LANES] = one_hot(
                        iota((LANES, LANES), 1) + m * LANES == along
                    )
    for wait in cot_waits:
        wait.wait_recv()

    norm1, f_waits, f_edges = [], [], []
    y2 = ref.y2
    for pair in range(PAIRS):
        e_waits[pair].wait_recv()
        for wait in e_edges[pair]:
            wait.wait_recv()
        center, factor = norm_of(summed(pair))
        norm1.append((center, factor))
        scaled = (y1[pair] - center) * factor
        pre = scaled * gain1 + bias1
        sigma = sigmoid(pre)
        edge = (ref.halo[1, pair] - center) * factor * gain1 + bias1
        fill_ext(0, pair, low(pre * sigma), low(edge * sigmoid(edge)) * halo_mask)
        for b in range(3):
            window = shifted(0, pair, b, range(EXT_ROWS))
            for a in range(3):
                t = 3 * a + b
                ref.im2[pair, :, t * LANES : (t + 1) * LANES] = jnp.concatenate(
                    window[a : a + HALF_ROWS], axis=0
                )
        value = dot_nn(ref.im2[pair], ref.wide2[...])
        y2[pair] = value
        f_waits.append(global_sums(2 + pair, column_sum(value), column_sum(value * value)))
        f_edges.append(halo_send(y2, 2, pair, True))
        ref.x1[pair] = scaled
        ref.s1[pair] = sigma * (1.0 + pre * (1.0 - sigma))

    def slopes(step, carry):
        s, block = step // 4, lax.rem(step, 4)
        rows = pl.ds(pl.multiple_of(block * 16, 16), 16)
        top = ref.pil[s, rows, :]

        def inner(j, sums):
            sums = list(sums)
            for t in range(2):
                n = 2 * j + t
                pre, active = ref.pre[s, n, rows, :], ref.act[s, n, rows, :]
                sigma = sigmoid(pre)
                share = jnp.exp(active - top) * (sigma + active * (1.0 - sigma))
                ref.share[s, n, rows, :] = share
                sums[0] = sums[0] + share
                sums[1] = sums[1] + share * pre
                for c in range(FEATS):
                    sums[2 + c] = sums[2 + c] + share * pts32[s, pl.ds(c * DEPTH + n, 1), :]
            return tuple(sums)

        zero = jnp.zeros((16, LANES), F32)
        sums = lax.fori_loop(0, DEPTH // 2, inner, (zero,) * (2 + FEATS))
        ref.q_sum[s, 0, rows, :] = sums[0]
        ref.q_sum[s, 1, rows, :] = sums[1]
        for c in range(FEATS):
            ref.t_sum[s, c, rows, :] = sums[2 + c]
        return carry

    lax.fori_loop(0, 2 * SCENES, slopes, 0)

    norm2, g_waits = [], []
    for pair in range(PAIRS):
        f_waits[pair].wait_recv()
        center, factor = norm_of(summed(2 + pair))
        norm2.append((center, factor))
        scaled = (y2[pair] - center) * factor
        pre = scaled * gain2 + bias2
        sigma = sigmoid(pre)
        grad = cot[pair] * (sigma * (1.0 + pre * (1.0 - sigma)))
        g_waits.append(global_sums(4 + pair, column_sum(grad), column_sum(grad * scaled)))
        ref.x2[pair] = scaled
        ref.g2[pair] = grad
        ref.feat[pair] = pre * sigma

    for pair in range(PAIRS):
        grid = ref.feat.at[pair]
        for m in range(HALF_COLS // 2):
            a = grid[pl.ds(2 * m, HALF_ROWS, stride=HALF_COLS), :]
            b = grid[pl.ds(2 * m + 1, HALF_ROWS, stride=HALF_COLS), :]
            at = slice(m * LANES, (m + 1) * LANES)
            ref.features[2 * pair, :, at] = jnp.where(first_half, a, roll64(b)).astype(BF16)
            ref.features[2 * pair + 1, :, at] = jnp.where(first_half, roll64(a), b).astype(BF16)
    outs = [wire.local(ref.features, results[0], out_sems, 0)]
    edges2 = []
    for pair in range(PAIRS):
        for wait in f_edges[pair]:
            wait.wait_recv()
        center, factor = norm2[pair]
        scaled = (ref.halo[2, pair] - center) * factor
        pre = scaled * gain2 + bias2
        sigma = sigmoid(pre)
        edges2.append((scaled, ref.halo[0, pair] * (sigma * (1.0 + pre * (1.0 - sigma)))))
    lax.fori_loop(2 * SCENES, 4 * SCENES, slopes, 0)

    total2, h_waits, h_edges = [], [], []
    for pair in range(PAIRS):
        g_waits[pair].wait_recv()
        sums = summed(4 + pair)
        total2.append(sums)
        scale = norm2[pair][1] * gain2
        mean_grad, mean_scaled = sums[0:1, :] / pixel_total, sums[1:2, :] / pixel_total
        inner = low(scale * (ref.g2[pair] - mean_grad - ref.x2[pair] * mean_scaled))
        edge_scaled, edge_grad = edges2[pair]
        edge = low(scale * (edge_grad - mean_grad - edge_scaled * mean_scaled)) * halo_mask
        ref.d2[pair] = inner.astype(BF16)
        fill_ext(1, pair, inner, edge)
        blocks = [None] * TAPS
        for b in range(3):
            window = shifted(1, pair, 2 - b, range(EXT_ROWS))
            for a in range(3):
                blocks[3 * a + b] = jnp.concatenate(window[2 - a : 2 - a + HALF_ROWS], axis=0)
        grad = dot_nn(jnp.concatenate(blocks, axis=1), ref.back2[...]) * ref.s1[pair]
        ref.g1[pair] = grad
        h_waits.append(global_sums(6 + pair, column_sum(grad), column_sum(grad * ref.x1[pair])))
        h_edges.append(halo_send(ref.g1, 3, pair, False))

    def both_halves(product):
        return product[0:CH, :] + roll64(product[CH:LANES, :])

    dk = ref.dk
    for t in range(TAPS):
        tap = slice(t * LANES, (t + 1) * LANES)
        product = dot_tn(ref.im2[0, :, tap], ref.d2[0]) + dot_tn(ref.im2[1, :, tap], ref.d2[1])
        dk[t * CH : (t + 1) * CH, :] = roll64(both_halves(product))

    total1, y_waits = [], []
    for pair in range(PAIRS):
        h_waits[pair].wait_recv()
        for wait in h_edges[pair]:
            wait.wait_recv()
        sums = summed(6 + pair)
        total1.append(sums)
        center, factor = norm1[pair]
        scale = factor * gain1
        mean_grad, mean_scaled = sums[0:1, :] / pixel_total, sums[1:2, :] / pixel_total
        inner = low(scale * (ref.g1[pair] - mean_grad - ref.x1[pair] * mean_scaled))
        edge_scaled = (ref.halo[1, pair] - center) * factor
        edge = low(scale * (ref.halo[3, pair] - mean_grad - edge_scaled * mean_scaled))
        edge = jnp.where(halo_mask > 0.0, edge, 0.0)
        ref.d1[pair] = inner
        fill_ext(2, pair, inner, edge)
        here = shifted(2, pair, 1, range(1, EXT_ROWS))
        beside = shifted(2, pair, 2, range(1, EXT_ROWS))
        windows = [here[:HALF_ROWS], beside[:HALF_ROWS], here[1:], beside[1:]]
        windows = jnp.concatenate([jnp.concatenate(w, axis=0) for w in windows], axis=1)
        value = dot_nn(windows, ref.back1[...]).astype(BF16)
        value = dot_nn(fetch[pair], value)
        y_send = ref.y_send.at[pair].reshape(128 * 8, LANES)
        chosen = []
        for block in range(2 * SLOTS):
            rows = slice(block * LANES, (block + 1) * LANES)
            picked = value[rows, 0:LANES] * parity[pair, rows, 0:LANES].astype(F32)
            for q in range(1, 4):
                tile = slice(q * LANES, (q + 1) * LANES)
                picked = picked + value[rows, tile] * parity[pair, rows, tile].astype(F32)
            chosen.append(picked)
        for k in range(SLOTS):
            y_send[pl.ds(k, 128, stride=8), :] = jnp.where(first_half, chosen[k], chosen[SLOTS + k])
        ref.y_land[pair, 0, 0:SLOTS, :] = ref.y_send[pair, 0, 0:SLOTS, :]
        y_waits.append(
            wire.spread(
                total,
                lambda i: wire.any_peer(-i),
                lambda i, pair=pair: ref.y_send.at[pair, i, pl.ds(0, SLOTS)],
                lambda i, pair=pair: ref.y_land.at[pair, i, pl.ds(0, SLOTS)],
                ref.y_land.at[pair, pl.ds(1, total - 1), pl.ds(0, SLOTS)],
            )
        )

    upper, lefts = jnp.zeros((3 * LANES, LANES), F32), jnp.zeros((3 * LANES, LANES), F32)
    own1 = [ref.d1[pair].astype(BF16) for pair in range(PAIRS)]
    for pair in range(PAIRS):
        beside = ref.d1.at[pair][pl.ds(0, HALF_ROWS, stride=HALF_COLS), :].astype(BF16)
        upper = upper + dot_tn(ref.top1[pair], own1[pair][0:HALF_COLS, :])
        lefts = lefts + dot_tn(ref.left1[pair], beside)
    for t in range(TAPS):
        tap = slice(t * LANES, (t + 1) * LANES)
        product = dot_tn(ref.im1[0, :, tap], own1[0]) + dot_tn(ref.im1[1, :, tap], own1[1])
        if t < 3:
            product = product + upper[tap, :]
        if t % 3 == 0:
            product = product + lefts[t // 3 * LANES : (t // 3 + 1) * LANES, :]
        at = slice(t * CH, (t + 1) * CH)
        dk[at, :] = jnp.where(first_half, both_halves(product), dk[at, :])
    padding = jnp.zeros((PAD_ROWS - OWN_ROWS, LANES), F32)
    for i in range(n_rows):
        owner = lax.rem(row + i, n_rows)
        block = dk[pl.ds(pl.multiple_of(owner * OWN_ROWS, 8), OWN_ROWS), :]
        block = jnp.concatenate([block, padding], axis=0).astype(BF16)
        ref.g_send[i] = block
        if i == 0:
            ref.g_land[0] = block
    g1_wait = wire.spread(
        n_rows,
        wire.row_peer,
        lambda i: ref.g_send.at[i],
        lambda i: ref.g_land.at[i],
        ref.g_land.at[pl.ds(1, n_rows - 1)],
    )
    scales = square_of(jnp.concatenate([norm0[s][2] for s in range(SCENES)], axis=0))
    scales = jnp.transpose(scales)[0:CH, :]

    k_waits = []
    ones = jnp.ones((8, LANES), F32)
    for pair in range(PAIRS):
        y_waits[pair].wait_recv()
        y_land = ref.y_land.at[pair].reshape(128 * 8, LANES)
        landed = [jnp.transpose(y_land[pl.ds(k, 128, stride=8), :]) for k in range(SLOTS)]
        landed = jnp.concatenate(landed, axis=1).astype(BF16)
        parts = [[], []]
        for half in range(2):
            s = 2 * pair + half
            pick = jnp.concatenate([hot[s * SLOTS + k] for k in range(SLOTS)], axis=0)
            grad = dot_nn(landed[half * CH : (half + 1) * CH, :], pick)
            ref.grads[s] = grad
            for kind in range(2):
                parts[kind].append(grad * ref.q_sum[s, kind])
        sums = [dot_nt(ones, jnp.concatenate(part, axis=0), HIGH)[0:1, :] for part in parts]
        k_waits.append(global_sums(8 + pair, *sums))

    scaled_grads = [ref.grads[s] * scales[:, s : s + 1] for s in range(SCENES)]
    weight_grad = jnp.zeros((CH, LANES), F32)
    for c in range(FEATS):
        product = scaled_grads[0] * ref.t_sum[0, c]
        for s in range(1, SCENES):
            product = product + scaled_grads[s] * ref.t_sum[s, c]
        weight_grad = jnp.where(lane == c, jnp.sum(product, axis=1, keepdims=True), weight_grad)
    ref.p_col[...] = weight_grad
    for i in range(n_rows):
        owner = lax.rem(row + i, n_rows)
        block = ref.p_col[pl.ds(pl.multiple_of(owner * 8, 8), 8), :]
        ref.p_send[i] = block
        if i == 0:
            ref.p_land[0] = block
    p_wait = wire.spread(
        n_rows,
        wire.row_peer,
        lambda i: ref.p_send.at[i],
        lambda i: ref.p_land.at[i],
        ref.p_land.at[pl.ds(1, n_rows - 1)],
    )
    g1_wait.wait_recv()
    block = jnp.sum(ref.g_land[...].astype(F32), axis=0).astype(BF16)
    ref.g2_send[...] = block
    ref.g2_land[0] = block
    g2_wait = wire.spread(
        n_cols,
        wire.col_peer,
        lambda i: ref.g2_send,
        lambda i: ref.g2_land.at[i],
        ref.g2_land.at[pl.ds(1, n_cols - 1)],
    )

    def update(s):
        scaled_w = w_row * norm0[s][2]
        coarse = low(scaled_w)
        matrix = jnp.where(first_half, coarse, roll64(scaled_w - coarse)).astype(BF16)
        grad = ref.grads[s]
        for j in range(DEPTH // 4):
            block = [(ref.share[s, 4 * j + t] * grad).astype(BF16) for t in range(4)]
            block = jnp.concatenate(block, axis=1)
            ref.upd[s, :, j * 4 * LANES : (j + 1) * 4 * LANES] = dot_nn(
                matrix, jnp.concatenate([block, block], axis=0)
            )

    update(0)
    update(1)
    p_wait.wait_recv()
    block = jnp.sum(ref.p_land[...], axis=0)
    ref.p2_send[...] = block
    ref.p2_land[0] = block
    p2_wait = wire.spread(
        n_cols,
        wire.col_peer,
        lambda i: ref.p2_send,
        lambda i: ref.p2_land.at[i],
        ref.p2_land.at[pl.ds(1, n_cols - 1)],
    )
    update(2)
    update(3)

    bias_sum, gain_sum = jnp.zeros((1, LANES), F32), jnp.zeros((1, LANES), F32)
    correction = jnp.zeros((16, LANES), F32)
    gain_safe = jnp.where(first_half, gain0, 1.0)
    for pair in range(PAIRS):
        k_waits[pair].wait_recv()
        sums = summed(8 + pair)
        for half in range(2):
            s = 2 * pair + half
            center, factor, scale, count, cross, products = norm0[s]
            own = jnp.where(first_half, roll64(sums) if half else sums, 0.0)
            grad_sum = own[0:1, :]
            scaled_sum = (own[1:2, :] - bias0 * grad_sum) / gain_safe
            bias_sum, gain_sum = bias_sum + grad_sum, gain_sum + scaled_sum
            grad_mean, scaled_mean = grad_sum / count, scaled_sum / count
            point_sums = products[:, 9:10]
            correction = correction + scale * (
                grad_mean * point_sums + scaled_mean * factor * (cross - center * point_sums)
            )
            unit = w_row * factor - jnp.where(feature_row == FEATS, center * factor, 0.0)
            unit = unit * scaled_mean + jnp.where(feature_row == FEATS, grad_mean, 0.0)
            mix = dot_nt(w_row * scale, unit, HIGH)
            coarse = low(mix)
            mix = jnp.concatenate([coarse, mix - coarse], axis=1).astype(BF16)
            out = ref.point_grads.at[s]
            for j in range(DEPTH // 4):
                lanes = slice(j * 4 * LANES, (j + 1) * 4 * LANES)
                points = aug[s, :, lanes]
                value = ref.upd[s, :, lanes] - dot_nn(
                    mix, jnp.concatenate([points, points], axis=0)
                )
                for t in range(4):
                    n = 4 * j + t
                    at = slice(t * LANES, (t + 1) * LANES)
                    out[pl.ds(n, 8, stride=DEPTH), :] = value[0:8, at]
                    out[8 * DEPTH + n : 8 * DEPTH + n + 1, :] = value[8:9, at]
        scenes = pl.ds(2 * pair, 2)
        outs.append(
            wire.local(ref.point_grads.at[scenes], results[1].at[scenes], out_sems, 1 + pair)
        )

    def own_lanes(values):
        return pltpu.roll(values, lax.rem(LANES - 8 * row, LANES), axis=1)

    def both_scenes(values, index):
        added = values[0][index : index + 1, :] + values[1][index : index + 1, :]
        return added + roll64(added)

    small = ref.small
    small[...] = jnp.zeros((8, LANES), F32)
    small[0:1, :] = bias_sum
    small[1:2, :] = both_scenes(total1, 0)
    small[2:3, :] = both_scenes(total2, 0)
    small[3:4, :] = gain_sum
    small[4:5, :] = both_scenes(total1, 1)
    small[5:6, :] = both_scenes(total2, 1)
    owned = own_lanes(small[...])
    ref.bias_grad[...] = owned[0:3, 0:8]
    ref.gain_grad[...] = owned[3:6, 0:8]
    outs.append(wire.local(ref.gain_grad, results[4], out_sems, 3))
    outs.append(wire.local(ref.bias_grad, results[5], out_sems, 4))
    correction = jnp.transpose(square_of(own_lanes(correction)))
    p2_wait.wait_recv()
    block = jnp.sum(ref.p2_land[...], axis=0)
    ref.pfn_grad[...] = (block - correction[0:8, :])[:, 0:FEATS]
    outs.append(wire.local(ref.pfn_grad, results[2], out_sems, 5))
    g2_wait.wait_recv()
    block = jnp.transpose(square_of(jnp.sum(ref.g2_land[...].astype(F32), axis=0)))
    ref.conv_grad[0] = block[0:CH, 0:OWN_ROWS]
    ref.conv_grad[1] = block[CH:LANES, 0:OWN_ROWS]
    outs.append(wire.local(ref.conv_grad, results[3], out_sems, 6))
    for copy in outs:
        copy.wait()
    wire.settle()


def result_kernel(*refs):
    given, results, held = refs[:RESULTS], refs[RESULTS : 2 * RESULTS], refs[2 * RESULTS : -2]
    in_sems, out_sems = refs[-2:]
    order = (1, 0, 3, 2, 4, 5)
    there = {i: pltpu.make_async_copy(given[i], held[i], in_sems.at[i]) for i in order}
    back = {i: pltpu.make_async_copy(held[i], results[i], out_sems.at[i]) for i in order}
    for i in order:
        there[i].start()
    for i in order:
        there[i].wait()
        back[i].start()
    for i in order:
        back[i].wait()


def body(points, counts, tiles, cells, pfn_weight, conv_weight, norm_gain, norm_bias, cotangent):
    scenes, feats, depth, pillars = points.shape
    n_rows, n_cols = lax.axis_size("rows"), lax.axis_size("cols")
    anywhere = pl.BlockSpec(memory_space=pl.ANY)
    shapes = [
        jax.ShapeDtypeStruct(cotangent.shape, BF16),
        jax.ShapeDtypeStruct((scenes, feats * depth, pillars), F32),
        jax.ShapeDtypeStruct(pfn_weight.shape[::-1], F32),
        jax.ShapeDtypeStruct((2, CH, OWN_ROWS), F32),
        jax.ShapeDtypeStruct(norm_gain.shape, F32),
        jax.ShapeDtypeStruct(norm_bias.shape, F32),
    ]
    results = pl.pallas_call(
        functools.partial(step_kernel, n_rows, n_cols),
        out_shape=shapes,
        in_specs=[anywhere] * INPUTS,
        out_specs=[anywhere] * RESULTS,
        scratch_shapes=[pltpu.VMEM(shape, dtype) for shape, dtype in SCRATCH.values()]
        + [
            pltpu.SemaphoreType.DMA((SEMS,)),
            pltpu.SemaphoreType.DMA((SEMS,)),
            pltpu.SemaphoreType.DMA((INPUTS,)),
            pltpu.SemaphoreType.DMA((8,)),
        ],
        compiler_params=pltpu.CompilerParams(
            collective_id=0, has_side_effects=True, vmem_limit_bytes=60 * 2**20
        ),
    )(
        points.reshape(scenes, feats * depth, pillars),
        counts,
        tiles.reshape(scenes, pillars),
        cells,
        pfn_weight.T,
        conv_weight.transpose(0, 2, 1),
        norm_gain,
        norm_bias,
        cotangent,
    )
    results = pl.pallas_call(
        result_kernel,
        out_shape=shapes,
        in_specs=[anywhere] * RESULTS,
        out_specs=[anywhere] * RESULTS,
        scratch_shapes=[pltpu.VMEM(shape.shape, shape.dtype) for shape in shapes]
        + [pltpu.SemaphoreType.DMA((RESULTS,)), pltpu.SemaphoreType.DMA((RESULTS,))],
    )(*results)
    return (
        results[0],
        results[1].reshape(points.shape),
        results[2].T,
        results[3].transpose(0, 2, 1),
        results[4],
        results[5],
    )


def solution(mesh):
    in_specs = (
        P(None, None, None, ("rows", "cols")),
        P(None, ("rows", "cols")),
        P(None, ("rows", "cols"), None),
        P(None, ("rows", "cols")),
        P(None, "rows"),
        P(None, "rows", None),
        P(None, "rows"),
        P(None, "rows"),
        P(None, "rows", "cols"),
    )
    out_specs = (
        P(None, "rows", "cols"),
        P(None, None, None, ("rows", "cols")),
        P(None, "rows"),
        P(None, "rows", None),
        P(None, "rows"),
        P(None, "rows"),
    )
    return jax.shard_map(body, mesh=mesh, in_specs=in_specs, out_specs=out_specs, check_vma=False)
```

time: 121 us -> 87.9 us (0.73)
  Pallas kernels: 110 us -> 86.7 us
  local copies, waits for them, and re-layouts: 9.58 us -> 0 us
    pallas_call x1, Pallas kernels: 110 us -> 84.6 us  [body(): pl.pallas_call(functools.partial(step_kernel, n_rows, n_cols), out_shape=...]
    unnamed x16 -> x0, local copies, waits for them, and re-layouts: 9.58 us -> none
    pallas_call x0 -> x1, Pallas kernels: none -> 2.09 us  [body(): pl.pallas_call(result_kernel, out_shape=shapes, in_specs=[anywhere] * RES...]
where the time goes in v2:
time: 87.9 us; the launch traced here: 87.5 us
  Pallas kernels  86.7 us (99%)
    pallas_call x1, Pallas kernels, body(): pl.pallas_call(functools.partial(step_kernel, n_rows, n_cols), out_shape=...  84.6 us
    pallas_call x1, Pallas kernels, body(): pl.pallas_call(result_kernel, out_shape=shapes, in_specs=[anywhere] * RES...  2.09 us

profile of v2, /device:TPU:0, one launch (start us, length us, event | category | flops | bytes accessed | tf_op | source)
XLA Modules:
  0.0 87.5 jit_solution(13618144062182960387)
XLA Ops:
  0.6 84.6 %shard_map.136 = (bf16[4,32,1024]{2,1,0:T(8,128)(2,1)}, f32[4,288,128]{2,1,0:T(8,128)}, f32[8,9]{1,0:T(8,128)}, f32[2,64,72]{2,1,0:T(8,128)}, f32[3,8]{1,0:T(4,128)}, /*index=5*/f32[3,8]{1,0:T(4,128)}) custom-call(bf16[4,288,128]{2,1,0:T(8,128)(2,1)} %bitcast.7, s32[4,128]{1,0:T(4,128)} %refs_1_.1, s32[4,128]{1,0:T(4,128)} %bitcast.9, s32[4,128]{1,0:T(4,128)} %refs_3_.1, ...), custom_call_target="tpu_custom_call" | custom-call | tf_op jit(solution)/shard_map/pallas_call | solution.py:1063
  85.2 2.1 %shard_map.137 = (bf16[4,32,1024]{2,1,0:T(8,128)(2,1)}, f32[4,288,128]{2,1,0:T(8,128)}, f32[8,9]{1,0:T(8,128)}, f32[2,64,72]{2,1,0:T(8,128)}, f32[3,8]{1,0:T(4,128)}, /*index=5*/f32[3,8]{1,0:T(4,128)}) custom-call(bf16[4,32,1024]{2,1,0:T(8,128)(2,1)} %get-tuple-element.18.refs_0_, f32[4,288,128]{2,1,0:T(8,128)} %get-tuple-element.19.refs_1_, ...), custom_call_target="tpu_custom_call" | custom-call | tf_op jit(solution)/shard_map/pallas_call | solution.py:1089

commit v3 on v2

--- a/solution.py
+++ b/solution.py
@@ -85,12 +85,6 @@
     gain=((3, 8), BF16),
     bias=((3, 8), BF16),
     cotangent=((SCENES, HALF_ROWS, HALF_COLS * CH), BF16),
-    features=((SCENES, HALF_ROWS, HALF_COLS * CH), BF16),
-    point_grads=((SCENES, FEATS * DEPTH, LANES), F32),
-    pfn_grad=((8, FEATS), F32),
-    conv_grad=((2, CH, OWN_ROWS), F32),
-    gain_grad=((3, 8), F32),
-    bias_grad=((3, 8), F32),
     square=((LANES, LANES), F32),
     w_tmp=((16, LANES), F32),
     w_send=((16, LANES), F32),
@@ -106,8 +100,15 @@
     pts32=((SCENES, 16 * DEPTH, LANES), F32),
     aug=((SCENES, 16, DEPTH * LANES), BF16),
     hot=((SCENES * SLOTS, LANES, LANES), BF16),
-    b_send=((128, 8, LANES), F32),
-    b_land=((128, 8, LANES), F32),
+    m_send=((2, 4, LANES), F32),
+    m_land=((8, 4, LANES), F32),
+    m2_land=((16, 4, LANES), F32),
+    hello=((4, 4, LANES), F32),
+    spots=((LANES, LANES), F32),
+    cell_send=((8, 16, LANES), F32),
+    cell_land=((8, 16, LANES), F32),
+    cell2_send=((16, 8, LANES), F32),
+    cell2_land=((16, 8, LANES), F32),
     gram=((SCENES, 16, LANES), F32),
     place=((PAIRS, PIXELS, 6 * LANES), BF16),
     rim=((PAIRS, 48, 6 * LANES), BF16),
@@ -164,28 +165,48 @@
 SEMS = 96
 
 
+HIGH_BITS, LOW_BITS = 0b1010101, 0b0101010
+
+
+def digits_add(a, b):
+    carried = jnp.bitwise_and(a, LOW_BITS) + jnp.bitwise_and(b, LOW_BITS)
+    return jnp.bitwise_xor(carried, jnp.bitwise_and(jnp.bitwise_xor(a, b), HIGH_BITS))
+
+
+def digits_sub(a, b):
+    borrowed = jnp.bitwise_or(a, HIGH_BITS) - jnp.bitwise_and(b, LOW_BITS)
+    kept = jnp.bitwise_and(jnp.bitwise_xor(jnp.bitwise_xor(a, b), HIGH_BITS), HIGH_BITS)
+    return jnp.bitwise_xor(borrowed, kept)
+
+
+def far_first(step):
+    return jnp.bitwise_xor(step, jnp.bitwise_and(jnp.right_shift(step, 1), LOW_BITS))
+
+
 class Wire:
     def __init__(self, n_rows, n_cols, send_sems, recv_sems):
         self.n_rows, self.n_cols = n_rows, n_cols
         self.total = n_rows * n_cols
         self.row, self.col = lax.axis_index("rows"), lax.axis_index("cols")
-        self.me = self.row * n_cols + self.col
+        self.me = self.col * n_rows + self.row
         self.send_sems, self.recv_sems = send_sems, recv_sems
         self.used = 0
         self.sent = []
 
-    def any_peer(self, step):
-        other = jnp.bitwise_and(self.me + step, self.total - 1)
+    def place(self, number):
         return (
-            jnp.right_shift(other, self.n_cols.bit_length() - 1),
-            jnp.bitwise_and(other, self.n_cols - 1),
+            jnp.bitwise_and(number, self.n_rows - 1),
+            jnp.right_shift(number, self.n_rows.bit_length() - 1),
         )
 
-    def row_peer(self, step):
-        return (lax.rem(self.row + step + self.n_rows, self.n_rows), self.col)
-
-    def col_peer(self, step):
-        return (self.row, lax.rem(self.col + step + self.n_cols, self.n_cols))
+    def peer(self, step):
+        return self.place(digits_add(self.me, step))
+
+    def source(self, step):
+        return self.place(digits_sub(self.me, step))
+
+    def along_cols(self, step):
+        return self.peer(step * self.n_rows)
 
     def near(self, down, right):
         return (
@@ -215,7 +236,8 @@
         sem = self.used
         self.used += 1
 
-        def step(i, carry):
+        def step(j, carry):
+            i = far_first(count - j)
             self.copy(src_of(i), dst_of(i), sem, peer_of(i)).start()
             return carry
 
@@ -237,7 +259,8 @@
 def step_kernel(n_rows, n_cols, *refs):
     inputs, results = refs[:INPUTS], refs[INPUTS : INPUTS + RESULTS]
     ref = types.SimpleNamespace(**dict(zip(SCRATCH, refs[INPUTS + RESULTS :], strict=False)))
-    send_sems, recv_sems, in_sems, out_sems = refs[-4:]
+    ref.features, ref.point_grads, ref.pfn_grad, ref.conv_grad, ref.gain_grad, ref.bias_grad = results
+    send_sems, recv_sems, in_sems = refs[-3:]
     wire = Wire(n_rows, n_cols, send_sems, recv_sems)
     total, row, col, me = wire.total, wire.row, wire.col, wire.me
     lane = iota((1, LANES), 1)
@@ -251,11 +274,9 @@
     loads = {i: wire.local(inputs[i], held[i], in_sems, i) for i in order}
     barrier = pltpu.get_barrier_semaphore()
 
-    def greet(i, carry):
-        pl.semaphore_signal(barrier, inc=1, device_id=wire.any_peer(i), device_id_type=MESH)
-        return carry
-
-    lax.fori_loop(1, total, greet, 0, unroll=8)
+    lines = [i for i in range(1, n_rows)] + [i * 8 for i in (1, 2, 3)] + [i * 32 for i in (1, 2, 3)]
+    for step in lines:
+        pl.semaphore_signal(barrier, inc=1, device_id=wire.peer(step), device_id_type=MESH)
 
     for i in range(INPUTS):
         loads[i].wait()
@@ -287,7 +308,11 @@
     above = iota((LANES, LANES), 0) < iota((LANES, LANES), 1)
     slot_row = iota((LANES, LANES), 0).astype(F32) * 4.0
     for s in range(SCENES):
-        tile = lax.rem(ref.tiles[s : s + 1, :] - me + total, total).astype(F32)
+        tile = ref.tiles[s : s + 1, :]
+        tile = jnp.bitwise_and(tile, n_cols - 1) * n_rows + jnp.right_shift(
+            tile, n_cols.bit_length() - 1
+        )
+        tile = digits_sub(tile, me).astype(F32)
         wide = jnp.broadcast_to(tile, (LANES, LANES))
         same = (jnp.transpose(wide) == wide) & above
         rank = jnp.sum(jnp.where(same, 1.0, 0.0), axis=0, keepdims=True)
@@ -295,19 +320,23 @@
         for k in range(SLOTS):
             hot[s * SLOTS + k] = one_hot(slot_row + float(k) == code)
 
-    b_send = ref.b_send.reshape(128 * 8, LANES)
     lane_row = iota((LANES, LANES), 0)
+    spots = jnp.zeros((LANES, LANES), F32)
     for q in range(4):
-        extra = jnp.zeros((LANES, LANES), F32)
         for pair in range(PAIRS):
             s = 2 * pair + q // 2
             cell = ref.cells[s : s + 1, :]
             spot = (jnp.bitwise_and(cell, 31) if q % 2 else jnp.right_shift(cell, 5)) + 1
             for k in range(SLOTS):
-                at = jnp.where(lane_row == 120 + 3 * pair + k, spot.astype(F32), 0.0)
-                extra = extra + dot_nt(hot[s * SLOTS + k], at.astype(BF16))
-        b_send[pl.ds(q, 128, stride=8), :] = extra + moments[q : q + 1, :]
-    ref.b_land[0, 0:4, :] = ref.b_send[0, 0:4, :]
+                at = jnp.where(lane_row == q * 8 + 3 * pair + k, spot.astype(F32), 0.0)
+                spots = spots + dot_nt(hot[s * SLOTS + k], at.astype(BF16))
+    ref.spots[...] = spots
+    for i in range(n_rows):
+        ref.cell_send[i] = ref.spots[pl.ds(i, n_cols, stride=n_rows), :]
+    ref.cell_land[0] = ref.cell_send[0]
+    ref.m_send[0] = moments
+    ref.m_land[0] = moments
+    ref.hello[0] = moments
 
     ref.square[...] = jnp.zeros((LANES, LANES), F32)
     ref.square[0:8, 0:FEATS] = ref.pfn[...].astype(F32)
@@ -316,20 +345,46 @@
     ref.w_tmp[12:15, 0:8] = ref.bias[...].astype(F32)
     ref.w_send[...] = pltpu.roll(ref.w_tmp[...], row * 8, axis=1)
     ref.w_land[0] = ref.w_send[...]
-    pl.semaphore_wait(barrier, total - 1)
+    pl.semaphore_wait(barrier, len(lines))
+    m_wait = wire.spread(
+        n_rows,
+        wire.peer,
+        lambda i: ref.m_send.at[0],
+        lambda i: ref.m_land.at[i],
+        ref.m_land.at[pl.ds(1, n_rows - 1)],
+    )
+    hello_wait = wire.spread(
+        4,
+        lambda i: wire.peer(i * 8),
+        lambda i: ref.hello.at[0],
+        lambda i: ref.hello.at[i],
+        ref.hello.at[pl.ds(1, 3)],
+    )
     w_wait = wire.spread(
         n_rows,
-        wire.row_peer,
+        wire.peer,
         lambda i: ref.w_send,
         lambda i: ref.w_land.at[i],
         ref.w_land.at[pl.ds(1, n_rows - 1)],
     )
-    b_wait = wire.spread(
-        total,
-        wire.any_peer,
-        lambda i: ref.b_send.at[i, pl.ds(0, 4)],
-        lambda i: ref.b_land.at[i, pl.ds(0, 4)],
-        ref.b_land.at[pl.ds(1, total - 1), pl.ds(0, 4)],
+    cell_wait = wire.spread(
+        n_rows,
+        wire.peer,
+        lambda i: ref.cell_send.at[i],
+        lambda i: ref.cell_land.at[i],
+        ref.cell_land.at[pl.ds(1, n_rows - 1)],
+    )
+    m_wait.wait_recv()
+    hello_wait.wait_recv()
+    moments = jnp.sum(ref.m_land[...], axis=0)
+    ref.m_send[1] = moments
+    ref.m2_land[0] = moments
+    m2_wait = wire.spread(
+        n_cols,
+        wire.along_cols,
+        lambda i: ref.m_send.at[1],
+        lambda i: ref.m2_land.at[i],
+        ref.m2_land.at[pl.ds(1, n_cols - 1)],
     )
 
     def halo_send(values, index, pair, full):
@@ -405,7 +460,7 @@
         land[0] = send[...]
         return wire.spread(
             total,
-            wire.any_peer,
+            wire.peer,
             lambda i: send,
             lambda i: land.at[i],
             land.at[pl.ds(1, total - 1)],
@@ -438,12 +493,24 @@
     )
     ref.c_send[...] = jnp.transpose(ref.square[...])[0:PAD_ROWS, :].astype(BF16)
     ref.c_land[0] = ref.c_send[...]
+    cell_wait.wait_recv()
+    cell_land = ref.cell_land.reshape(n_rows * n_cols, LANES)
+    for i in range(n_cols):
+        ref.cell2_send[i] = cell_land[pl.ds(i, n_rows, stride=n_cols), :]
+    ref.cell2_land[0] = ref.cell2_send[0]
+    cell2_wait = wire.spread(
+        n_cols,
+        wire.along_cols,
+        lambda i: ref.cell2_send.at[i],
+        lambda i: ref.cell2_land.at[i],
+        ref.cell2_land.at[pl.ds(1, n_cols - 1)],
+    )
     w_wait.wait_recv()
-    b_wait.wait_recv()
+    m2_wait.wait_recv()
 
     c_wait = wire.spread(
         n_rows,
-        wire.row_peer,
+        wire.peer,
         lambda i: ref.c_send,
         lambda i: ref.c_land.at[i],
         ref.c_land.at[pl.ds(1, n_rows - 1)],
@@ -459,7 +526,7 @@
     gain0, bias0 = w_full[9:10, :], w_full[12:13, :]
     gain1, bias1 = twice(w_full[10:11, :]), twice(w_full[13:14, :])
     gain2, bias2 = twice(w_full[11:12, :]), twice(w_full[14:15, :])
-    moments = jnp.sum(ref.b_land[:, 0:4, :], axis=0)
+    moments = jnp.sum(ref.m2_land[...], axis=0)
     gram = ref.gram
     norm0, matrices = [], []
     for s in range(SCENES):
@@ -488,9 +555,9 @@
             bound = ref.counts[s : s + 1, :]
             matrix = matrices[s]
 
-            def forward(j, peak, s=s, matrix=matrix, bound=bound):
-                width = STEP * LANES
-                points = aug[s, :, pl.ds(pl.multiple_of(j * width, width), width)]
+            peak = jnp.full((CH, LANES), -1e30, F32)
+            for j in range(DEPTH // STEP):
+                points = aug[s, :, j * STEP * LANES : (j + 1) * STEP * LANES]
                 value = dot_nn(matrix, jnp.concatenate([points, points], axis=0))
                 for t in range(STEP):
                     n = STEP * j + t
@@ -499,16 +566,9 @@
                     ref.pre[s, n] = pre
                     ref.act[s, n] = active
                     peak = jnp.maximum(peak, active)
-                return peak
-
-            peak = lax.fori_loop(0, DEPTH // STEP, forward, jnp.full((CH, LANES), -1e30, F32))
-
-            def gather_exp(j, whole, s=s, peak=peak):
-                for t in range(STEP):
-                    whole = whole + jnp.exp(ref.act[s, STEP * j + t] - peak)
-                return whole
-
-            whole = lax.fori_loop(0, DEPTH // STEP, gather_exp, jnp.zeros((CH, LANES), F32))
+            whole = jnp.zeros((CH, LANES), F32)
+            for n in range(DEPTH):
+                whole = whole + jnp.exp(ref.act[s, n] - peak)
             ref.pil[s] = peak + jnp.log(whole)
         x_send = ref.x_send.at[pair].reshape(128 * 8, LANES)
         a, b = ref.pil[2 * pair].astype(BF16), ref.pil[2 * pair + 1].astype(BF16)
@@ -525,16 +585,16 @@
         x_waits.append(
             wire.spread(
                 total,
-                wire.any_peer,
+                wire.peer,
                 lambda i, pair=pair: ref.x_send.at[pair, i, pl.ds(0, SLOTS)],
                 lambda i, pair=pair: ref.x_land.at[pair, i, pl.ds(0, SLOTS)],
                 ref.x_land.at[pair, pl.ds(1, total - 1), pl.ds(0, SLOTS)],
             )
         )
 
-    b_land = ref.b_land.reshape(128 * 8, LANES)
-    pieces = [b_land[pl.ds(q, 128, stride=8), :] for q in range(4)]
-    turned = [jnp.transpose(piece) for piece in pieces]
+    cell2_wait.wait_recv()
+    along_all = ref.cell2_land[...].reshape(LANES, LANES)
+    across_all = jnp.transpose(along_all)
     place, rim, parity, fetch = ref.place, ref.rim, ref.parity, ref.fetch
 
     def pixel_of(tall, wide):
@@ -548,15 +608,11 @@
     for pair in range(PAIRS):
         for half in range(2):
             for k in range(SLOTS):
-                at = 120 + 3 * pair + k
+                at = 16 * half + 3 * pair + k
                 block = (half * SLOTS + k) * LANES
                 blocks = slice(block, block + LANES)
-                across, _ = pixel_of(
-                    turned[2 * half][at : at + 1, :], turned[2 * half + 1][at : at + 1, :]
-                )
-                _, along = pixel_of(
-                    pieces[2 * half][:, at : at + 1], pieces[2 * half + 1][:, at : at + 1]
-                )
+                across, _ = pixel_of(across_all[at : at + 1, :], across_all[at + 8 : at + 9, :])
+                _, along = pixel_of(along_all[:, at : at + 1], along_all[:, at + 8 : at + 9])
                 along = jnp.broadcast_to(along, (LANES, LANES))
                 for m in range(4):
                     tile = slice(m * LANES, (m + 1) * LANES)
@@ -569,7 +625,7 @@
     c_wait.wait_recv()
     taps = ref.taps
     for i in range(n_rows):
-        owner = lax.rem(row - i + n_rows, n_rows)
+        owner = wire.source(i)[0]
         taps[pl.ds(pl.multiple_of(owner * OWN_ROWS, 8), OWN_ROWS), :] = ref.c_land[i].astype(F32)[
             0:OWN_ROWS, :
         ]
@@ -668,11 +724,9 @@
     for pair in range(PAIRS):
         for half in range(2):
             for k in range(SLOTS):
-                at = 120 + 3 * pair + k
+                at = 16 * half + 3 * pair + k
                 block = (half * SLOTS + k) * LANES
-                along, _ = pixel_of(
-                    pieces[2 * half][:, at : at + 1], pieces[2 * half + 1][:, at : at + 1]
-                )
+                along, _ = pixel_of(along_all[:, at : at + 1], along_all[:, at + 8 : at + 9])
                 along = jnp.broadcast_to(along, (LANES, LANES))
                 for m in range(4):
                     fetch[pair, block : block + LANES, m * LANES : (m + 1) * LANES] = one_hot(
@@ -759,7 +813,6 @@
             at = slice(m * LANES, (m + 1) * LANES)
             ref.features[2 * pair, :, at] = jnp.where(first_half, a, roll64(b)).astype(BF16)
             ref.features[2 * pair + 1, :, at] = jnp.where(first_half, roll64(a), b).astype(BF16)
-    outs = [wire.local(ref.features, results[0], out_sems, 0)]
     edges2 = []
     for pair in range(PAIRS):
         for wait in f_edges[pair]:
@@ -839,7 +892,7 @@
         y_waits.append(
             wire.spread(
                 total,
-                lambda i: wire.any_peer(-i),
+                lambda i: wire.source(i),
                 lambda i, pair=pair: ref.y_send.at[pair, i, pl.ds(0, SLOTS)],
                 lambda i, pair=pair: ref.y_land.at[pair, i, pl.ds(0, SLOTS)],
                 ref.y_land.at[pair, pl.ds(1, total - 1), pl.ds(0, SLOTS)],
@@ -863,7 +916,7 @@
         dk[at, :] = jnp.where(first_half, both_halves(product), dk[at, :])
     padding = jnp.zeros((PAD_ROWS - OWN_ROWS, LANES), F32)
     for i in range(n_rows):
-        owner = lax.rem(row + i, n_rows)
+        owner = wire.peer(i)[0]
         block = dk[pl.ds(pl.multiple_of(owner * OWN_ROWS, 8), OWN_ROWS), :]
         block = jnp.concatenate([block, padding], axis=0).astype(BF16)
         ref.g_send[i] = block
@@ -871,7 +924,7 @@
             ref.g_land[0] = block
     g1_wait = wire.spread(
         n_rows,
-        wire.row_peer,
+        wire.peer,
         lambda i: ref.g_send.at[i],
         lambda i: ref.g_land.at[i],
         ref.g_land.at[pl.ds(1, n_rows - 1)],
@@ -906,14 +959,14 @@
         weight_grad = jnp.where(lane == c, jnp.sum(product, axis=1, keepdims=True), weight_grad)
     ref.p_col[...] = weight_grad
     for i in range(n_rows):
-        owner = lax.rem(row + i, n_rows)
+        owner = wire.peer(i)[0]
         block = ref.p_col[pl.ds(pl.multiple_of(owner * 8, 8), 8), :]
         ref.p_send[i] = block
         if i == 0:
             ref.p_land[0] = block
     p_wait = wire.spread(
         n_rows,
-        wire.row_peer,
+        wire.peer,
         lambda i: ref.p_send.at[i],
         lambda i: ref.p_land.at[i],
         ref.p_land.at[pl.ds(1, n_rows - 1)],
@@ -924,7 +977,7 @@
     ref.g2_land[0] = block
     g2_wait = wire.spread(
         n_cols,
-        wire.col_peer,
+        wire.along_cols,
         lambda i: ref.g2_send,
         lambda i: ref.g2_land.at[i],
         ref.g2_land.at[pl.ds(1, n_cols - 1)],
@@ -950,7 +1003,7 @@
     ref.p2_land[0] = block
     p2_wait = wire.spread(
         n_cols,
-        wire.col_peer,
+        wire.along_cols,
         lambda i: ref.p2_send,
         lambda i: ref.p2_land.at[i],
         ref.p2_land.at[pl.ds(1, n_cols - 1)],
@@ -993,10 +1046,6 @@
                     at = slice(t * LANES, (t + 1) * LANES)
                     out[pl.ds(n, 8, stride=DEPTH), :] = value[0:8, at]
                     out[8 * DEPTH + n : 8 * DEPTH + n + 1, :] = value[8:9, at]
-        scenes = pl.ds(2 * pair, 2)
-        outs.append(
-            wire.local(ref.point_grads.at[scenes], results[1].at[scenes], out_sems, 1 + pair)
-        )
 
     def own_lanes(values):
         return pltpu.roll(values, lax.rem(LANES - 8 * row, LANES), axis=1)
@@ -1016,42 +1065,33 @@
     owned = own_lanes(small[...])
     ref.bias_grad[...] = owned[0:3, 0:8]
     ref.gain_grad[...] = owned[3:6, 0:8]
-    outs.append(wire.local(ref.gain_grad, results[4], out_sems, 3))
-    outs.append(wire.local(ref.bias_grad, results[5], out_sems, 4))
     correction = jnp.transpose(square_of(own_lanes(correction)))
     p2_wait.wait_recv()
     block = jnp.sum(ref.p2_land[...], axis=0)
     ref.pfn_grad[...] = (block - correction[0:8, :])[:, 0:FEATS]
-    outs.append(wire.local(ref.pfn_grad, results[2], out_sems, 5))
     g2_wait.wait_recv()
     block = jnp.transpose(square_of(jnp.sum(ref.g2_land[...].astype(F32), axis=0)))
     ref.conv_grad[0] = block[0:CH, 0:OWN_ROWS]
     ref.conv_grad[1] = block[CH:LANES, 0:OWN_ROWS]
-    outs.append(wire.local(ref.conv_grad, results[3], out_sems, 6))
-    for copy in outs:
+    wire.settle()
+
+
+def result_kernel(*refs):
+    sems = refs[-1]
+    copies = [
+        pltpu.make_async_copy(refs[i], refs[RESULTS + i], sems.at[i]) for i in range(RESULTS)
+    ]
+    for copy in copies:
+        copy.start()
+    for copy in copies:
         copy.wait()
-    wire.settle()
-
-
-def result_kernel(*refs):
-    given, results, held = refs[:RESULTS], refs[RESULTS : 2 * RESULTS], refs[2 * RESULTS : -2]
-    in_sems, out_sems = refs[-2:]
-    order = (1, 0, 3, 2, 4, 5)
-    there = {i: pltpu.make_async_copy(given[i], held[i], in_sems.at[i]) for i in order}
-    back = {i: pltpu.make_async_copy(held[i], results[i], out_sems.at[i]) for i in order}
-    for i in order:
-        there[i].start()
-    for i in order:
-        there[i].wait()
-        back[i].start()
-    for i in order:
-        back[i].wait()
 
 
 def body(points, counts, tiles, cells, pfn_weight, conv_weight, norm_gain, norm_bias, cotangent):
     scenes, feats, depth, pillars = points.shape
     n_rows, n_cols = lax.axis_size("rows"), lax.axis_size("cols")
     anywhere = pl.BlockSpec(memory_space=pl.ANY)
+    inside = pl.BlockSpec(memory_space=pltpu.VMEM)
     shapes = [
         jax.ShapeDtypeStruct(cotangent.shape, BF16),
         jax.ShapeDtypeStruct((scenes, feats * depth, pillars), F32),
@@ -1062,18 +1102,17 @@
     ]
     results = pl.pallas_call(
         functools.partial(step_kernel, n_rows, n_cols),
-        out_shape=shapes,
+        out_shape=[pltpu.VMEM(shape.shape, shape.dtype) for shape in shapes],
         in_specs=[anywhere] * INPUTS,
-        out_specs=[anywhere] * RESULTS,
+        out_specs=[inside] * RESULTS,
         scratch_shapes=[pltpu.VMEM(shape, dtype) for shape, dtype in SCRATCH.values()]
         + [
             pltpu.SemaphoreType.DMA((SEMS,)),
             pltpu.SemaphoreType.DMA((SEMS,)),
             pltpu.SemaphoreType.DMA((INPUTS,)),
-            pltpu.SemaphoreType.DMA((8,)),
         ],
         compiler_params=pltpu.CompilerParams(
-            collective_id=0, has_side_effects=True, vmem_limit_bytes=60 * 2**20
+            collective_id=0, has_side_effects=True, vmem_limit_bytes=54 * 2**20
         ),
     )(
         points.reshape(scenes, feats * depth, pillars),
@@ -1089,11 +1128,10 @@
     results = pl.pallas_call(
         result_kernel,
         out_shape=shapes,
-        in_specs=[anywhere] * RESULTS,
+        in_specs=[inside] * RESULTS,
         out_specs=[anywhere] * RESULTS,
-        scratch_shapes=[pltpu.VMEM(shape.shape, shape.dtype) for shape in shapes]
-        + [pltpu.SemaphoreType.DMA((RESULTS,)), pltpu.SemaphoreType.DMA((RESULTS,))],
-    )(*results)
+        scratch_shapes=[pltpu.SemaphoreType.DMA((RESULTS,))],
+    )(*[pltpu.with_memory_space_constraint(result, pltpu.VMEM) for result in results])
     return (
         results[0],
         results[1].reshape(points.shape),

time: 87.9 us -> 82.5 us (0.939)
  Pallas kernels: 86.7 us -> 81 us
    pallas_call x1, Pallas kernels: 84.6 us -> 80 us  [body(): pl.pallas_call(functools.partial(step_kernel, n_rows, n_cols), out_shape=...]
    pallas_call x1, Pallas kernels: 2.09 us -> 0.97 us  [body(): pl.pallas_call(result_kernel, out_shape=shapes, in_specs=[inside] * RESUL...]
where the time goes in v3:
time: 82.5 us; the launch traced here: 81.8 us
  Pallas kernels  81 us (98%)
    pallas_call x1, Pallas kernels, body(): pl.pallas_call(functools.partial(step_kernel, n_rows, n_cols), out_shape=...  80 us

profile of v3, /device:TPU:0, one launch (start us, length us, event | category | flops | bytes accessed | tf_op | source)
XLA Modules:
  0.0 81.8 jit_solution(4999583845174886350)
XLA Ops:
  0.6 80.0 %shard_map.136 = (bf16[4,32,1024]{2,1,0:T(8,128)(2,1)S(1)}, f32[4,288,128]{2,1,0:T(8,128)S(1)}, f32[8,9]{1,0:T(8,128)S(1)}, f32[2,64,72]{2,1,0:T(8,128)S(1)}, f32[3,8]{1,0:T(4,128)S(1)}, /*index=5*/f32[3,8]{1,0:T(4,128)S(1)}) custom-call(bf16[4,288,128]{2,1,0:T(8,128)(2,1)} %bitcast.7, s32[4,128]{1,0:T(4,128)} %refs_1_.1, s32[4,128]{1,0:T(4,128)} %bitcast.9, ...), custom_call_target="tpu_custom_call" | custom-call | tf_op jit(solution)/shard_map/pallas_call | solution.py:1103
  80.6 1.0 %shard_map.137 = (bf16[4,32,1024]{2,1,0:T(8,128)(2,1)}, f32[4,288,128]{2,1,0:T(8,128)}, f32[8,9]{1,0:T(8,128)}, f32[2,64,72]{2,1,0:T(8,128)}, f32[3,8]{1,0:T(4,128)}, /*index=5*/f32[3,8]{1,0:T(4,128)}) custom-call(bf16[4,32,1024]{2,1,0:T(8,128)(2,1)S(1)} %get-tuple-element.18.refs_0_, f32[4,288,128]{2,1,0:T(8,128)S(1)} %get-tuple-element.19.refs_1_, ...), custom_call_target="tpu_custom_call" | custom-call | tf_op jit(solution)/shard_map/pallas_call | solution.py:1128

commit v4 on v3

--- a/solution.py
+++ b/solution.py
@@ -30,6 +30,10 @@
 TAPS = 9
 OWN_ROWS = 72
 PAD_ROWS = 80
+PIECE = 40
+UNROLL = 4
+PARTS = (0, 4, 10, 13)
+BLOCK = 48
 
 
 def dot_nn(a, b, precision=None):
@@ -109,12 +113,13 @@
     cell_land=((8, 16, LANES), F32),
     cell2_send=((16, 8, LANES), F32),
     cell2_land=((16, 8, LANES), F32),
-    gram=((SCENES, 16, LANES), F32),
+    gram=((SCENES * 16, LANES), F32),
     place=((PAIRS, PIXELS, 6 * LANES), BF16),
     rim=((PAIRS, 48, 6 * LANES), BF16),
     parity=((PAIRS, 6 * LANES, 4 * LANES), BF16),
     fetch=((PAIRS, 6 * LANES, PIXELS), BF16),
-    pre=((SCENES, DEPTH, CH, LANES), F32),
+    linear=((SCENES, DEPTH, CH, LANES), F32),
+    halves=((SCENES, 2, CH, LANES), F32),
     act=((SCENES, DEPTH, CH, LANES), F32),
     share=((SCENES, DEPTH, CH, LANES), F32),
     pil=((SCENES, CH, LANES), F32),
@@ -130,6 +135,10 @@
     top1=((PAIRS, 16, 3 * LANES), BF16),
     left1=((PAIRS, 32, 3 * LANES), BF16),
     im2=((PAIRS, PIXELS, TAPS * LANES), BF16),
+    im3=((PAIRS, PIXELS, TAPS * LANES), BF16),
+    im4=((PAIRS, PIXELS, 4 * LANES), BF16),
+    back=((PAIRS, PIXELS, 4 * LANES), BF16),
+    pick_c=((FEATS * LANES, LANES), BF16),
     y1=((PAIRS, PIXELS, LANES), F32),
     y2=((PAIRS, PIXELS, LANES), F32),
     x1=((PAIRS, PIXELS, LANES), F32),
@@ -148,15 +157,14 @@
     st_land=((10, 128, 2, LANES), F32),
     grads=((SCENES, CH, LANES), F32),
     p_col=((CH, LANES), F32),
-    p_send=((8, 8, LANES), F32),
-    p_land=((8, 8, LANES), F32),
-    p2_send=((8, LANES), F32),
-    p2_land=((16, 8, LANES), F32),
-    dk=((TAPS * CH, LANES), F32),
-    g_send=((8, PAD_ROWS, LANES), BF16),
-    g_land=((8, PAD_ROWS, LANES), BF16),
-    g2_send=((PAD_ROWS, LANES), BF16),
-    g2_land=((16, PAD_ROWS, LANES), BF16),
+    k_send=((8, 4, LANES), F32),
+    k_land=((128, 4, LANES), F32),
+    dk=((2, TAPS * CH, LANES), F32),
+    g_send=((2, 8, BLOCK, LANES), BF16),
+    g_land=((2, 8, BLOCK, LANES), BF16),
+    gx_land=((4, BLOCK, LANES), BF16),
+    gz_land=((4, BLOCK, LANES), BF16),
+    gc_land=((16, BLOCK, LANES), BF16),
     upd=((SCENES, 16, DEPTH * LANES), F32),
     small=((8, LANES), F32),
 )
@@ -266,18 +274,17 @@
     lane = iota((1, LANES), 1)
     first_half = lane < CH
 
+    barrier = pltpu.get_barrier_semaphore()
+
+    lines = [i for i in range(1, n_rows)] + [i * 8 for i in (1, 2, 3)] + [i * 32 for i in (1, 2, 3)]
+    for step in lines:
+        pl.semaphore_signal(barrier, inc=1, device_id=wire.peer(step), device_id_type=MESH)
     held = [
         ref.points, ref.counts, ref.tiles, ref.cells, ref.pfn, ref.conv, ref.gain, ref.bias,
         ref.cotangent,
     ]
     order = [1, 0, 2, 3, 4, 6, 7, 5, 8]
     loads = {i: wire.local(inputs[i], held[i], in_sems, i) for i in order}
-    barrier = pltpu.get_barrier_semaphore()
-
-    lines = [i for i in range(1, n_rows)] + [i * 8 for i in (1, 2, 3)] + [i * 32 for i in (1, 2, 3)]
-    for step in lines:
-        pl.semaphore_signal(barrier, inc=1, device_id=wire.peer(step), device_id_type=MESH)
-
     for i in range(INPUTS):
         loads[i].wait()
     pts32, aug = ref.pts32, ref.aug
@@ -367,13 +374,6 @@
         lambda i: ref.w_land.at[i],
         ref.w_land.at[pl.ds(1, n_rows - 1)],
     )
-    cell_wait = wire.spread(
-        n_rows,
-        wire.peer,
-        lambda i: ref.cell_send.at[i],
-        lambda i: ref.cell_land.at[i],
-        ref.cell_land.at[pl.ds(1, n_rows - 1)],
-    )
     m_wait.wait_recv()
     hello_wait.wait_recv()
     moments = jnp.sum(ref.m_land[...], axis=0)
@@ -385,6 +385,14 @@
         lambda i: ref.m_send.at[1],
         lambda i: ref.m2_land.at[i],
         ref.m2_land.at[pl.ds(1, n_cols - 1)],
+    )
+
+    cell_wait = wire.spread(
+        n_rows,
+        wire.peer,
+        lambda i: ref.cell_send.at[i],
+        lambda i: ref.cell_land.at[i],
+        ref.cell_land.at[pl.ds(1, n_rows - 1)],
     )
 
     def halo_send(values, index, pair, full):
@@ -476,23 +484,22 @@
         spread = sums[1:2, :] / pixel_total - center * center
         return center, lax.rsqrt(spread + EPSILON)
 
-    cot = ref.cot
-    for pair in range(PAIRS):
-        spread_to = cot.at[pair]
-        for m in range(HALF_COLS // 2):
-            a = ref.cotangent[2 * pair, :, m * LANES : (m + 1) * LANES].astype(F32)
-            b = ref.cotangent[2 * pair + 1, :, m * LANES : (m + 1) * LANES].astype(F32)
-            spread_to[pl.ds(2 * m, HALF_ROWS, stride=HALF_COLS), :] = jnp.where(
-                first_half, a, roll64(b)
-            )
-            spread_to[pl.ds(2 * m + 1, HALF_ROWS, stride=HALF_COLS), :] = jnp.where(
-                first_half, roll64(a), b
-            )
     ref.square[:, 0:OWN_ROWS] = jnp.concatenate(
         [ref.conv[0].astype(F32), ref.conv[1].astype(F32)], axis=0
     )
     ref.c_send[...] = jnp.transpose(ref.square[...])[0:PAD_ROWS, :].astype(BF16)
     ref.c_land[0] = ref.c_send[...]
+    w_wait.wait_recv()
+    w_full = jnp.sum(ref.w_land[...], axis=0)
+    feature_row = iota((16, LANES), 0)
+    w_row = jnp.where(feature_row < FEATS, w_full, 0.0)
+    matrix = jnp.transpose(square_of(w_row))[0:CH, 0:16].astype(BF16)
+    STEP = 8
+    for s in range(SCENES):
+        for j in range(DEPTH // STEP):
+            value = dot_nn(matrix, aug[s, :, j * STEP * LANES : (j + 1) * STEP * LANES])
+            for t in range(STEP):
+                ref.linear[s, STEP * j + t] = value[:, t * LANES : (t + 1) * LANES]
     cell_wait.wait_recv()
     cell_land = ref.cell_land.reshape(n_rows * n_cols, LANES)
     for i in range(n_cols):
@@ -505,20 +512,8 @@
         lambda i: ref.cell2_land.at[i],
         ref.cell2_land.at[pl.ds(1, n_cols - 1)],
     )
-    w_wait.wait_recv()
     m2_wait.wait_recv()
 
-    c_wait = wire.spread(
-        n_rows,
-        wire.peer,
-        lambda i: ref.c_send,
-        lambda i: ref.c_land.at[i],
-        ref.c_land.at[pl.ds(1, n_rows - 1)],
-    )
-    cot_waits = [wait for pair in range(PAIRS) for wait in halo_send(cot, 0, pair, True)]
-    w_full = jnp.sum(ref.w_land[...], axis=0)
-    feature_row = iota((16, LANES), 0)
-    w_row = jnp.where(feature_row < FEATS, w_full, 0.0)
 
     def twice(v):
         return v + roll64(v)
@@ -528,44 +523,40 @@
     gain2, bias2 = twice(w_full[11:12, :]), twice(w_full[14:15, :])
     moments = jnp.sum(ref.m2_land[...], axis=0)
     gram = ref.gram
-    norm0, matrices = [], []
+    gram[...] = jnp.zeros((SCENES * 16, LANES), F32)
     for s in range(SCENES):
-        gram[s] = jnp.zeros((16, LANES), F32)
         for b in range(3):
             piece = pltpu.roll(moments, (LANES - 40 * b - 10 * s) % LANES, axis=1)
-            gram[s, 4 * b : 4 * b + 4, :] = jnp.where(lane < 10, piece, 0.0)
+            at = 16 * s + 4 * b
+            gram[at : at + 4, :] = jnp.where(lane < 10, piece, 0.0)
+    crosses = dot_nn(gram[:, 0:16], w_row, HIGH)
+    norm0, columns = [], []
     for s in range(SCENES):
-        products = gram[s]
-        cross = dot_nn(products[:, 0:16], w_row, HIGH)
+        products, cross = gram[16 * s : 16 * s + 16, :], crosses[16 * s : 16 * s + 16, :]
         count = products[9:10, 9:10]
         center = cross[9:10, :] / count
         spread = column_sum(w_row * cross) / count - center * center
         factor = lax.rsqrt(spread + EPSILON)
         scale = factor * gain0
         norm0.append((center, factor, scale, count, cross, products))
-        folded = w_row * scale + jnp.where(feature_row == FEATS, bias0 - center * scale, 0.0)
-        coarse = low(folded)
-        both = square_of(jnp.concatenate([coarse, low(folded - coarse)], axis=0))
-        matrices.append(jnp.transpose(both)[0:CH, 0:32].astype(BF16))
-
-    STEP = 8
+        columns += [scale, 0.5 * scale, 0.5 * (bias0 - center * scale)]
+    columns = jnp.transpose(square_of(jnp.concatenate(columns, axis=0)))[0:CH, :]
+    for s in range(SCENES):
+        for kind in range(2):
+            at = 3 * s + 1 + kind
+            ref.halves[s, kind] = jnp.broadcast_to(columns[:, at : at + 1], (CH, LANES))
+
     x_waits = []
     for pair in range(PAIRS):
         for s in (2 * pair, 2 * pair + 1):
             bound = ref.counts[s : s + 1, :]
-            matrix = matrices[s]
-
+            half_scale, half_shift = ref.halves[s, 0], ref.halves[s, 1]
             peak = jnp.full((CH, LANES), -1e30, F32)
-            for j in range(DEPTH // STEP):
-                points = aug[s, :, j * STEP * LANES : (j + 1) * STEP * LANES]
-                value = dot_nn(matrix, jnp.concatenate([points, points], axis=0))
-                for t in range(STEP):
-                    n = STEP * j + t
-                    pre = value[:, t * LANES : (t + 1) * LANES]
-                    active = jnp.where(n < bound, pre * sigmoid(pre), -1e30)
-                    ref.pre[s, n] = pre
-                    ref.act[s, n] = active
-                    peak = jnp.maximum(peak, active)
+            for n in range(DEPTH):
+                half = ref.linear[s, n] * half_scale + half_shift
+                active = jnp.where(n < bound, half * jnp.tanh(half) + half, -1e30)
+                ref.act[s, n] = active
+                peak = jnp.maximum(peak, active)
             whole = jnp.zeros((CH, LANES), F32)
             for n in range(DEPTH):
                 whole = whole + jnp.exp(ref.act[s, n] - peak)
@@ -591,6 +582,43 @@
                 ref.x_land.at[pair, pl.ds(1, total - 1), pl.ds(0, SLOTS)],
             )
         )
+
+    c_wait = wire.spread(
+        n_rows,
+        wire.peer,
+        lambda i: ref.c_send,
+        lambda i: ref.c_land.at[i],
+        ref.c_land.at[pl.ds(1, n_rows - 1)],
+    )
+
+    def slopes(step, carry):
+        s, block = step // 4, lax.rem(step, 4)
+        rows = pl.ds(pl.multiple_of(block * 16, 16), 16)
+        top = ref.pil[s, rows, :]
+        half_scale, half_shift = ref.halves[s, 0, rows, :], ref.halves[s, 1, rows, :]
+
+        def inner(j, sums):
+            sums = list(sums)
+            for t in range(UNROLL):
+                n = UNROLL * j + t
+                line, active = ref.linear[s, n, rows, :], ref.act[s, n, rows, :]
+                half = line * half_scale + half_shift
+                turn = jnp.tanh(half)
+                share = jnp.exp(active - top) * ((0.5 + 0.5 * turn) * (1.0 + half * (1.0 - turn)))
+                ref.share[s, n, rows, :] = share
+                sums[0] = sums[0] + share
+                sums[1] = sums[1] + share * line
+                for c in range(FEATS):
+                    sums[2 + c] = sums[2 + c] + share * pts32[s, pl.ds(c * DEPTH + n, 1), :]
+            return tuple(sums)
+
+        zero = jnp.zeros((16, LANES), F32)
+        sums = lax.fori_loop(0, DEPTH // UNROLL, inner, (zero,) * (2 + FEATS))
+        ref.q_sum[s, 0, rows, :] = sums[0]
+        ref.q_sum[s, 1, rows, :] = sums[1]
+        for c in range(FEATS):
+            ref.t_sum[s, c, rows, :] = sums[2 + c] * (2.0 * half_scale)
+        return carry
 
     cell2_wait.wait_recv()
     along_all = ref.cell2_land[...].reshape(LANES, LANES)
@@ -622,35 +650,7 @@
                     parity[pair, blocks, tile] = one_hot(along == m)
                 rim[pair, :, blocks] = one_hot(rim_pixel == across)
 
-    c_wait.wait_recv()
-    taps = ref.taps
-    for i in range(n_rows):
-        owner = wire.source(i)[0]
-        taps[pl.ds(pl.multiple_of(owner * OWN_ROWS, 8), OWN_ROWS), :] = ref.c_land[i].astype(F32)[
-            0:OWN_ROWS, :
-        ]
-    ref.back1[...] = jnp.zeros((4 * LANES, 4 * LANES), BF16)
-    for t in range(TAPS):
-        both = taps[t * CH : (t + 1) * CH, :]
-        swapped = roll64(both)
-        at = t * LANES
-        k1 = jnp.concatenate(
-            [jnp.where(first_half, both, 0.0), jnp.where(first_half, 0.0, swapped)], axis=0
-        )
-        k2 = jnp.concatenate(
-            [jnp.where(first_half, swapped, 0.0), jnp.where(first_half, 0.0, both)], axis=0
-        )
-        ref.wide1[at : at + LANES, :] = k1.astype(BF16)
-        if t % 3 == 0:
-            ref.side1[t // 3 * LANES : (t // 3 + 1) * LANES, :] = k1.astype(BF16)
-        ref.wide2[at : at + LANES, :] = k2.astype(BF16)
-        ref.back2[at : at + LANES, :] = jnp.transpose(k2).astype(BF16)
-        a, b = t // 3, t % 3
-        window = 2 * (a == 0) + (b == 0)
-        plane = 2 * (a != 1) + (b != 1)
-        ref.back1[
-            window * LANES : (window + 1) * LANES, plane * LANES : (plane + 1) * LANES
-        ] = jnp.transpose(k1).astype(BF16)
+    lax.fori_loop(0, PARTS[0], slopes, 0)
 
     planes_of, d_waits = [], []
     for pair in range(PAIRS):
@@ -677,6 +677,36 @@
                 wire.one(rim_send.at[:, pl.ds(0, 16)], rim_land.at[:, pl.ds(0, 16)], wire.near(1, 0)),
             ]
         )
+
+    c_wait.wait_recv()
+    taps = ref.taps
+    for i in range(n_rows):
+        owner = wire.source(i)[0]
+        taps[pl.ds(pl.multiple_of(owner * OWN_ROWS, 8), OWN_ROWS), :] = ref.c_land[i].astype(F32)[
+            0:OWN_ROWS, :
+        ]
+    ref.back1[...] = jnp.zeros((4 * LANES, 4 * LANES), BF16)
+    for t in range(TAPS):
+        both = taps[t * CH : (t + 1) * CH, :]
+        swapped = roll64(both)
+        at = t * LANES
+        k1 = jnp.concatenate(
+            [jnp.where(first_half, both, 0.0), jnp.where(first_half, 0.0, swapped)], axis=0
+        )
+        k2 = jnp.concatenate(
+            [jnp.where(first_half, swapped, 0.0), jnp.where(first_half, 0.0, both)], axis=0
+        )
+        ref.wide1[at : at + LANES, :] = k1.astype(BF16)
+        if t % 3 == 0:
+            ref.side1[t // 3 * LANES : (t // 3 + 1) * LANES, :] = k1.astype(BF16)
+        ref.wide2[at : at + LANES, :] = k2.astype(BF16)
+        ref.back2[at : at + LANES, :] = jnp.transpose(k2).astype(BF16)
+        a, b = t // 3, t % 3
+        window = 2 * (a == 0) + (b == 0)
+        plane = 2 * (a != 1) + (b != 1)
+        ref.back1[
+            window * LANES : (window + 1) * LANES, plane * LANES : (plane + 1) * LANES
+        ] = jnp.transpose(k1).astype(BF16)
 
     y1 = ref.y1
     first_col = jnp.bitwise_and(iota((PIXELS, LANES), 0), HALF_COLS - 1) == 0
@@ -721,6 +751,22 @@
         e_waits.append(global_sums(pair, column_sum(value), column_sum(value * value)))
         e_edges.append(halo_send(y1, 1, pair, True))
 
+    cot = ref.cot
+    for pair in range(PAIRS):
+        spread_to = cot.at[pair]
+        for m in range(HALF_COLS // 2):
+            a = ref.cotangent[2 * pair, :, m * LANES : (m + 1) * LANES].astype(F32)
+            b = ref.cotangent[2 * pair + 1, :, m * LANES : (m + 1) * LANES].astype(F32)
+            spread_to[pl.ds(2 * m, HALF_ROWS, stride=HALF_COLS), :] = jnp.where(
+                first_half, a, roll64(b)
+            )
+            spread_to[pl.ds(2 * m + 1, HALF_ROWS, stride=HALF_COLS), :] = jnp.where(
+                first_half, roll64(a), b
+            )
+    cot_waits = [wait for pair in range(PAIRS) for wait in halo_send(cot, 0, pair, True)]
+
+    for c in range(FEATS):
+        ref.pick_c[c * LANES : (c + 1) * LANES, :] = one_hot(iota((LANES, LANES), 1) == c)
     for pair in range(PAIRS):
         for half in range(2):
             for k in range(SLOTS):
@@ -732,8 +778,7 @@
                     fetch[pair, block : block + LANES, m * LANES : (m + 1) * LANES] = one_hot(
                         iota((LANES, LANES), 1) + m * LANES == along
                     )
-    for wait in cot_waits:
-        wait.wait_recv()
+    lax.fori_loop(PARTS[0], PARTS[1], slopes, 0)
 
     norm1, f_waits, f_edges = [], [], []
     y2 = ref.y2
@@ -762,34 +807,7 @@
         ref.x1[pair] = scaled
         ref.s1[pair] = sigma * (1.0 + pre * (1.0 - sigma))
 
-    def slopes(step, carry):
-        s, block = step // 4, lax.rem(step, 4)
-        rows = pl.ds(pl.multiple_of(block * 16, 16), 16)
-        top = ref.pil[s, rows, :]
-
-        def inner(j, sums):
-            sums = list(sums)
-            for t in range(2):
-                n = 2 * j + t
-                pre, active = ref.pre[s, n, rows, :], ref.act[s, n, rows, :]
-                sigma = sigmoid(pre)
-                share = jnp.exp(active - top) * (sigma + active * (1.0 - sigma))
-                ref.share[s, n, rows, :] = share
-                sums[0] = sums[0] + share
-                sums[1] = sums[1] + share * pre
-                for c in range(FEATS):
-                    sums[2 + c] = sums[2 + c] + share * pts32[s, pl.ds(c * DEPTH + n, 1), :]
-            return tuple(sums)
-
-        zero = jnp.zeros((16, LANES), F32)
-        sums = lax.fori_loop(0, DEPTH // 2, inner, (zero,) * (2 + FEATS))
-        ref.q_sum[s, 0, rows, :] = sums[0]
-        ref.q_sum[s, 1, rows, :] = sums[1]
-        for c in range(FEATS):
-            ref.t_sum[s, c, rows, :] = sums[2 + c]
-        return carry
-
-    lax.fori_loop(0, 2 * SCENES, slopes, 0)
+    lax.fori_loop(PARTS[1], PARTS[2], slopes, 0)
 
     norm2, g_waits = [], []
     for pair in range(PAIRS):
@@ -815,14 +833,14 @@
             ref.features[2 * pair + 1, :, at] = jnp.where(first_half, roll64(a), b).astype(BF16)
     edges2 = []
     for pair in range(PAIRS):
-        for wait in f_edges[pair]:
+        for wait in f_edges[pair] + cot_waits[8 * pair : 8 * pair + 8]:
             wait.wait_recv()
         center, factor = norm2[pair]
         scaled = (ref.halo[2, pair] - center) * factor
         pre = scaled * gain2 + bias2
         sigma = sigmoid(pre)
         edges2.append((scaled, ref.halo[0, pair] * (sigma * (1.0 + pre * (1.0 - sigma)))))
-    lax.fori_loop(2 * SCENES, 4 * SCENES, slopes, 0)
+    lax.fori_loop(PARTS[2], PARTS[3], slopes, 0)
 
     total2, h_waits, h_edges = [], [], []
     for pair in range(PAIRS):
@@ -836,24 +854,50 @@
         edge = low(scale * (edge_grad - mean_grad - edge_scaled * mean_scaled)) * halo_mask
         ref.d2[pair] = inner.astype(BF16)
         fill_ext(1, pair, inner, edge)
-        blocks = [None] * TAPS
         for b in range(3):
             window = shifted(1, pair, 2 - b, range(EXT_ROWS))
             for a in range(3):
-                blocks[3 * a + b] = jnp.concatenate(window[2 - a : 2 - a + HALF_ROWS], axis=0)
-        grad = dot_nn(jnp.concatenate(blocks, axis=1), ref.back2[...]) * ref.s1[pair]
+                t = 3 * a + b
+                ref.im3[pair, :, t * LANES : (t + 1) * LANES] = jnp.concatenate(
+                    window[2 - a : 2 - a + HALF_ROWS], axis=0
+                )
+        grad = dot_nn(ref.im3[pair], ref.back2[...]) * ref.s1[pair]
         ref.g1[pair] = grad
         h_waits.append(global_sums(6 + pair, column_sum(grad), column_sum(grad * ref.x1[pair])))
         h_edges.append(halo_send(ref.g1, 3, pair, False))
 
-    def both_halves(product):
-        return product[0:CH, :] + roll64(product[CH:LANES, :])
-
-    dk = ref.dk
-    for t in range(TAPS):
-        tap = slice(t * LANES, (t + 1) * LANES)
-        product = dot_tn(ref.im2[0, :, tap], ref.d2[0]) + dot_tn(ref.im2[1, :, tap], ref.d2[1])
-        dk[t * CH : (t + 1) * CH, :] = roll64(both_halves(product))
+    def kernel_grad(grads, windows):
+        product = sum(dot_tn(grads[pair], windows[pair]) for pair in range(PAIRS))
+        taps = [product[:, t * LANES : (t + 1) * LANES] for t in range(windows[0].shape[1] // LANES)]
+        return [tap[0:CH, :] + roll64(tap[CH:LANES, :]) for tap in taps]
+
+    def to_owners(index, grads):
+        dk = ref.dk.at[index]
+        for t in range(0, TAPS, 2):
+            both = [grads[t], grads[min(t + 1, TAPS - 1)]]
+            both = jnp.transpose(jnp.concatenate(both, axis=0))[0:CH, :]
+            dk[t * CH : (t + 1) * CH, :] = both
+            if t + 1 < TAPS:
+                dk[(t + 1) * CH : (t + 2) * CH, :] = roll64(both)
+        none = jnp.zeros((BLOCK - PIECE, LANES), F32)
+        for i in range(n_rows):
+            at = wire.peer(i)[0] * OWN_ROWS
+            first = dk[pl.ds(pl.multiple_of(at, 8), PIECE), :]
+            second = dk[pl.ds(pl.multiple_of(at + OWN_ROWS - PIECE, 8), PIECE), :]
+            block = jnp.where(first_half, first, roll64(second))
+            ref.g_send[index, i] = jnp.concatenate([block, none], axis=0).astype(BF16)
+        ref.g_land[index, 0] = ref.g_send[index, 0]
+        return wire.spread(
+            n_rows,
+            wire.peer,
+            lambda i: ref.g_send.at[index, i],
+            lambda i: ref.g_land.at[index, i],
+            ref.g_land.at[index, pl.ds(1, n_rows - 1)],
+        )
+
+    lax.fori_loop(PARTS[3], 4 * SCENES, slopes, 0)
+    grads2 = kernel_grad([ref.d2[0], ref.d2[1]], [ref.im2[0], ref.im2[1]])
+    g_waits = [to_owners(1, grads2)]
 
     total1, y_waits = [], []
     for pair in range(PAIRS):
@@ -874,9 +918,10 @@
         here = shifted(2, pair, 1, range(1, EXT_ROWS))
         beside = shifted(2, pair, 2, range(1, EXT_ROWS))
         windows = [here[:HALF_ROWS], beside[:HALF_ROWS], here[1:], beside[1:]]
-        windows = jnp.concatenate([jnp.concatenate(w, axis=0) for w in windows], axis=1)
-        value = dot_nn(windows, ref.back1[...]).astype(BF16)
-        value = dot_nn(fetch[pair], value)
+        for w in range(4):
+            ref.im4[pair, :, w * LANES : (w + 1) * LANES] = jnp.concatenate(windows[w], axis=0)
+        ref.back[pair] = dot_nn(ref.im4[pair], ref.back1[...]).astype(BF16)
+        value = dot_nn(fetch[pair], ref.back[pair])
         y_send = ref.y_send.at[pair].reshape(128 * 8, LANES)
         chosen = []
         for block in range(2 * SLOTS):
@@ -899,41 +944,33 @@
             )
         )
 
-    upper, lefts = jnp.zeros((3 * LANES, LANES), F32), jnp.zeros((3 * LANES, LANES), F32)
+    def owned_sum(index):
+        return jnp.sum(ref.g_land[index].astype(F32), axis=0).astype(BF16)
+
+    g_waits[0].wait_recv()
+    ref.gx_land[0] = owned_sum(1)
+    gx_wait = wire.spread(
+        4,
+        lambda i: wire.peer(i * 8),
+        lambda i: ref.gx_land.at[0],
+        lambda i: ref.gx_land.at[i],
+        ref.gx_land.at[pl.ds(1, 3)],
+    )
     own1 = [ref.d1[pair].astype(BF16) for pair in range(PAIRS)]
-    for pair in range(PAIRS):
-        beside = ref.d1.at[pair][pl.ds(0, HALF_ROWS, stride=HALF_COLS), :].astype(BF16)
-        upper = upper + dot_tn(ref.top1[pair], own1[pair][0:HALF_COLS, :])
-        lefts = lefts + dot_tn(ref.left1[pair], beside)
-    for t in range(TAPS):
-        tap = slice(t * LANES, (t + 1) * LANES)
-        product = dot_tn(ref.im1[0, :, tap], own1[0]) + dot_tn(ref.im1[1, :, tap], own1[1])
-        if t < 3:
-            product = product + upper[tap, :]
-        if t % 3 == 0:
-            product = product + lefts[t // 3 * LANES : (t // 3 + 1) * LANES, :]
-        at = slice(t * CH, (t + 1) * CH)
-        dk[at, :] = jnp.where(first_half, both_halves(product), dk[at, :])
-    padding = jnp.zeros((PAD_ROWS - OWN_ROWS, LANES), F32)
-    for i in range(n_rows):
-        owner = wire.peer(i)[0]
-        block = dk[pl.ds(pl.multiple_of(owner * OWN_ROWS, 8), OWN_ROWS), :]
-        block = jnp.concatenate([block, padding], axis=0).astype(BF16)
-        ref.g_send[i] = block
-        if i == 0:
-            ref.g_land[0] = block
-    g1_wait = wire.spread(
-        n_rows,
-        wire.peer,
-        lambda i: ref.g_send.at[i],
-        lambda i: ref.g_land.at[i],
-        ref.g_land.at[pl.ds(1, n_rows - 1)],
-    )
-    scales = square_of(jnp.concatenate([norm0[s][2] for s in range(SCENES)], axis=0))
-    scales = jnp.transpose(scales)[0:CH, :]
+    beside1 = [
+        ref.d1.at[pair][pl.ds(0, HALF_ROWS, stride=HALF_COLS), :].astype(BF16)
+        for pair in range(PAIRS)
+    ]
+    grads = kernel_grad(own1, [ref.im1[0], ref.im1[1]])
+    upper = kernel_grad([own[0:HALF_COLS, :] for own in own1], [ref.top1[0], ref.top1[1]])
+    lefts = kernel_grad(beside1, [ref.left1[0], ref.left1[1]])
+    for t in range(3):
+        grads[t] = grads[t] + upper[t]
+        grads[3 * t] = grads[3 * t] + lefts[t]
+    g_waits.append(to_owners(0, grads))
 
     k_waits = []
-    ones = jnp.ones((8, LANES), F32)
+    ones = jnp.ones((16, 2 * LANES), BF16)
     for pair in range(PAIRS):
         y_waits[pair].wait_recv()
         y_land = ref.y_land.at[pair].reshape(128 * 8, LANES)
@@ -947,40 +984,65 @@
             ref.grads[s] = grad
             for kind in range(2):
                 parts[kind].append(grad * ref.q_sum[s, kind])
-        sums = [dot_nt(ones, jnp.concatenate(part, axis=0), HIGH)[0:1, :] for part in parts]
-        k_waits.append(global_sums(8 + pair, *sums))
-
-    scaled_grads = [ref.grads[s] * scales[:, s : s + 1] for s in range(SCENES)]
+        products = jnp.concatenate(parts[0] + parts[1], axis=0)
+        coarse = low(products)
+        products = jnp.concatenate([coarse, products - coarse], axis=1).astype(BF16)
+        sums = dot_nt(ones, products)
+        sums = (sums[0:1, 0:LANES], sums[0:1, LANES:])
+        if pair == 0:
+            k_waits.append(global_sums(8, *sums))
+            for c in range(FEATS):
+                ref.t_sum[0, c] = ref.grads[0] * ref.t_sum[0, c] + ref.grads[1] * ref.t_sum[1, c]
+            gx_wait.wait_recv()
+            ref.gz_land[0] = jnp.sum(ref.gx_land[...].astype(F32), axis=0).astype(BF16)
+            gz_wait = wire.spread(
+                4,
+                lambda i: wire.peer(i * 32),
+                lambda i: ref.gz_land.at[0],
+                lambda i: ref.gz_land.at[i],
+                ref.gz_land.at[pl.ds(1, 3)],
+            )
+
+    split = [[], []]
+    for c in range(FEATS):
+        product = ref.t_sum[0, c]
+        for s in range(2, SCENES):
+            product = product + ref.grads[s] * ref.t_sum[s, c]
+        coarse = low(product)
+        split[0].append(coarse)
+        split[1].append(product - coarse)
     weight_grad = jnp.zeros((CH, LANES), F32)
-    for c in range(FEATS):
-        product = scaled_grads[0] * ref.t_sum[0, c]
-        for s in range(1, SCENES):
-            product = product + scaled_grads[s] * ref.t_sum[s, c]
-        weight_grad = jnp.where(lane == c, jnp.sum(product, axis=1, keepdims=True), weight_grad)
+    for part in split:
+        weight_grad = weight_grad + dot_nn(
+            jnp.concatenate(part, axis=1).astype(BF16), ref.pick_c[...]
+        )
     ref.p_col[...] = weight_grad
-    for i in range(n_rows):
-        owner = wire.peer(i)[0]
-        block = ref.p_col[pl.ds(pl.multiple_of(owner * 8, 8), 8), :]
-        ref.p_send[i] = block
-        if i == 0:
-            ref.p_land[0] = block
-    p_wait = wire.spread(
-        n_rows,
-        wire.peer,
-        lambda i: ref.p_send.at[i],
-        lambda i: ref.p_land.at[i],
-        ref.p_land.at[pl.ds(1, n_rows - 1)],
-    )
-    g1_wait.wait_recv()
-    block = jnp.sum(ref.g_land[...].astype(F32), axis=0).astype(BF16)
-    ref.g2_send[...] = block
-    ref.g2_land[0] = block
-    g2_wait = wire.spread(
+    packed = jnp.zeros((8, LANES), F32)
+    for k in range(8):
+        packed = packed + pltpu.roll(ref.p_col[pl.ds(k, 8, stride=8), :], 16 * k, axis=1)
+    for r in range(n_rows):
+        ref.k_send[r, 0:1, :] = sums[0]
+        ref.k_send[r, 1:2, :] = sums[1]
+        ref.k_send[r, 2:3, :] = packed[r : r + 1, :]
+        ref.k_send[r, 3:4, :] = packed[r : r + 1, :]
+    ref.k_land[0] = ref.k_send[row]
+    k_waits.append(
+        wire.spread(
+            total,
+            wire.peer,
+            lambda i: ref.k_send.at[wire.peer(i)[0]],
+            lambda i: ref.k_land.at[i],
+            ref.k_land.at[pl.ds(1, total - 1)],
+        )
+    )
+    g_waits[1].wait_recv()
+    ref.gc_land[0] = owned_sum(0)
+    gc_wait = wire.spread(
         n_cols,
         wire.along_cols,
-        lambda i: ref.g2_send,
-        lambda i: ref.g2_land.at[i],
-        ref.g2_land.at[pl.ds(1, n_cols - 1)],
+        lambda i: ref.gc_land.at[0],
+        lambda i: ref.gc_land.at[i],
+        ref.gc_land.at[pl.ds(1, n_cols - 1)],
     )
 
     def update(s):
@@ -995,34 +1057,20 @@
                 matrix, jnp.concatenate([block, block], axis=0)
             )
 
-    update(0)
-    update(1)
-    p_wait.wait_recv()
-    block = jnp.sum(ref.p_land[...], axis=0)
-    ref.p2_send[...] = block
-    ref.p2_land[0] = block
-    p2_wait = wire.spread(
-        n_cols,
-        wire.along_cols,
-        lambda i: ref.p2_send,
-        lambda i: ref.p2_land.at[i],
-        ref.p2_land.at[pl.ds(1, n_cols - 1)],
-    )
-    update(2)
-    update(3)
+    for s in range(SCENES):
+        update(s)
 
     bias_sum, gain_sum = jnp.zeros((1, LANES), F32), jnp.zeros((1, LANES), F32)
     correction = jnp.zeros((16, LANES), F32)
-    gain_safe = jnp.where(first_half, gain0, 1.0)
     for pair in range(PAIRS):
         k_waits[pair].wait_recv()
-        sums = summed(8 + pair)
+        sums = jnp.sum(ref.k_land[...], axis=0) if pair else summed(8)
         for half in range(2):
             s = 2 * pair + half
             center, factor, scale, count, cross, products = norm0[s]
             own = jnp.where(first_half, roll64(sums) if half else sums, 0.0)
             grad_sum = own[0:1, :]
-            scaled_sum = (own[1:2, :] - bias0 * grad_sum) / gain_safe
+            scaled_sum = factor * (own[1:2, :] - center * grad_sum)
             bias_sum, gain_sum = bias_sum + grad_sum, gain_sum + scaled_sum
             grad_mean, scaled_mean = grad_sum / count, scaled_sum / count
             point_sums = products[:, 9:10]
@@ -1035,17 +1083,12 @@
             coarse = low(mix)
             mix = jnp.concatenate([coarse, mix - coarse], axis=1).astype(BF16)
             out = ref.point_grads.at[s]
-            for j in range(DEPTH // 4):
-                lanes = slice(j * 4 * LANES, (j + 1) * 4 * LANES)
-                points = aug[s, :, lanes]
-                value = ref.upd[s, :, lanes] - dot_nn(
-                    mix, jnp.concatenate([points, points], axis=0)
-                )
-                for t in range(4):
-                    n = 4 * j + t
-                    at = slice(t * LANES, (t + 1) * LANES)
-                    out[pl.ds(n, 8, stride=DEPTH), :] = value[0:8, at]
-                    out[8 * DEPTH + n : 8 * DEPTH + n + 1, :] = value[8:9, at]
+            points = aug[s]
+            value = ref.upd[s] - dot_nn(mix, jnp.concatenate([points, points], axis=0))
+            for n in range(DEPTH):
+                at = slice(n * LANES, (n + 1) * LANES)
+                out[pl.ds(n, 8, stride=DEPTH), :] = value[0:8, at]
+                out[8 * DEPTH + n : 8 * DEPTH + n + 1, :] = value[8:9, at]
 
     def own_lanes(values):
         return pltpu.roll(values, lax.rem(LANES - 8 * row, LANES), axis=1)
@@ -1066,13 +1109,14 @@
     ref.bias_grad[...] = owned[0:3, 0:8]
     ref.gain_grad[...] = owned[3:6, 0:8]
     correction = jnp.transpose(square_of(own_lanes(correction)))
-    p2_wait.wait_recv()
-    block = jnp.sum(ref.p2_land[...], axis=0)
+    block = [pltpu.roll(sums[2:3, :], (LANES - 16 * k) % LANES, axis=1) for k in range(8)]
+    block = jnp.concatenate(block, axis=0)
     ref.pfn_grad[...] = (block - correction[0:8, :])[:, 0:FEATS]
-    g2_wait.wait_recv()
-    block = jnp.transpose(square_of(jnp.sum(ref.g2_land[...].astype(F32), axis=0)))
-    ref.conv_grad[0] = block[0:CH, 0:OWN_ROWS]
-    ref.conv_grad[1] = block[CH:LANES, 0:OWN_ROWS]
+    for index, (wait, land) in enumerate([(gc_wait, ref.gc_land), (gz_wait, ref.gz_land)]):
+        wait.wait_recv()
+        block = jnp.transpose(square_of(jnp.sum(land[...].astype(F32), axis=0)))
+        ref.conv_grad[index, :, 0:PIECE] = block[0:CH, 0:PIECE]
+        ref.conv_grad[index, :, OWN_ROWS - PIECE :] = block[CH:LANES, 0:PIECE]
     wire.settle()
 
 

time: 82.5 us -> 79.3 us (0.961)
  Pallas kernels: 81 us -> 77.9 us
    pallas_call x1, Pallas kernels: 80 us -> 76.9 us  [body(): pl.pallas_call(functools.partial(step_kernel, n_rows, n_cols), out_shape=...]
where the time goes in v4:
time: 79.3 us; the launch traced here: 78.7 us
  Pallas kernels  77.9 us (98%)
  between operations  0.8 us (1%)
    pallas_call x1, Pallas kernels, body(): pl.pallas_call(functools.partial(step_kernel, n_rows, n_cols), out_shape=...  76.9 us

profile of v4, /device:TPU:0, one launch (start us, length us, event | category | flops | bytes accessed | tf_op | source)
XLA Modules:
  0.0 78.7 jit_solution(2412866102993196375)
XLA Ops:
  0.6 76.9 %shard_map.136 = (bf16[4,32,1024]{2,1,0:T(8,128)(2,1)S(1)}, f32[4,288,128]{2,1,0:T(8,128)S(1)}, f32[8,9]{1,0:T(8,128)S(1)}, f32[2,64,72]{2,1,0:T(8,128)S(1)}, f32[3,8]{1,0:T(4,128)S(1)}, /*index=5*/f32[3,8]{1,0:T(4,128)S(1)}) custom-call(bf16[4,288,128]{2,1,0:T(8,128)(2,1)} %bitcast.7, s32[4,128]{1,0:T(4,128)} %refs_1_.1, s32[4,128]{1,0:T(4,128)} %bitcast.9, ...), custom_call_target="tpu_custom_call" | custom-call | tf_op jit(solution)/shard_map/pallas_call | solution.py:1147
  77.6 1.0 %shard_map.137 = (bf16[4,32,1024]{2,1,0:T(8,128)(2,1)}, f32[4,288,128]{2,1,0:T(8,128)}, f32[8,9]{1,0:T(8,128)}, f32[2,64,72]{2,1,0:T(8,128)}, f32[3,8]{1,0:T(4,128)}, /*index=5*/f32[3,8]{1,0:T(4,128)}) custom-call(bf16[4,32,1024]{2,1,0:T(8,128)(2,1)S(1)} %get-tuple-element.18.refs_0_, f32[4,288,128]{2,1,0:T(8,128)S(1)} %get-tuple-element.19.refs_1_, ...), custom_call_target="tpu_custom_call" | custom-call | tf_op jit(solution)/shard_map/pallas_call | solution.py:1172

commit v5 on v4

--- a/solution.py
+++ b/solution.py
@@ -157,8 +157,8 @@
     st_land=((10, 128, 2, LANES), F32),
     grads=((SCENES, CH, LANES), F32),
     p_col=((CH, LANES), F32),
-    k_send=((8, 4, LANES), F32),
-    k_land=((128, 4, LANES), F32),
+    k_send=((8, 8, LANES), F32),
+    k_land=((128, 8, LANES), F32),
     dk=((2, TAPS * CH, LANES), F32),
     g_send=((2, 8, BLOCK, LANES), BF16),
     g_land=((2, 8, BLOCK, LANES), BF16),
@@ -993,16 +993,6 @@
             k_waits.append(global_sums(8, *sums))
             for c in range(FEATS):
                 ref.t_sum[0, c] = ref.grads[0] * ref.t_sum[0, c] + ref.grads[1] * ref.t_sum[1, c]
-            gx_wait.wait_recv()
-            ref.gz_land[0] = jnp.sum(ref.gx_land[...].astype(F32), axis=0).astype(BF16)
-            gz_wait = wire.spread(
-                4,
-                lambda i: wire.peer(i * 32),
-                lambda i: ref.gz_land.at[0],
-                lambda i: ref.gz_land.at[i],
-                ref.gz_land.at[pl.ds(1, 3)],
-            )
-
     split = [[], []]
     for c in range(FEATS):
         product = ref.t_sum[0, c]
@@ -1024,17 +1014,26 @@
         ref.k_send[r, 0:1, :] = sums[0]
         ref.k_send[r, 1:2, :] = sums[1]
         ref.k_send[r, 2:3, :] = packed[r : r + 1, :]
-        ref.k_send[r, 3:4, :] = packed[r : r + 1, :]
-    ref.k_land[0] = ref.k_send[row]
+    ref.k_land[0, 0:3, :] = ref.k_send[row, 0:3, :]
     k_waits.append(
         wire.spread(
             total,
             wire.peer,
-            lambda i: ref.k_send.at[wire.peer(i)[0]],
-            lambda i: ref.k_land.at[i],
-            ref.k_land.at[pl.ds(1, total - 1)],
-        )
-    )
+            lambda i: ref.k_send.at[wire.peer(i)[0], pl.ds(0, 3)],
+            lambda i: ref.k_land.at[i, pl.ds(0, 3)],
+            ref.k_land.at[pl.ds(1, total - 1), pl.ds(0, 3)],
+        )
+    )
+    gx_wait.wait_recv()
+    ref.gz_land[0] = jnp.sum(ref.gx_land[...].astype(F32), axis=0).astype(BF16)
+    gz_wait = wire.spread(
+        4,
+        lambda i: wire.peer(i * 32),
+        lambda i: ref.gz_land.at[0],
+        lambda i: ref.gz_land.at[i],
+        ref.gz_land.at[pl.ds(1, 3)],
+    )
+
     g_waits[1].wait_recv()
     ref.gc_land[0] = owned_sum(0)
     gc_wait = wire.spread(
@@ -1064,7 +1063,7 @@
     correction = jnp.zeros((16, LANES), F32)
     for pair in range(PAIRS):
         k_waits[pair].wait_recv()
-        sums = jnp.sum(ref.k_land[...], axis=0) if pair else summed(8)
+        sums = jnp.sum(ref.k_land[:, 0:3, :], axis=0) if pair else summed(8)
         for half in range(2):
             s = 2 * pair + half
             center, factor, scale, count, cross, products = norm0[s]

time: 79.3 us -> 78.9 us (level)
  no operation moved by 1% of the time
where the time goes in v5:
time: 78.9 us; the launch traced here: 78.2 us
  Pallas kernels  77.4 us (98%)
  between operations  0.8 us (1%)
    pallas_call x1, Pallas kernels, body(): pl.pallas_call(functools.partial(step_kernel, n_rows, n_cols), out_shape=...  76.4 us

profile of v5, /device:TPU:0, one launch (start us, length us, event | category | flops | bytes accessed | tf_op | source)
XLA Modules:
  0.0 78.2 jit_solution(10914734981393194329)
XLA Ops:
  0.6 76.4 %shard_map.136 = (bf16[4,32,1024]{2,1,0:T(8,128)(2,1)S(1)}, f32[4,288,128]{2,1,0:T(8,128)S(1)}, f32[8,9]{1,0:T(8,128)S(1)}, f32[2,64,72]{2,1,0:T(8,128)S(1)}, f32[3,8]{1,0:T(4,128)S(1)}, /*index=5*/f32[3,8]{1,0:T(4,128)S(1)}) custom-call(bf16[4,288,128]{2,1,0:T(8,128)(2,1)} %bitcast.7, s32[4,128]{1,0:T(4,128)} %refs_1_.1, s32[4,128]{1,0:T(4,128)} %bitcast.9, ...), custom_call_target="tpu_custom_call" | custom-call | tf_op jit(solution)/shard_map/pallas_call | solution.py:1146
  77.0 1.0 %shard_map.137 = (bf16[4,32,1024]{2,1,0:T(8,128)(2,1)}, f32[4,288,128]{2,1,0:T(8,128)}, f32[8,9]{1,0:T(8,128)}, f32[2,64,72]{2,1,0:T(8,128)}, f32[3,8]{1,0:T(4,128)}, /*index=5*/f32[3,8]{1,0:T(4,128)}) custom-call(bf16[4,32,1024]{2,1,0:T(8,128)(2,1)S(1)} %get-tuple-element.18.refs_0_, f32[4,288,128]{2,1,0:T(8,128)S(1)} %get-tuple-element.19.refs_1_, ...), custom_call_target="tpu_custom_call" | custom-call | tf_op jit(solution)/shard_map/pallas_call | solution.py:1171

commit v6 on v5

--- a/solution.py
+++ b/solution.py
@@ -704,9 +704,13 @@
         a, b = t // 3, t % 3
         window = 2 * (a == 0) + (b == 0)
         plane = 2 * (a != 1) + (b != 1)
-        ref.back1[
-            window * LANES : (window + 1) * LANES, plane * LANES : (plane + 1) * LANES
-        ] = jnp.transpose(k1).astype(BF16)
+        turned = jnp.transpose(k1)
+        for half in range(2):
+            own = turned[half * CH : (half + 1) * CH, :]
+            own = (own if half == plane % 2 else roll64(own)).astype(BF16)
+            at = window * LANES + half * CH
+            tile = (2 * half + plane // 2) * LANES
+            ref.back1[at : at + CH, tile : tile + LANES] += own
 
     y1 = ref.y1
     first_col = jnp.bitwise_and(iota((PIXELS, LANES), 0), HALF_COLS - 1) == 0
@@ -921,16 +925,16 @@
         for w in range(4):
             ref.im4[pair, :, w * LANES : (w + 1) * LANES] = jnp.concatenate(windows[w], axis=0)
         ref.back[pair] = dot_nn(ref.im4[pair], ref.back1[...]).astype(BF16)
-        value = dot_nn(fetch[pair], ref.back[pair])
         y_send = ref.y_send.at[pair].reshape(128 * 8, LANES)
         chosen = []
-        for block in range(2 * SLOTS):
-            rows = slice(block * LANES, (block + 1) * LANES)
-            picked = value[rows, 0:LANES] * parity[pair, rows, 0:LANES].astype(F32)
-            for q in range(1, 4):
-                tile = slice(q * LANES, (q + 1) * LANES)
-                picked = picked + value[rows, tile] * parity[pair, rows, tile].astype(F32)
-            chosen.append(picked)
+        for half in range(2):
+            slots = slice(half * SLOTS * LANES, (half + 1) * SLOTS * LANES)
+            value = dot_nn(fetch[pair, slots, :], ref.back[pair, :, 2 * half * LANES : 2 * (half + 1) * LANES])
+            masks = [parity[pair, slots, q * LANES : (q + 1) * LANES].astype(F32) for q in range(4)]
+            picked = value[:, 0:LANES] * jnp.where(first_half, masks[0], masks[1])
+            picked = picked + value[:, LANES:] * jnp.where(first_half, masks[2], masks[3])
+            picked = picked + roll64(picked)
+            chosen += [picked[k * LANES : (k + 1) * LANES, :] for k in range(SLOTS)]
         for k in range(SLOTS):
             y_send[pl.ds(k, 128, stride=8), :] = jnp.where(first_half, chosen[k], chosen[SLOTS + k])
         ref.y_land[pair, 0, 0:SLOTS, :] = ref.y_send[pair, 0, 0:SLOTS, :]

time: 78.9 us -> 78.7 us (level)
  no operation moved by 1% of the time
where the time goes in v6:
time: 78.7 us; the launch traced here: 78 us
  Pallas kernels  77.2 us (98%)
  between operations  0.8 us (1%)
    pallas_call x1, Pallas kernels, body(): pl.pallas_call(functools.partial(step_kernel, n_rows, n_cols), out_shape=...  76.2 us

profile of v6, /device:TPU:0, one launch (start us, length us, event | category | flops | bytes accessed | tf_op | source)
XLA Modules:
  0.0 78.0 jit_solution(1873308158239619405)
XLA Ops:
  0.6 76.2 %shard_map.136 = (bf16[4,32,1024]{2,1,0:T(8,128)(2,1)S(1)}, f32[4,288,128]{2,1,0:T(8,128)S(1)}, f32[8,9]{1,0:T(8,128)S(1)}, f32[2,64,72]{2,1,0:T(8,128)S(1)}, f32[3,8]{1,0:T(4,128)S(1)}, /*index=5*/f32[3,8]{1,0:T(4,128)S(1)}) custom-call(bf16[4,288,128]{2,1,0:T(8,128)(2,1)} %bitcast.7, s32[4,128]{1,0:T(4,128)} %refs_1_.1, s32[4,128]{1,0:T(4,128)} %bitcast.9, ...), custom_call_target="tpu_custom_call" | custom-call | tf_op jit(solution)/shard_map/pallas_call | solution.py:1150
  76.9 1.0 %shard_map.137 = (bf16[4,32,1024]{2,1,0:T(8,128)(2,1)}, f32[4,288,128]{2,1,0:T(8,128)}, f32[8,9]{1,0:T(8,128)}, f32[2,64,72]{2,1,0:T(8,128)}, f32[3,8]{1,0:T(4,128)}, /*index=5*/f32[3,8]{1,0:T(4,128)}) custom-call(bf16[4,32,1024]{2,1,0:T(8,128)(2,1)S(1)} %get-tuple-element.18.refs_0_, f32[4,288,128]{2,1,0:T(8,128)S(1)} %get-tuple-element.19.refs_1_, ...), custom_call_target="tpu_custom_call" | custom-call | tf_op jit(solution)/shard_map/pallas_call | solution.py:1175
